TPU v7x, 32 devices: a whole 2x2x4 slice. The times are simulated.
32 devices in a mesh: seq: 8 (over z, y), tp: 4 (over x, core).
Axes of the slice: x: 2, y: 2, z: 4, core: 2. Of those that a mesh axis runs over, the one named last changes fastest.
Arguments:
- query_in: bfloat16 [1024, 8192], P('seq', 'tp'), may hold values from -6 to 6
- key_in: bfloat16 [1024, 8192], P('seq', 'tp'), may hold values from -6 to 6
- value_in: bfloat16 [1024, 8192], P('seq', 'tp'), may hold values from -6 to 6
- stream: bfloat16 [1024, 8192], P('seq', 'tp'), may hold values from -6 to 6
- short_filter: float32 [3, 3, 8192], P(None, None, 'tp'), may hold values from -3 to 3
- decay_rate: float32 [16, 8192], P(None, 'tp'), as said below
- residue: float32 [16, 8192], P(None, 'tp'), as said below
- norm_gain: float32 [8192], P('tp'), may hold values from 0.5 to 1.5
- cotangent: bfloat16 [1024, 8192], P('seq', 'tp'), may hold values from -6 to 6
Outputs:
- normed: bfloat16 [1024, 8192], P('seq', 'tp')
- stream_grad: bfloat16 [1024, 8192], P('seq', 'tp')
- query_grad: bfloat16 [1024, 8192], P('seq', 'tp')
- key_grad: bfloat16 [1024, 8192], P('seq', 'tp')
- value_grad: bfloat16 [1024, 8192], P('seq', 'tp')
Inputs may be any that keep to these rules, and one draw needn't show every extreme that they name: The pole of mode m of channel c is exp(-decay_rate[m, c]); every rate is positive and at most 1/30. `residue`: residues are real numbers.
All inputs are finite; a program needn't handle non-finite values.
Results may differ from a plain program's by a relative error of at most 0.0012.
Values may be sent and summed in bfloat16 or wider, within the bound.
No kernel may reach another device: no remote copies, remote signals or barrier semaphores. Data moves between devices by JAX's collectives and lax.ppermute only.
A program may use at most 128 MiB of HBM per device.

v0:
```python
import functools

import jax
import jax.numpy as jnp
from jax import lax
from jax.experimental import pallas as pl
from jax.experimental.pallas import tpu as pltpu
from jax.sharding import PartitionSpec as P

f32 = jnp.float32
bf16 = jnp.bfloat16
epsilon = 1e-05
LANES = 128
SUB = 8
GROUP = LANES * SUB
FORWARD_EXTRA = 12
BACKWARD_EXTRA = 4
GRANT = 20 * 1024 * 1024


class Sizes:
    def __init__(self, length, channels, modes, devices):
        self.length, self.channels, self.modes, self.devices = length, channels, modes, devices
        self.tiles = channels // LANES
        self.halves = channels // GROUP
        self.direct = devices == SUB

    def chunk_row(self, r, h, extra):
        if r < self.modes:
            return h * self.modes + r
        return self.halves * self.modes + h * extra + r - self.modes

    def chunk_rows(self, extra):
        return self.halves * (self.modes + extra)

    def exchange_shape(self, extra):
        if self.direct:
            return (self.devices * self.chunk_rows(extra), LANES)
        return ((self.modes + extra) * self.tiles, LANES)

    def exchange_slice(self, r, h, extra):
        if self.direct:
            return pl.ds(self.chunk_row(r, h, extra), SUB, stride=self.chunk_rows(extra))
        return pl.ds(r * self.tiles + h * SUB, SUB)


def staged(s, block, offset, h):
    start = block * (s.tiles * SUB) + (h * SUB * SUB + offset)
    return pl.ds(start, SUB, stride=SUB)


def major(s, t, h):
    start = t * s.tiles + h * SUB
    if not isinstance(start, int):
        start = pl.multiple_of(start, SUB)
    return pl.ds(start, SUB)


def staged_before(s, block, offset, h):
    if offset < 2:
        return staged(s, block - 1, offset + SUB - 2, h)
    return staged(s, block, offset - 2, h)


def aligned(start, unit):
    return start if isinstance(start, int) else pl.multiple_of(start, unit)


def columns(h):
    return pl.ds(aligned(h * GROUP, GROUP), GROUP)


def stage(s, x_ref, out_ref, i, h, pad=0):
    rows = x_ref[pl.ds(aligned(i * 16, 16), 16), columns(h)].astype(f32)
    base = (i + pad) * (2 * s.tiles * SUB) + h * (SUB * SUB)
    for part in range(2):
        for j in range(SUB):
            out_ref[pl.ds(aligned(base + (part * s.tiles + j) * SUB, SUB), SUB), :] = rows[
                part * SUB : (part + 1) * SUB, j * LANES : (j + 1) * LANES
            ]


def unstage(s, in_ref, x_ref, i, h, to=None):
    base = i * (2 * s.tiles * SUB) + h * (SUB * SUB)
    rows = [
        jnp.concatenate(
            [
                in_ref[pl.ds(aligned(base + (part * s.tiles + j) * SUB, SUB), SUB), :]
                for part in range(2)
            ],
            axis=0,
        )
        for j in range(SUB)
    ]
    to = i if to is None else to
    x_ref[pl.ds(aligned(to * 16, 16), 16), columns(h)] = jnp.concatenate(rows, axis=1).astype(bf16)


def stage_wide(s, x_ref, out_ref):
    for h in range(s.halves):
        stage(s, x_ref, out_ref, 0, h)


def each_half(s, body):
    def step(h, carry):
        body(h)
        return carry

    lax.fori_loop(0, s.halves, step, 0)


def sixteen(i, reverse=False):
    pairs = [(2 * i + part, offset) for part in range(2) for offset in range(SUB)]
    return pairs[::-1] if reverse else pairs


def stage_modes(s, x_ref, out_ref, f):
    for g in range(s.modes // SUB):
        rows = f(x_ref[g * SUB : (g + 1) * SUB, :])
        for j in range(s.tiles):
            start = (g * s.tiles + j) * SUB
            out_ref[start : start + SUB, :] = rows[:, j * LANES : (j + 1) * LANES]


def mode_tiles(s, ref, h):
    return [ref[staged(s, m // SUB, m % SUB, h), :] for m in range(s.modes)]


def stage_taps(s, filter_ref, out_ref):
    for i in range(3):
        rows = filter_ref[i]
        for j in range(s.tiles):
            start = (i * s.tiles + j) * SUB
            out_ref[start : start + 3, :] = rows[:, j * LANES : (j + 1) * LANES]


def tap_tiles(s, ref, i, h):
    return [ref[staged(s, i, tap, h), :] for tap in range(3)]


def total(parts):
    while len(parts) > 1:
        parts = [
            parts[i] + parts[i + 1] if i + 1 < len(parts) else parts[i]
            for i in range(0, len(parts), 2)
        ]
    return parts[0]


def mix(taps, now, before, before2):
    return taps[0] * now + taps[1] * before + taps[2] * before2


def recur(s, from_ref, to_ref, p, w, states, h, reverse=False):
    steps = s.length // 16

    def step(i, states):
        i = steps - 1 - i if reverse else i
        for block, offset in sixteen(0, reverse):
            rows = major(s, (2 * i + block) * SUB + offset, h)
            signal = from_ref[rows, :]
            states = [p[m] * states[m] + signal for m in range(s.modes)]
            to_ref[rows, :] = total([w[m] * states[m] for m in range(s.modes)])
        return states

    lax.fori_loop(0, steps, step, states)


def begin_kernel(
    s, q_hbm, k_hbm, v_hbm, filter_hbm, decay_hbm, pay_ref,
    kb, vb, qb, fb, db, ks, vs, qs, taps, poles, sems,
):
    copies = [(decay_hbm, db), (filter_hbm, fb), (q_hbm.at[pl.ds(s.length - 16, 16), :], qb)]
    for h in range(s.halves):
        cut = pl.ds(h * GROUP, GROUP)
        copies += [(k_hbm.at[:, cut], kb.at[:, cut]), (v_hbm.at[:, cut], vb.at[:, cut])]
    copies = [pltpu.make_async_copy(a, b, sems.at[i]) for i, (a, b) in enumerate(copies)]
    for copy in copies:
        copy.start()
    copies[0].wait()
    stage_modes(s, db, poles, lambda x: jnp.exp(-x))
    copies[1].wait()
    stage_taps(s, fb, taps)
    blank = jnp.zeros((SUB, LANES), f32)
    steps = s.length // 16
    copies[2].wait()
    stage_wide(s, qb, qs)

    def half(h):
        for i, (from_hbm, to) in enumerate(((k_hbm, kb), (v_hbm, vb))):
            cut = columns(h)
            pltpu.make_async_copy(from_hbm.at[:, cut], to.at[:, cut], sems.at[3 + 2 * h + i]).wait()
        p = mode_tiles(s, poles, h)
        taps_k, taps_v = (tap_tiles(s, taps, i, h) for i in (1, 2))

        def bring(i):
            stage(s, kb, ks, i, h)
            stage(s, vb, vs, i, h)

        def step(i, carry):
            (k1, k2, v1, v2), states = carry
            for block, offset in sixteen(0):
                rows = staged(s, 2 * i + block, offset, h)
                k0, v0 = ks[rows, :], vs[rows, :]
                product = mix(taps_k, k0, k1, k2) * mix(taps_v, v0, v1, v2)
                if block == 0 and offset < 2:
                    product = jnp.where(i == 0, 0.0, product)
                states = [p[m] * states[m] + product for m in range(s.modes)]
                k1, k2, v1, v2 = k0, k1, v0, v1
            bring(jnp.minimum(i + 1, steps - 1))
            return (k1, k2, v1, v2), states

        bring(0)
        held, states = lax.fori_loop(0, steps, step, ((blank,) * 4, [blank] * s.modes))
        for m in range(s.modes):
            pay_ref[s.exchange_slice(m, h, FORWARD_EXTRA), :] = states[m]
        k1, k2, v1, v2 = held
        first = [staged(s, 0, offset, h) for offset in range(2)]
        last = [staged(s, 1, offset, h) for offset in (6, 7)]
        extra = [
            ks[first[0], :], ks[first[1], :], k2, k1,
            vs[first[0], :], vs[first[1], :], v2, v1,
            qs[last[0], :], qs[last[1], :], blank, blank,
        ]
        for r, value in enumerate(extra):
            pay_ref[s.exchange_slice(s.modes + r, h, FORWARD_EXTRA), :] = value

    each_half(s, half)


def forward_middle(length, rates, taps, ends, extras):
    devices = len(ends)
    whole, step0, step1 = (jnp.exp(-float(length - i) * rates) for i in range(3))
    blank = jnp.zeros_like(extras[0][0])
    arriving = jnp.zeros_like(ends[0])
    result = []
    for i in range(devices):
        k0, k1, _, _, v0, v1 = extras[i][:6]
        if i:
            _, _, ka, kb, _, _, va, vb, qa, qb = extras[i - 1][:10]
        else:
            ka = kb = va = vb = qa = qb = blank
        if i + 1 < devices:
            kc, kd, _, _, vc, vd = extras[i + 1][:6]
        else:
            kc = kd = vc = vd = blank
        prod0 = mix(taps[1], k0, kb, ka) * mix(taps[2], v0, vb, va)
        prod1 = mix(taps[1], k1, k0, kb) * mix(taps[2], v1, v0, vb)
        result.append((arriving, [prod0, prod1, ka, kb, va, vb, qa, qb, kc, kd, vc, vd]))
        arriving = whole * arriving + (ends[i] + step0 * prod0 + step1 * prod1)
    return result


def backward_middle(length, rates, ends, extras):
    devices = len(ends)
    whole = jnp.exp(-float(length) * rates)
    blank = jnp.zeros_like(extras[0][0])
    arriving = jnp.zeros_like(ends[0])
    result = [None] * devices
    for i in reversed(range(devices)):
        result[i] = (arriving, extras[i + 1] if i + 1 < devices else [blank] * len(extras[0]))
        arriving = whole * arriving + ends[i]
    return result


def middle_kernel(s, extra, in_ref, decay_ref, filter_ref, out_ref):
    me = lax.axis_index("seq")
    rows = s.chunk_rows(extra)
    for h in range(s.halves):
        lanes = pl.ds(pl.multiple_of((me + h * SUB) * LANES, LANES), LANES)
        rates = decay_ref[:, lanes]
        ends, extras = [], []
        for i in range(s.devices):
            base = i * rows
            e = base + s.chunk_row(0, h, extra)
            ends.append(in_ref[e : e + s.modes, :])
            x = base + s.chunk_row(s.modes, h, extra)
            extras.append([in_ref[x + r : x + r + 1, :] for r in range(extra)])
        if extra == FORWARD_EXTRA:
            taps = [[filter_ref[i, tap : tap + 1, lanes] for tap in range(3)] for i in range(3)]
            result = forward_middle(s.length, rates, taps, ends, extras)
        else:
            result = backward_middle(s.length, rates, ends, extras)
        for i in range(s.devices):
            base = i * rows
            e = base + s.chunk_row(0, h, extra)
            out_ref[e : e + s.modes, :] = result[i][0]
            x = base + s.chunk_row(s.modes, h, extra)
            for r in range(extra):
                out_ref[x + r : x + r + 1, :] = result[i][1][r]


def exchange(s, pay, decay_rate, short_filter, extra):
    if s.direct:
        got = lax.all_to_all(pay, "seq", 0, 0, tiled=True)
        back = pl.pallas_call(
            functools.partial(middle_kernel, s, extra),
            out_shape=jax.ShapeDtypeStruct(pay.shape, f32),
            compiler_params=pltpu.CompilerParams(vmem_limit_bytes=GRANT),
        )(got, decay_rate, short_filter)
        return lax.all_to_all(back, "seq", 0, 0, tiled=True)
    rows = s.modes + extra
    width = s.channels // s.devices
    start = lax.axis_index("seq") * width
    rates = lax.dynamic_slice_in_dim(decay_rate, start, width, 1)
    part = lax.dynamic_slice_in_dim(short_filter, start, width, 2)
    pay = pay.reshape(rows, s.devices, width).transpose(1, 0, 2)
    got = lax.all_to_all(pay, "seq", 0, 0, tiled=True)
    ends = [got[i, : s.modes] for i in range(s.devices)]
    extras = [[got[i, s.modes + r][None] for r in range(extra)] for i in range(s.devices)]
    if extra == FORWARD_EXTRA:
        taps = [[part[i, tap][None] for tap in range(3)] for i in range(3)]
        result = forward_middle(s.length, rates, taps, ends, extras)
    else:
        result = backward_middle(s.length, rates, ends, extras)
    back = jnp.stack([jnp.concatenate([state] + list(more)) for state, more in result])
    back = lax.all_to_all(back, "seq", 0, 0, tiled=True)
    return back.transpose(1, 0, 2).reshape(rows * s.tiles, LANES)


def inside_kernel(
    s, k_hbm, v_hbm, filter_hbm, decay_hbm, residue_hbm, inside_ref,
    kb, vb, fb, db, rb, ks, vs, prod, taps, poles, weights, sems,
):
    pairs = [(decay_hbm, db), (residue_hbm, rb), (filter_hbm, fb), (k_hbm, kb), (v_hbm, vb)]
    copies = [pltpu.make_async_copy(a, b, sems.at[i]) for i, (a, b) in enumerate(pairs)]
    for copy in copies:
        copy.start()
    for copy in copies:
        copy.wait()
    stage_modes(s, db, poles, lambda x: jnp.exp(-x))
    stage_modes(s, rb, weights, lambda x: x)
    stage_taps(s, fb, taps)
    blank = jnp.zeros((SUB, LANES), f32)
    steps = s.length // 16

    def half(h):
        taps_k, taps_v = (tap_tiles(s, taps, i, h) for i in (1, 2))

        def products(i, held):
            stage(s, kb, ks, i, h)
            stage(s, vb, vs, i, h)
            k1, k2, v1, v2 = held
            for block, offset in sixteen(0):
                rows = staged(s, 2 * i + block, offset, h)
                k0, v0 = ks[rows, :], vs[rows, :]
                product = mix(taps_k, k0, k1, k2) * mix(taps_v, v0, v1, v2)
                if block == 0 and offset < 2:
                    product = jnp.where(i == 0, 0.0, product)
                prod[major(s, (2 * i + block) * SUB + offset, h), :] = product
                k1, k2, v1, v2 = k0, k1, v0, v1
            return k1, k2, v1, v2

        lax.fori_loop(0, steps, products, (blank,) * 4)
        recur(s, prod, inside_ref, mode_tiles(s, poles, h), mode_tiles(s, weights, h), [blank] * s.modes, h)

    each_half(s, half)


def forward_kernel(
    s, inside_ref, q_ref, stream_ref, cot_ref, back_ref, filter_ref, decay_ref, residue_ref, gain_ref,
    conv_ref, sums_ref,
    qs, xs, gs, taps, poles, weights, squares, inners,
):
    stage_modes(s, decay_ref, poles, lambda x: jnp.exp(-x))
    stage_modes(s, residue_ref, weights, lambda x: x)
    stage_taps(s, filter_ref, taps)

    def back(r, h):
        return back_ref[s.exchange_slice(r, h, FORWARD_EXTRA), :]

    steps = s.length // 16

    def half(h):
        p = mode_tiles(s, poles, h)
        w = mode_tiles(s, weights, h)
        gain = gain_ref[pl.ds(aligned(h * SUB, SUB), SUB), :]
        taps_q = tap_tiles(s, taps, 0, h)
        conv, states = [], [back(m, h) for m in range(s.modes)]
        for offset in range(2):
            product = back(s.modes + offset, h)
            states = [p[m] * states[m] + product for m in range(s.modes)]
            conv.append(total([w[m] * states[m] for m in range(s.modes)]))
        states = [w[m] * states[m] / (p[m] * p[m]) for m in range(s.modes)]
        first, ahead = [], states
        for offset in range(2):
            ahead = [p[m] * ahead[m] for m in range(s.modes)]
            first.append(conv[offset] - total(ahead))

        def bring(i):
            stage(s, q_ref, qs, i, h)
            stage(s, stream_ref, xs, i, h)
            stage(s, cot_ref, gs, i, h)

        def step(i, carry):
            (q1, q2), states = carry
            for block, offset in sixteen(0):
                rows = staged(s, 2 * i + block, offset, h)
                t = (2 * i + block) * SUB + offset
                out = major(s, t, h)
                inside = inside_ref[out, :]
                if block == 0 and offset < 2:
                    inside = jnp.where(i == 0, first[offset], inside)
                states = [p[m] * states[m] for m in range(s.modes)]
                conv = inside + total(states)
                conv_ref[out, :] = conv
                q0 = qs[rows, :]
                mixed = xs[rows, :] + mix(taps_q, q0, q1, q2) * conv
                part = pl.ds(pl.multiple_of(t * SUB, SUB), SUB)
                square, inner = mixed * mixed, gain * gs[rows, :] * mixed
                squares[part, :] = square + jnp.where(h == 0, 0.0, squares[part, :])
                inners[part, :] = inner + jnp.where(h == 0, 0.0, inners[part, :])
                q1, q2 = q0, q1
            bring(jnp.minimum(i + 1, steps - 1))
            return (q1, q2), states

        bring(0)
        lax.fori_loop(0, steps, step, ((back(s.modes + 7, h), back(s.modes + 6, h)), states))

    each_half(s, half)
    for r, ref in enumerate((squares, inners)):
        parts = []
        for b in range(s.length // SUB):
            parts.append(
                total([ref[pl.ds(b * SUB * SUB + i, SUB, stride=SUB), :] for i in range(SUB)])
            )
        rows = jnp.concatenate(parts, axis=0)
        sums_ref[r : r + 1, :] = jnp.sum(rows.T, axis=0, keepdims=True)


def norm_kernel(
    s, width, sums_ref, conv_ref, q_ref, stream_ref, cot_ref, back_ref, filter_ref, decay_ref, gain_ref,
    normed_hbm, dstream_hbm, qgrad_hbm, dconv_ref, tail_ref, pay_ref,
    qs, xs, gs, ns, ds, normed_b, dstream_b, qgrad_b, taps, poles, inv_s, coef_s, sems,
):
    inverse = lax.rsqrt(sums_ref[0:1, :] / width + epsilon)
    coef = inverse * inverse * inverse * sums_ref[1:2, :] / width
    inv_s[...] = jnp.broadcast_to(inverse, (LANES, s.length)).T
    coef_s[...] = jnp.broadcast_to(coef, (LANES, s.length)).T
    stage_modes(s, decay_ref, poles, lambda x: jnp.exp(-x))
    stage_taps(s, filter_ref, taps)
    blank = jnp.zeros((SUB, LANES), f32)
    steps = s.length // 16

    def back(r, h):
        return back_ref[s.exchange_slice(r, h, FORWARD_EXTRA), :]

    def pieces(h):
        cut = columns(h)
        sources = [
            (normed_b.at[:, cut], normed_hbm.at[:, cut]),
            (dstream_b.at[:, cut], dstream_hbm.at[:, cut]),
            (qgrad_b.at[pl.ds(16, s.length - 16), cut], qgrad_hbm.at[pl.ds(0, s.length - 16), cut]),
        ]
        return [pltpu.make_async_copy(a, b, sems.at[3 * h + i]) for i, (a, b) in enumerate(sources)]

    def half(h):
        gain = gain_ref[pl.ds(aligned(h * SUB, SUB), SUB), :]
        taps_q = tap_tiles(s, taps, 0, h)

        def bring(i):
            rows = jnp.minimum(i, steps - 1)
            stage(s, q_ref, qs, rows, h, i - rows + 1)
            stage(s, stream_ref, xs, rows, h)
            stage(s, cot_ref, gs, rows, h)

        def step(i, held):
            q1, q2, dq1, dq2 = held
            for block, offset in sixteen(0):
                rows = staged(s, 2 * i + block, offset, h)
                t = (2 * i + block) * SUB + offset
                out = major(s, t, h)
                inv = jnp.broadcast_to(inv_s[pl.ds(t, 1), :], (SUB, LANES))
                cf = jnp.broadcast_to(coef_s[pl.ds(t, 1), :], (SUB, LANES))
                q0 = qs[staged(s, 2 * i + block + 2, offset, h), :]
                qmix = mix(taps_q, q0, q1, q2)
                conv = conv_ref[out, :]
                mixed = xs[rows, :] + qmix * conv
                dmixed = inv * (gain * gs[rows, :]) - mixed * cf
                ns[rows, :] = mixed * inv * gain
                ds[rows, :] = dmixed
                dq0 = dmixed * conv
                dconv_ref[out, :] = dmixed * qmix
                qs[staged_before(s, 2 * i + block + 2, offset, h), :] = mix(taps_q, dq2, dq1, dq0)
                q1, q2, dq1, dq2 = q0, q1, dq0, dq1
            unstage(s, ns, normed_b, i, h)
            unstage(s, ds, dstream_b, i, h)
            unstage(s, qs, qgrad_b, i, h)
            bring(i + 1)
            return q1, q2, dq1, dq2

        bring(0)
        held = (back(s.modes + 7, h), back(s.modes + 6, h), blank, blank)
        _, _, dq1, dq2 = lax.fori_loop(0, steps, step, held)
        qs[staged(s, 2 * steps + 1, 6, h), :] = taps_q[0] * dq2 + taps_q[1] * dq1
        qs[staged(s, 2 * steps + 1, 7, h), :] = taps_q[0] * dq1
        for copy in pieces(h):
            copy.start()

    each_half(s, half)
    start = steps * 2 * s.tiles * SUB
    tail_ref[...] = qs[start : start + 2 * s.tiles * SUB, :]

    def ends(h):
        p = mode_tiles(s, poles, h)

        def step(i, states):
            for block, offset in sixteen(0, True):
                t = (2 * (steps - 1 - i) + block) * SUB + offset
                dconv = dconv_ref[major(s, t, h), :]
                states = [p[m] * states[m] + dconv for m in range(s.modes)]
            return states

        states = lax.fori_loop(0, steps, step, [blank] * s.modes)
        for m in range(s.modes):
            pay_ref[s.exchange_slice(m, h, BACKWARD_EXTRA), :] = states[m]
        first = [ds[staged(s, 0, offset, h), :] * conv_ref[major(s, offset, h), :] for offset in range(2)]
        for r, value in enumerate([dconv_ref[major(s, 0, h), :], *first, blank]):
            pay_ref[s.exchange_slice(s.modes + r, h, BACKWARD_EXTRA), :] = value

    each_half(s, ends)

    def finish(h):
        for copy in pieces(h):
            copy.wait()

    each_half(s, finish)


def backward_kernel(
    s, k_ref, v_ref, dconv_ref, tail_ref, ahead_ref, back_ref, filter_ref, decay_ref, residue_ref, qgrad_in,
    qgrad_hbm, kgrad_hbm, vgrad_hbm,
    ks, vs, dprod, qs, kgrad_b, vgrad_b, qgrad_b, taps, poles, weights, sems,
):
    del qgrad_in
    stage_modes(s, decay_ref, poles, lambda x: jnp.exp(-x))
    stage_modes(s, residue_ref, weights, lambda x: x)
    stage_taps(s, filter_ref, taps)
    steps = s.length // 16

    def near(r, h):
        return ahead_ref[s.exchange_slice(s.modes + r, h, FORWARD_EXTRA), :]

    def back(r, h):
        return back_ref[s.exchange_slice(r, h, BACKWARD_EXTRA), :]

    qs[...] = tail_ref[...]

    def tails(h):
        taps_q = tap_tiles(s, taps, 0, h)
        dq0, dq1 = back(s.modes + 1, h), back(s.modes + 2, h)
        rows = [staged(s, 1, offset, h) for offset in (6, 7)]
        qs[rows[0], :] = qs[rows[0], :] + taps_q[2] * dq0
        qs[rows[1], :] = qs[rows[1], :] + (taps_q[1] * dq0 + taps_q[2] * dq1)
        unstage(s, qs, qgrad_b, 0, h)

    each_half(s, tails)
    last = pltpu.make_async_copy(qgrad_b, qgrad_hbm.at[pl.ds(s.length - 16, 16), :], sems.at[2 * s.halves])
    last.start()

    def pieces(h):
        cut = columns(h)
        sources = [(kgrad_b, kgrad_hbm), (vgrad_b, vgrad_hbm)]
        return [
            pltpu.make_async_copy(a.at[:, cut], b.at[:, cut], sems.at[2 * h + i])
            for i, (a, b) in enumerate(sources)
        ]

    def half(h):
        p = mode_tiles(s, poles, h)
        w = mode_tiles(s, weights, h)
        arriving = [back(m, h) for m in range(s.modes)]
        recur(s, dconv_ref, dprod, p, w, arriving, h, reverse=True)
        taps_k, taps_v = (tap_tiles(s, taps, i, h) for i in (1, 2))

        def bring(i):
            stage(s, k_ref, ks, i, h, 1)
            stage(s, v_ref, vs, i, h, 1)

        def advance(inputs, grads, k2, v2, d):
            k0, k1, v0, v1 = inputs
            dk1, dk2, dv1, dv2 = grads
            dk0 = d * mix(taps_v, v0, v1, v2)
            dv0 = d * mix(taps_k, k0, k1, k2)
            out = mix(taps_k, dk0, dk1, dk2), mix(taps_v, dv0, dv1, dv2)
            return (k1, k2, v1, v2), (dk0, dk1, dv0, dv1), out

        bring(steps - 1)
        ka, kb, va, vb, _, _, kc, kd, vc, vd = (near(2 + r, h) for r in range(10))
        for ref, rows in ((ks, (ka, kb)), (vs, (va, vb))):
            for offset in range(2):
                ref[staged(s, 1, 6 + offset, h), :] = rows[offset]
        arriving = [back(m, h) for m in range(s.modes)]
        dconv0 = back(s.modes, h)
        d0 = total([w[m] * arriving[m] for m in range(s.modes)])
        d1 = total([w[m] * ((arriving[m] - dconv0) / p[m]) for m in range(s.modes)])
        ends = [staged(s, 2 * steps + 1, offset, h) for offset in (6, 7)]
        inputs = (kd, kc, vd, vc)
        grads = (jnp.zeros((SUB, LANES), f32),) * 4
        inputs, grads, _ = advance(inputs, grads, ks[ends[1], :], vs[ends[1], :], d1)
        inputs, grads, _ = advance(inputs, grads, ks[ends[0], :], vs[ends[0], :], d0)

        def step(i, carry):
            inputs, grads = carry
            i = steps - 1 - i

            @pl.when(i > 0)
            def _():
                bring(jnp.maximum(i - 1, 0))

            for block, offset in sixteen(0, True):
                d = dprod[major(s, (2 * i + block) * SUB + offset, h), :]
                rows = staged_before(s, 2 * i + block + 2, offset, h)
                inputs, grads, out = advance(inputs, grads, ks[rows, :], vs[rows, :], d)
                rows = staged(s, 2 * i + block + 2, offset, h)
                ks[rows, :], vs[rows, :] = out
            unstage(s, ks, kgrad_b, i + 1, h, i)
            unstage(s, vs, vgrad_b, i + 1, h, i)
            return inputs, grads

        lax.fori_loop(0, steps, step, (inputs, grads))
        for copy in pieces(h):
            copy.start()

    each_half(s, half)
    last.wait()

    def finish(h):
        for copy in pieces(h):
            copy.wait()

    each_half(s, finish)


def body(
    query_in, key_in, value_in, stream, short_filter, decay_rate, residue, norm_gain, cotangent
):
    length, channels = query_in.shape
    modes = decay_rate.shape[0]
    s = Sizes(length, channels, modes, lax.axis_size("seq"))
    total_width = channels * lax.axis_size("tp")
    wide = jax.ShapeDtypeStruct((length * s.tiles, LANES), f32)
    narrow = jax.ShapeDtypeStruct((length, channels), bf16)
    rows = 16 * s.tiles
    wide_s = pltpu.VMEM(wide.shape, f32)
    longer_s = pltpu.VMEM(((length + 16) * s.tiles, LANES), f32)
    narrow_s = pltpu.VMEM(narrow.shape, bf16)
    last_s = pltpu.VMEM((16, channels), bf16)
    tail_s = pltpu.VMEM((rows, LANES), f32)
    taps_s = pltpu.VMEM((3 * s.tiles * SUB, LANES), f32)
    mode_s = pltpu.VMEM((modes * s.tiles, LANES), f32)
    sum_s = pltpu.VMEM((length * SUB, LANES), f32)
    square_s = pltpu.VMEM((length, LANES), f32)
    gain = norm_gain.reshape(s.tiles, LANES)
    there = pl.BlockSpec(memory_space=pltpu.HBM)
    here = pl.BlockSpec(memory_space=pltpu.VMEM)

    def call(kernel, ins, outs, out_shape, scratch_shapes, operands, aliases={}, cost=None):
        return pl.pallas_call(
            functools.partial(kernel, s),
            in_specs=[there if c == "h" else here for c in ins],
            out_specs=[there if c == "h" else here for c in outs],
            out_shape=out_shape,
            scratch_shapes=scratch_shapes,
            input_output_aliases=aliases,
            cost_estimate=cost,
            compiler_params=pltpu.CompilerParams(vmem_limit_bytes=GRANT),
        )(*operands)

    def pay_shape(extra):
        return jax.ShapeDtypeStruct(s.exchange_shape(extra), f32)

    def far(*arrays):
        return [pltpu.with_memory_space_constraint(x, pltpu.HBM) for x in arrays]

    def cost(per_element, arrays):
        return pl.CostEstimate(
            flops=per_element * length * channels, bytes_accessed=arrays * 4 * length * channels, transcendentals=0
        )

    filter_s = pltpu.VMEM(short_filter.shape, f32)
    rates_s = pltpu.VMEM(decay_rate.shape, f32)
    (pay,) = call(
        begin_kernel, "hhhhh", "v",
        (pay_shape(FORWARD_EXTRA),),
        [narrow_s, narrow_s, last_s, filter_s, rates_s]
        + [wide_s, wide_s, tail_s, taps_s, mode_s, pltpu.SemaphoreType.DMA((3 + 2 * s.halves,))],
        far(query_in, key_in, value_in, short_filter, decay_rate),
    )
    (inside,) = call(
        inside_kernel, "hhhhh", "v", (wide,),
        [narrow_s, narrow_s, filter_s, rates_s, rates_s]
        + [wide_s] * 3 + [taps_s, mode_s, mode_s, pltpu.SemaphoreType.DMA((5,))],
        far(key_in, value_in, short_filter, decay_rate, residue),
        cost=cost(75, 3),
    )
    back = exchange(s, pay, decay_rate, short_filter, FORWARD_EXTRA)
    conv, sums = call(
        forward_kernel, "v" * 9, "vv",
        (wide, jax.ShapeDtypeStruct((2, length), f32)),
        [wide_s] * 3 + [taps_s, mode_s, mode_s, sum_s, sum_s],
        (inside, query_in, stream, cotangent, back, short_filter, decay_rate, residue, gain),
        {0: 0},
    )
    sums = lax.psum(sums, "tp")
    normed, dstream, query_grad, dconv, tail, pay_back = call(
        lambda s, *refs: norm_kernel(s, total_width, *refs), "v" * 9, "hhhvvv",
        (narrow, narrow, narrow, wide, jax.ShapeDtypeStruct((rows, LANES), f32), pay_shape(BACKWARD_EXTRA)),
        [pltpu.VMEM(((length + 32) * s.tiles, LANES), f32)] + [longer_s] * 2 + [wide_s] * 2 + [narrow_s] * 2
        + [pltpu.VMEM((length + 16, channels), bf16)]
        + [taps_s, mode_s, square_s, square_s, pltpu.SemaphoreType.DMA((3 * s.halves,))],
        (sums, conv, query_in, stream, cotangent, back, short_filter, decay_rate, gain),
    )
    back_back = exchange(s, pay_back, decay_rate, short_filter, BACKWARD_EXTRA)
    query_grad, key_grad, value_grad = call(
        backward_kernel, "v" * 9 + "h", "hhh",
        (narrow, narrow, narrow),
        [longer_s] * 2 + [wide_s, tail_s] + [narrow_s] * 2 + [last_s, taps_s, mode_s, mode_s]
        + [pltpu.SemaphoreType.DMA((1 + 2 * s.halves,))],
        (key_in, value_in, dconv, tail, back, back_back, short_filter, decay_rate, residue, query_grad),
        {9: 0},
    )
    return (normed, dstream, query_grad, key_grad, value_grad)


def solution(mesh):
    cut = P("seq", "tp")
    return jax.shard_map(
        body,
        mesh=mesh,
        in_specs=(cut, cut, cut, cut, P(None, None, "tp"), P(None, "tp"), P(None, "tp"), P("tp"), cut),
        out_specs=(cut,) * 5,
        check_vma=False,
    )
```

profile of v0, /device:TPU:0, one launch (start us, length us, event | category | flops | bytes accessed | tf_op | source)
XLA Modules:
  0.0 68.8 jit_solution(2705354079078482712)
XLA Ops:
  0.6 3.2 %shard_map.129 = f32[448,128]{1,0:T(8,128)S(1)} custom-call(bf16[128,2048]{1,0:T(8,128)(2,1)} %refs_2_.1, bf16[128,2048]{1,0:T(8,128)(2,1)} %k_ref.1, bf16[128,2048]{1,0:T(8,128)(2,1)} %v_ref.1, f32[3,3,2048]{2,1,0:T(4,128)} %filter_ref.7, f32[16,2048]{1,0:T(8,128)} %decay_ref.7), custom_call_target="tpu_custom_call" | custom-call | tf_op jit(solution)/shard_map/pallas_call | solution.py:659
  3.8 0.0 copy-start
  3.9 0.0 copy-start.2
  3.9 15.6 %all_to_all.44 = f32[8,56,128]{2,1,0:T(8,128)S(1)} all-to-all(f32[8,56,128]{2,1,0:T(8,128)S(1)} %bitcast.13), channel_id=1, replica_groups=mesh['seq'=8,'tp'=4] {'seq'}, dimensions={0} | all-to-all | bytes 458752 | tf_op jit(solution)/shard_map/all_to_all | solution.py:295
  19.5 0.0 copy-done
  19.5 0.0 copy-done.2
  19.5 0.8 %shard_map.130 = f32[448,128]{1,0:T(8,128)} custom-call(f32[448,128]{1,0:T(8,128)S(1)} %bitcast.12, f32[16,2048]{1,0:T(8,128)S(1)} %copy-done, f32[3,3,2048]{2,1,0:T(4,128)S(1)} %copy-done.2), custom_call_target="tpu_custom_call" | custom-call | tf_op jit(solution)/shard_map/pallas_call | solution.py:296
  20.3 3.4 %all-to-all-start.1 = ((f32[8,56,128]{2,1,0:T(8,128)}), f32[8,56,128]{2,1,0:T(8,128)S(1)}, u32[]{:S(2)}, u32[]{:S(2)}) async-start(f32[8,56,128]{2,1,0:T(8,128)} %bitcast.2), calls=%async_computation.1 | async-start | bytes 458752 | tf_op jit(solution)/shard_map/all_to_all | solution.py:301
  23.7 0.0 copy-start.1
  23.8 0.0 copy-start.3
  23.8 0.0 copy-start.4
  23.8 0.0 copy-start.7
  23.8 0.0 copy-start.8
  23.8 0.0 copy-start.9
  23.8 0.0 copy-start.10
  23.8 4.5 %shard_map.128.inside_ref = f32[2048,128]{1,0:T(8,128)S(1)} custom-call(bf16[128,2048]{1,0:T(8,128)(2,1)} %k_ref.1, bf16[128,2048]{1,0:T(8,128)(2,1)} %v_ref.1, f32[3,3,2048]{2,1,0:T(4,128)} %filter_ref.7, f32[16,2048]{1,0:T(8,128)} %decay_ref.7, f32[16,2048]{1,0:T(8,128)} %residue_ref.3), custom_call_target="tpu_custom_call" | custom-call | flops 19660800 | bytes 3145728 | tf_op jit(solution)/shard_map/pallas_call | solution.py:659
  28.4 3.5 %all-to-all-done.1 = f32[8,56,128]{2,1,0:T(8,128)S(1)} async-done(((f32[8,56,128]{2,1,0:T(8,128)}), f32[8,56,128]{2,1,0:T(8,128)S(1)}, u32[]{:S(2)}, u32[]{:S(2)}) %all-to-all-start.1) | async-done | bytes 229408 | tf_op jit(solution)/shard_map/all_to_all | solution.py:301
  31.8 0.0 copy-done.1
  31.8 0.0 copy-done.3
  31.8 0.0 copy-done.4
  31.8 0.0 copy-done.7
  31.8 0.0 copy-done.8
  31.9 0.0 copy-done.9
  31.9 0.0 copy-done.10
  31.9 2.3 %shard_map.131 = (f32[2048,128]{1,0:T(8,128)S(1)}, f32[2,128]{1,0:T(2,128)S(1)}) custom-call(f32[2048,128]{1,0:T(8,128)S(1)} %shard_map.128.inside_ref, bf16[128,2048]{1,0:T(8,128)(2,1)S(1)} %copy-done.4, bf16[128,2048]{1,0:T(8,128)(2,1)S(1)} %copy-done.7, bf16[128,2048]{1,0:T(8,128)(2,1)S(1)} %copy-done.8, ...), custom_call_target="tpu_custom_call", output_to_operand_aliasing={{0}: (0, {})} | custom-call | tf_op jit(solution)/shard_map/pallas_call | solution.py:659
  34.2 5.7 %psum.7.refs_0_ = f32[2,128]{1,0:T(2,128)S(1)} all-reduce(f32[2,128]{1,0:T(2,128)S(1)} %get-tuple-element.16), channel_id=1, replica_groups=mesh['seq'=8,'tp'=4] {'tp'}, use_global_device_ids=true, to_apply=%region_0.0 | all-reduce | flops 256 | bytes 2048 | tf_op jit(solution)/shard_map/psum | solution.py:705
  39.9 2.8 %shard_map.132 = (bf16[128,2048]{1,0:T(8,128)(2,1)}, bf16[128,2048]{1,0:T(8,128)(2,1)}, bf16[128,2048]{1,0:T(8,128)(2,1)}, f32[2048,128]{1,0:T(8,128)S(1)}, f32[...) custom-call(f32[2,128]{1,0:T(2,128)S(1)} %psum.7.refs_0_, f32[2048,128]{1,0:T(8,128)S(1)} %get-tuple-element.17.refs_1_, ...), custom_call_target="tpu_custom_call" | custom-call | tf_op jit(solution)/shard_map/pallas_call | solution.py:659
  42.7 0.0 copy-start.6
  42.7 11.4 %all_to_all.45 = f32[8,40,128]{2,1,0:T(8,128)S(1)} all-to-all(f32[8,40,128]{2,1,0:T(8,128)S(1)} %bitcast.17), channel_id=1, replica_groups=mesh['seq'=8,'tp'=4] {'seq'}, dimensions={0} | all-to-all | bytes 327680 | tf_op jit(solution)/shard_map/all_to_all | solution.py:295
  54.1 0.0 copy-start.5
  54.1 10.1 %all_to_all.46 = f32[8,40,128]{2,1,0:T(8,128)S(1)} all-to-all(f32[8,40,128]{2,1,0:T(8,128)S(1)} %bitcast.15), channel_id=1, replica_groups=mesh['seq'=8,'tp'=4] {'seq'}, dimensions={0} | all-to-all | bytes 327680 | tf_op jit(solution)/shard_map/all_to_all | solution.py:301
  64.2 0.0 copy-done.6
  64.2 0.0 copy-done.5
  64.2 4.6 %shard_map.134 = (bf16[128,2048]{1,0:T(8,128)(2,1)}, bf16[128,2048]{1,0:T(8,128)(2,1)}, bf16[128,2048]{1,0:T(8,128)(2,1)}) custom-call(bf16[128,2048]{1,0:T(8,128)(2,1)S(1)} %copy-done.5, bf16[128,2048]{1,0:T(8,128)(2,1)S(1)} %copy-done.6, f32[2048,128]{1,0:T(8,128)S(1)} %get-tuple-element.20.dconv_ref, ...), custom_call_target="tpu_custom_call", output_to_operand_aliasing={{0}: (9, {})} | custom-call | tf_op jit(solution)/shard_map/pallas_call | solution.py:659
  (1 shorter events, 0.0 us)
Async XLA Ops:
  3.8 15.7 %copy-start = (f32[16,2048]{1,0:T(8,128)S(1)}, f32[16,2048]{1,0:T(8,128)}, u32[]{:S(2)}) copy-start(f32[16,2048]{1,0:T(8,128)} %decay_ref.7) | copy-start | bytes 393220
  3.9 15.7 %copy-start.2 = (f32[3,3,2048]{2,1,0:T(4,128)S(1)}, f32[3,3,2048]{2,1,0:T(4,128)}, u32[]{:S(2)}) copy-start(f32[3,3,2048]{2,1,0:T(4,128)} %filter_ref.7) | copy-start | bytes 221188
  20.3 11.5 %all-to-all-start.1 = ((f32[8,56,128]{2,1,0:T(8,128)}), f32[8,56,128]{2,1,0:T(8,128)S(1)}, u32[]{:S(2)}, u32[]{:S(2)}) async-start(f32[8,56,128]{2,1,0:T(8,128)} %bitcast.2), calls=%async_computation.1 | async-start | bytes 458752 | tf_op jit(solution)/shard_map/all_to_all | solution.py:301
  23.7 8.1 %copy-start.1 = (f32[16,2048]{1,0:T(8,128)S(1)}, f32[16,2048]{1,0:T(8,128)}, u32[]{:S(2)}) copy-start(f32[16,2048]{1,0:T(8,128)} %decay_ref.7) | copy-start | bytes 393220
  23.8 8.1 %copy-start.3 = (f32[3,3,2048]{2,1,0:T(4,128)S(1)}, f32[3,3,2048]{2,1,0:T(4,128)}, u32[]{:S(2)}) copy-start(f32[3,3,2048]{2,1,0:T(4,128)} %filter_ref.7) | copy-start | bytes 221188
  23.8 8.1 %copy-start.4 = (bf16[128,2048]{1,0:T(8,128)(2,1)S(1)}, bf16[128,2048]{1,0:T(8,128)(2,1)}, u32[]{:S(2)}) copy-start(bf16[128,2048]{1,0:T(8,128)(2,1)} %refs_2_.1) | copy-start | bytes 1572868
  23.8 8.1 %copy-start.7 = (bf16[128,2048]{1,0:T(8,128)(2,1)S(1)}, bf16[128,2048]{1,0:T(8,128)(2,1)}, u32[]{:S(2)}) copy-start(bf16[128,2048]{1,0:T(8,128)(2,1)} %refs_3_.1) | copy-start | bytes 1572868
  23.8 8.1 %copy-start.8 = (bf16[128,2048]{1,0:T(8,128)(2,1)S(1)}, bf16[128,2048]{1,0:T(8,128)(2,1)}, u32[]{:S(2)}) copy-start(bf16[128,2048]{1,0:T(8,128)(2,1)} %refs_4_.1) | copy-start | bytes 1572868
  23.8 8.1 %copy-start.9 = (f32[16,2048]{1,0:T(8,128)S(1)}, f32[16,2048]{1,0:T(8,128)}, u32[]{:S(2)}) copy-start(f32[16,2048]{1,0:T(8,128)} %residue_ref.3) | copy-start | bytes 393220
  23.8 8.1 %copy-start.10 = (f32[2048]{0:T(1024)S(1)}, f32[2048]{0:T(1024)}, u32[]{:S(2)}) copy-start(f32[2048]{0:T(1024)} %param.16) | copy-start | bytes 24580
  42.7 21.5 %copy-start.6 = (bf16[128,2048]{1,0:T(8,128)(2,1)S(1)}, bf16[128,2048]{1,0:T(8,128)(2,1)}, u32[]{:S(2)}) copy-start(bf16[128,2048]{1,0:T(8,128)(2,1)} %v_ref.1) | copy-start | bytes 1572868
  54.1 10.1 %copy-start.5 = (bf16[128,2048]{1,0:T(8,128)(2,1)S(1)}, bf16[128,2048]{1,0:T(8,128)(2,1)}, u32[]{:S(2)}) copy-start(bf16[128,2048]{1,0:T(8,128)(2,1)} %k_ref.1) | copy-start | bytes 1572868
where the time goes:
time: 69.2 us; the launch traced here: 68.8 us
  blocking collectives  42.8 us (62%)
  Pallas kernels  18.3 us (26%)
  waiting for transfers between devices  3.45 us (5%)
  starting transfers between devices  3.4 us (5%)
  between operations  0.79 us (1%)
    all_to_all x2, blocking collectives, exchange(): got = lax.all_to_all(pay, 'seq', 0, 0, tiled=True)  27 us
    pallas_call x5, Pallas kernels, call(): pl.pallas_call(functools.partial(kernel, s), in_specs=[there if c == 'h'...  17.4 us
    all_to_all x1, blocking collectives, exchange(): return lax.all_to_all(back, 'seq', 0, 0, tiled=True)  10.1 us
    psum x1, blocking collectives, body(): sums = lax.psum(sums, 'tp')  5.66 us
    all_to_all x1, waiting for transfers between devices, exchange(): return lax.all_to_all(back, 'seq', 0, 0, tiled=True)  3.45 us
    all_to_all x1, starting transfers between devices, exchange(): return lax.all_to_all(back, 'seq', 0, 0, tiled=True)  3.4 us
  transfers between devices with their start and end apart: 1, of which 1 were waited for; matrix products, arithmetic and copies ran while one was open for 0% of the time, Pallas kernels for 7%

commit v1 on v0

--- a/solution.py
+++ b/solution.py
@@ -13,7 +13,7 @@
 LANES = 128
 SUB = 8
 GROUP = LANES * SUB
-FORWARD_EXTRA = 12
+FORWARD_EXTRA = 10
 BACKWARD_EXTRA = 4
 GRANT = 20 * 1024 * 1024
 
@@ -25,22 +25,22 @@
         self.halves = channels // GROUP
         self.direct = devices == SUB
 
-    def chunk_row(self, r, h, extra):
-        if r < self.modes:
-            return h * self.modes + r
-        return self.halves * self.modes + h * extra + r - self.modes
-
-    def chunk_rows(self, extra):
-        return self.halves * (self.modes + extra)
-
-    def exchange_shape(self, extra):
+    def chunk_row(self, r, h, lead, extra):
+        if r < lead:
+            return h * lead + r
+        return self.halves * lead + h * extra + r - lead
+
+    def chunk_rows(self, lead, extra):
+        return -(-self.halves * (lead + extra) // SUB) * SUB
+
+    def exchange_shape(self, lead, extra):
         if self.direct:
-            return (self.devices * self.chunk_rows(extra), LANES)
-        return ((self.modes + extra) * self.tiles, LANES)
-
-    def exchange_slice(self, r, h, extra):
+            return (self.devices * self.chunk_rows(lead, extra), LANES)
+        return ((lead + extra) * self.tiles, LANES)
+
+    def exchange_slice(self, r, h, lead, extra):
         if self.direct:
-            return pl.ds(self.chunk_row(r, h, extra), SUB, stride=self.chunk_rows(extra))
+            return pl.ds(self.chunk_row(r, h, lead, extra), SUB, stride=self.chunk_rows(lead, extra))
         return pl.ds(r * self.tiles + h * SUB, SUB)
 
 
@@ -166,9 +166,41 @@
     lax.fori_loop(0, steps, step, states)
 
 
+def forward_slice(s, r, h):
+    return s.exchange_slice(r, h, 2 * s.modes, FORWARD_EXTRA)
+
+
+def split(x):
+    high = x.astype(bf16).astype(f32)
+    return high, x - high
+
+
+def put_states(s, ref, states, h):
+    for m in range(s.modes):
+        high, low = split(states[m])
+        ref[forward_slice(s, m, h), :] = high
+        ref[forward_slice(s, s.modes + m, h), :] = low
+
+
+def narrowed(from_ref, to_ref):
+    rows = from_ref.shape[0]
+    for i in range(0, rows, 16):
+        to_ref[i : min(i + 16, rows), :] = from_ref[i : min(i + 16, rows), :].astype(bf16)
+
+
+def widened(from_ref, to_ref):
+    rows = from_ref.shape[0]
+    for i in range(0, rows, 16):
+        to_ref[i : min(i + 16, rows), :] = from_ref[i : min(i + 16, rows), :].astype(f32)
+
+
+def backward_slice(s, r, h):
+    return s.exchange_slice(r, h, s.modes, BACKWARD_EXTRA)
+
+
 def begin_kernel(
     s, q_hbm, k_hbm, v_hbm, filter_hbm, decay_hbm, pay_ref,
-    kb, vb, qb, fb, db, ks, vs, qs, taps, poles, sems,
+    kb, vb, qb, fb, db, ks, vs, qs, pay_s, taps, poles, sems,
 ):
     copies = [(decay_hbm, db), (filter_hbm, fb), (q_hbm.at[pl.ds(s.length - 16, 16), :], qb)]
     for h in range(s.halves):
@@ -212,20 +244,20 @@
 
         bring(0)
         held, states = lax.fori_loop(0, steps, step, ((blank,) * 4, [blank] * s.modes))
-        for m in range(s.modes):
-            pay_ref[s.exchange_slice(m, h, FORWARD_EXTRA), :] = states[m]
+        put_states(s, pay_s, states, h)
         k1, k2, v1, v2 = held
         first = [staged(s, 0, offset, h) for offset in range(2)]
         last = [staged(s, 1, offset, h) for offset in (6, 7)]
         extra = [
             ks[first[0], :], ks[first[1], :], k2, k1,
             vs[first[0], :], vs[first[1], :], v2, v1,
-            qs[last[0], :], qs[last[1], :], blank, blank,
+            qs[last[0], :], qs[last[1], :],
         ]
         for r, value in enumerate(extra):
-            pay_ref[s.exchange_slice(s.modes + r, h, FORWARD_EXTRA), :] = value
+            pay_s[forward_slice(s, 2 * s.modes + r, h), :] = value
 
     each_half(s, half)
+    narrowed(pay_s, pay_ref)
 
 
 def forward_middle(length, rates, taps, ends, extras):
@@ -246,7 +278,7 @@
             kc = kd = vc = vd = blank
         prod0 = mix(taps[1], k0, kb, ka) * mix(taps[2], v0, vb, va)
         prod1 = mix(taps[1], k1, k0, kb) * mix(taps[2], v1, v0, vb)
-        result.append((arriving, [prod0, prod1, ka, kb, va, vb, qa, qb, kc, kd, vc, vd]))
+        result.append((arriving, [ka, kb, va, vb, qa, qb, kc, kd, vc, vd]))
         arriving = whole * arriving + (ends[i] + step0 * prod0 + step1 * prod1)
     return result
 
@@ -263,63 +295,79 @@
     return result
 
 
-def middle_kernel(s, extra, in_ref, decay_ref, filter_ref, out_ref):
+def middle_kernel(s, forward, pay_ref, decay_ref, filter_ref, back_ref, *wide):
     me = lax.axis_index("seq")
-    rows = s.chunk_rows(extra)
+    lead, extra = (2 * s.modes, FORWARD_EXTRA) if forward else (s.modes, BACKWARD_EXTRA)
+    in_ref, out_ref = wide if forward else (pay_ref, back_ref)
+    if forward:
+        widened(pay_ref, in_ref)
+    rows = s.chunk_rows(lead, extra)
     for h in range(s.halves):
         lanes = pl.ds(pl.multiple_of((me + h * SUB) * LANES, LANES), LANES)
         rates = decay_ref[:, lanes]
         ends, extras = [], []
         for i in range(s.devices):
-            base = i * rows
-            e = base + s.chunk_row(0, h, extra)
-            ends.append(in_ref[e : e + s.modes, :])
-            x = base + s.chunk_row(s.modes, h, extra)
+            e = i * rows + s.chunk_row(0, h, lead, extra)
+            end = in_ref[e : e + s.modes, :]
+            ends.append(end + in_ref[e + s.modes : e + lead, :] if forward else end)
+            x = i * rows + s.chunk_row(lead, h, lead, extra)
             extras.append([in_ref[x + r : x + r + 1, :] for r in range(extra)])
-        if extra == FORWARD_EXTRA:
+        if forward:
             taps = [[filter_ref[i, tap : tap + 1, lanes] for tap in range(3)] for i in range(3)]
             result = forward_middle(s.length, rates, taps, ends, extras)
         else:
             result = backward_middle(s.length, rates, ends, extras)
-        for i in range(s.devices):
-            base = i * rows
-            e = base + s.chunk_row(0, h, extra)
-            out_ref[e : e + s.modes, :] = result[i][0]
-            x = base + s.chunk_row(s.modes, h, extra)
+        for i, (state, more) in enumerate(result):
+            e = i * rows + s.chunk_row(0, h, lead, extra)
+            if forward:
+                out_ref[e : e + s.modes, :], out_ref[e + s.modes : e + lead, :] = split(state)
+            else:
+                out_ref[e : e + s.modes, :] = state
+            x = i * rows + s.chunk_row(lead, h, lead, extra)
             for r in range(extra):
-                out_ref[x + r : x + r + 1, :] = result[i][1][r]
-
-
-def exchange(s, pay, decay_rate, short_filter, extra):
+                out_ref[x + r : x + r + 1, :] = more[r]
+    if forward:
+        narrowed(out_ref, back_ref)
+
+
+def exchange(s, pay, decay_rate, short_filter, forward):
+    lead, extra = (2 * s.modes, FORWARD_EXTRA) if forward else (s.modes, BACKWARD_EXTRA)
     if s.direct:
-        got = lax.all_to_all(pay, "seq", 0, 0, tiled=True)
+        chunks = (s.devices, s.chunk_rows(lead, extra), LANES)
+        got = lax.all_to_all(pay.reshape(chunks), "seq", 0, 0, tiled=True)
         back = pl.pallas_call(
-            functools.partial(middle_kernel, s, extra),
-            out_shape=jax.ShapeDtypeStruct(pay.shape, f32),
+            functools.partial(middle_kernel, s, forward),
+            out_shape=jax.ShapeDtypeStruct(pay.shape, pay.dtype),
+            scratch_shapes=[pltpu.VMEM(pay.shape, f32)] * 2 if forward else [],
             compiler_params=pltpu.CompilerParams(vmem_limit_bytes=GRANT),
-        )(got, decay_rate, short_filter)
-        return lax.all_to_all(back, "seq", 0, 0, tiled=True)
-    rows = s.modes + extra
+        )(got.reshape(pay.shape), decay_rate, short_filter)
+        return lax.all_to_all(back.reshape(chunks), "seq", 0, 0, tiled=True).reshape(pay.shape)
+    rows = lead + extra
     width = s.channels // s.devices
     start = lax.axis_index("seq") * width
     rates = lax.dynamic_slice_in_dim(decay_rate, start, width, 1)
     part = lax.dynamic_slice_in_dim(short_filter, start, width, 2)
     pay = pay.reshape(rows, s.devices, width).transpose(1, 0, 2)
-    got = lax.all_to_all(pay, "seq", 0, 0, tiled=True)
+    got = lax.all_to_all(pay, "seq", 0, 0, tiled=True).astype(f32)
     ends = [got[i, : s.modes] for i in range(s.devices)]
-    extras = [[got[i, s.modes + r][None] for r in range(extra)] for i in range(s.devices)]
-    if extra == FORWARD_EXTRA:
+    extras = [[got[i, lead + r][None] for r in range(extra)] for i in range(s.devices)]
+    if forward:
+        ends = [end + got[i, s.modes : lead] for i, end in enumerate(ends)]
         taps = [[part[i, tap][None] for tap in range(3)] for i in range(3)]
         result = forward_middle(s.length, rates, taps, ends, extras)
+        highs = [lax.reduce_precision(state, 8, 7) for state, _ in result]
+        result = [
+            (jnp.concatenate([high, state - high]), more) for high, (state, more) in zip(highs, result)
+        ]
     else:
         result = backward_middle(s.length, rates, ends, extras)
     back = jnp.stack([jnp.concatenate([state] + list(more)) for state, more in result])
-    back = lax.all_to_all(back, "seq", 0, 0, tiled=True)
+    back = lax.all_to_all(back.astype(pay.dtype), "seq", 0, 0, tiled=True)
     return back.transpose(1, 0, 2).reshape(rows * s.tiles, LANES)
 
 
 def inside_kernel(
-    s, k_hbm, v_hbm, filter_hbm, decay_hbm, residue_hbm, inside_ref,
+    s, k_hbm, v_hbm, filter_hbm, decay_hbm, residue_hbm, inside_ref, first_ref,
     kb, vb, fb, db, rb, ks, vs, prod, taps, poles, weights, sems,
 ):
     pairs = [(decay_hbm, db), (residue_hbm, rb), (filter_hbm, fb), (k_hbm, kb), (v_hbm, vb)]
@@ -352,34 +400,48 @@
             return k1, k2, v1, v2
 
         lax.fori_loop(0, steps, products, (blank,) * 4)
+        for i, (ref, part) in enumerate(((ks, taps_k), (vs, taps_v))):
+            x0, x1 = (ref[staged(s, 0, offset, h), :] for offset in range(2))
+            first_ref[major(s, 2 * i, h), :] = part[0] * x0
+            first_ref[major(s, 2 * i + 1, h), :] = part[0] * x1 + part[1] * x0
         recur(s, prod, inside_ref, mode_tiles(s, poles, h), mode_tiles(s, weights, h), [blank] * s.modes, h)
 
     each_half(s, half)
 
 
 def forward_kernel(
-    s, inside_ref, q_ref, stream_ref, cot_ref, back_ref, filter_ref, decay_ref, residue_ref, gain_ref,
-    conv_ref, sums_ref,
-    qs, xs, gs, taps, poles, weights, squares, inners,
+    s, inside_ref, first_ref, q_ref, stream_ref, cot_ref, back_ref, filter_ref, decay_ref, residue_ref, gain_ref,
+    conv_ref, sums_ref, near_ref,
+    qs, xs, gs, back_s, taps, poles, weights, squares, inners,
 ):
     stage_modes(s, decay_ref, poles, lambda x: jnp.exp(-x))
     stage_modes(s, residue_ref, weights, lambda x: x)
     stage_taps(s, filter_ref, taps)
 
-    def back(r, h):
-        return back_ref[s.exchange_slice(r, h, FORWARD_EXTRA), :]
-
+    widened(back_ref, back_s)
     steps = s.length // 16
 
     def half(h):
         p = mode_tiles(s, poles, h)
         w = mode_tiles(s, weights, h)
         gain = gain_ref[pl.ds(aligned(h * SUB, SUB), SUB), :]
-        taps_q = tap_tiles(s, taps, 0, h)
-        conv, states = [], [back(m, h) for m in range(s.modes)]
+        taps_q, taps_k, taps_v = (tap_tiles(s, taps, i, h) for i in range(3))
+        near = [back_s[forward_slice(s, 2 * s.modes + r, h), :] for r in range(FORWARD_EXTRA)]
+        for r, value in enumerate(near):
+            near_ref[major(s, r, h), :] = value
+        ka, kb, va, vb, qa, qb = near[:6]
+        k0, k1, v0, v1 = (first_ref[major(s, r, h), :] for r in range(4))
+        products = [
+            (k0 + taps_k[1] * kb + taps_k[2] * ka) * (v0 + taps_v[1] * vb + taps_v[2] * va),
+            (k1 + taps_k[2] * kb) * (v1 + taps_v[2] * vb),
+        ]
+        conv = []
+        states = [
+            back_s[forward_slice(s, m, h), :] + back_s[forward_slice(s, s.modes + m, h), :]
+            for m in range(s.modes)
+        ]
         for offset in range(2):
-            product = back(s.modes + offset, h)
-            states = [p[m] * states[m] + product for m in range(s.modes)]
+            states = [p[m] * states[m] + products[offset] for m in range(s.modes)]
             conv.append(total([w[m] * states[m] for m in range(s.modes)]))
         states = [w[m] * states[m] / (p[m] * p[m]) for m in range(s.modes)]
         first, ahead = [], states
@@ -415,7 +477,7 @@
             return (q1, q2), states
 
         bring(0)
-        lax.fori_loop(0, steps, step, ((back(s.modes + 7, h), back(s.modes + 6, h)), states))
+        lax.fori_loop(0, steps, step, ((qb, qa), states))
 
     each_half(s, half)
     for r, ref in enumerate((squares, inners)):
@@ -429,7 +491,7 @@
 
 
 def norm_kernel(
-    s, width, sums_ref, conv_ref, q_ref, stream_ref, cot_ref, back_ref, filter_ref, decay_ref, gain_ref,
+    s, width, sums_ref, conv_ref, q_ref, stream_ref, cot_ref, near_ref, filter_ref, decay_ref, gain_ref,
     normed_hbm, dstream_hbm, qgrad_hbm, dconv_ref, tail_ref, pay_ref,
     qs, xs, gs, ns, ds, normed_b, dstream_b, qgrad_b, taps, poles, inv_s, coef_s, sems,
 ):
@@ -441,9 +503,6 @@
     stage_taps(s, filter_ref, taps)
     blank = jnp.zeros((SUB, LANES), f32)
     steps = s.length // 16
-
-    def back(r, h):
-        return back_ref[s.exchange_slice(r, h, FORWARD_EXTRA), :]
 
     def pieces(h):
         cut = columns(h)
@@ -490,7 +549,7 @@
             return q1, q2, dq1, dq2
 
         bring(0)
-        held = (back(s.modes + 7, h), back(s.modes + 6, h), blank, blank)
+        held = (near_ref[major(s, 5, h), :], near_ref[major(s, 4, h), :], blank, blank)
         _, _, dq1, dq2 = lax.fori_loop(0, steps, step, held)
         qs[staged(s, 2 * steps + 1, 6, h), :] = taps_q[0] * dq2 + taps_q[1] * dq1
         qs[staged(s, 2 * steps + 1, 7, h), :] = taps_q[0] * dq1
@@ -513,10 +572,10 @@
 
         states = lax.fori_loop(0, steps, step, [blank] * s.modes)
         for m in range(s.modes):
-            pay_ref[s.exchange_slice(m, h, BACKWARD_EXTRA), :] = states[m]
+            pay_ref[backward_slice(s, m, h), :] = states[m]
         first = [ds[staged(s, 0, offset, h), :] * conv_ref[major(s, offset, h), :] for offset in range(2)]
         for r, value in enumerate([dconv_ref[major(s, 0, h), :], *first, blank]):
-            pay_ref[s.exchange_slice(s.modes + r, h, BACKWARD_EXTRA), :] = value
+            pay_ref[backward_slice(s, s.modes + r, h), :] = value
 
     each_half(s, ends)
 
@@ -528,7 +587,7 @@
 
 
 def backward_kernel(
-    s, k_ref, v_ref, dconv_ref, tail_ref, ahead_ref, back_ref, filter_ref, decay_ref, residue_ref, qgrad_in,
+    s, k_ref, v_ref, dconv_ref, tail_ref, near_ref, back_ref, filter_ref, decay_ref, residue_ref, qgrad_in,
     qgrad_hbm, kgrad_hbm, vgrad_hbm,
     ks, vs, dprod, qs, kgrad_b, vgrad_b, qgrad_b, taps, poles, weights, sems,
 ):
@@ -538,11 +597,8 @@
     stage_taps(s, filter_ref, taps)
     steps = s.length // 16
 
-    def near(r, h):
-        return ahead_ref[s.exchange_slice(s.modes + r, h, FORWARD_EXTRA), :]
-
     def back(r, h):
-        return back_ref[s.exchange_slice(r, h, BACKWARD_EXTRA), :]
+        return back_ref[backward_slice(s, r, h), :]
 
     qs[...] = tail_ref[...]
 
@@ -586,7 +642,7 @@
             return (k1, k2, v1, v2), (dk0, dk1, dv0, dv1), out
 
         bring(steps - 1)
-        ka, kb, va, vb, _, _, kc, kd, vc, vd = (near(2 + r, h) for r in range(10))
+        ka, kb, va, vb, _, _, kc, kd, vc, vd = (near_ref[major(s, r, h), :] for r in range(10))
         for ref, rows in ((ks, (ka, kb)), (vs, (va, vb))):
             for offset in range(2):
                 ref[staged(s, 1, 6 + offset, h), :] = rows[offset]
@@ -667,8 +723,8 @@
             compiler_params=pltpu.CompilerParams(vmem_limit_bytes=GRANT),
         )(*operands)
 
-    def pay_shape(extra):
-        return jax.ShapeDtypeStruct(s.exchange_shape(extra), f32)
+    forward_shape = s.exchange_shape(2 * modes, FORWARD_EXTRA)
+    near_shape = jax.ShapeDtypeStruct((FORWARD_EXTRA * s.tiles, LANES), f32)
 
     def far(*arrays):
         return [pltpu.with_memory_space_constraint(x, pltpu.HBM) for x in arrays]
@@ -682,42 +738,43 @@
     rates_s = pltpu.VMEM(decay_rate.shape, f32)
     (pay,) = call(
         begin_kernel, "hhhhh", "v",
-        (pay_shape(FORWARD_EXTRA),),
+        (jax.ShapeDtypeStruct(forward_shape, bf16),),
         [narrow_s, narrow_s, last_s, filter_s, rates_s]
-        + [wide_s, wide_s, tail_s, taps_s, mode_s, pltpu.SemaphoreType.DMA((3 + 2 * s.halves,))],
+        + [wide_s, wide_s, tail_s, pltpu.VMEM(forward_shape, f32), taps_s, mode_s]
+        + [pltpu.SemaphoreType.DMA((3 + 2 * s.halves,))],
         far(query_in, key_in, value_in, short_filter, decay_rate),
     )
-    (inside,) = call(
-        inside_kernel, "hhhhh", "v", (wide,),
+    inside, first = call(
+        inside_kernel, "hhhhh", "vv", (wide, jax.ShapeDtypeStruct((4 * s.tiles, LANES), f32)),
         [narrow_s, narrow_s, filter_s, rates_s, rates_s]
         + [wide_s] * 3 + [taps_s, mode_s, mode_s, pltpu.SemaphoreType.DMA((5,))],
         far(key_in, value_in, short_filter, decay_rate, residue),
         cost=cost(75, 3),
     )
-    back = exchange(s, pay, decay_rate, short_filter, FORWARD_EXTRA)
-    conv, sums = call(
-        forward_kernel, "v" * 9, "vv",
-        (wide, jax.ShapeDtypeStruct((2, length), f32)),
-        [wide_s] * 3 + [taps_s, mode_s, mode_s, sum_s, sum_s],
-        (inside, query_in, stream, cotangent, back, short_filter, decay_rate, residue, gain),
+    back = exchange(s, pay, decay_rate, short_filter, True)
+    conv, sums, near = call(
+        forward_kernel, "v" * 10, "vvv",
+        (wide, jax.ShapeDtypeStruct((2, length), f32), near_shape),
+        [wide_s] * 3 + [pltpu.VMEM(forward_shape, f32), taps_s, mode_s, mode_s, sum_s, sum_s],
+        (inside, first, query_in, stream, cotangent, back, short_filter, decay_rate, residue, gain),
         {0: 0},
     )
     sums = lax.psum(sums, "tp")
     normed, dstream, query_grad, dconv, tail, pay_back = call(
         lambda s, *refs: norm_kernel(s, total_width, *refs), "v" * 9, "hhhvvv",
-        (narrow, narrow, narrow, wide, jax.ShapeDtypeStruct((rows, LANES), f32), pay_shape(BACKWARD_EXTRA)),
+        (narrow, narrow, narrow, wide, jax.ShapeDtypeStruct((rows, LANES), f32), jax.ShapeDtypeStruct(s.exchange_shape(modes, BACKWARD_EXTRA), f32)),
         [pltpu.VMEM(((length + 32) * s.tiles, LANES), f32)] + [longer_s] * 2 + [wide_s] * 2 + [narrow_s] * 2
         + [pltpu.VMEM((length + 16, channels), bf16)]
         + [taps_s, mode_s, square_s, square_s, pltpu.SemaphoreType.DMA((3 * s.halves,))],
-        (sums, conv, query_in, stream, cotangent, back, short_filter, decay_rate, gain),
+        (sums, conv, query_in, stream, cotangent, near, short_filter, decay_rate, gain),
     )
-    back_back = exchange(s, pay_back, decay_rate, short_filter, BACKWARD_EXTRA)
+    back_back = exchange(s, pay_back, decay_rate, short_filter, False)
     query_grad, key_grad, value_grad = call(
         backward_kernel, "v" * 9 + "h", "hhh",
         (narrow, narrow, narrow),
         [longer_s] * 2 + [wide_s, tail_s] + [narrow_s] * 2 + [last_s, taps_s, mode_s, mode_s]
         + [pltpu.SemaphoreType.DMA((1 + 2 * s.halves,))],
-        (key_in, value_in, dconv, tail, back, back_back, short_filter, decay_rate, residue, query_grad),
+        (key_in, value_in, dconv, tail, near, back_back, short_filter, decay_rate, residue, query_grad),
         {9: 0},
     )
     return (normed, dstream, query_grad, key_grad, value_grad)

time: 69.2 us -> 67.6 us (0.977)
  blocking collectives: 42.8 us -> 41.3 us
    all_to_all x3, blocking collectives: 37.1 us -> 35.7 us  [the longest x2 25.3 us: exchange(): got = lax.all_to_all(pay.reshape(chunks), 'seq', 0, 0, tiled=True)]
where the time goes in v1:
time: 67.6 us; the launch traced here: 67.1 us
  blocking collectives  41.3 us (61%)
  Pallas kernels  18.4 us (27%)
  starting transfers between devices  3.52 us (5%)
  waiting for transfers between devices  3.02 us (4%)
  between operations  0.78 us (1%)
    all_to_all x2, blocking collectives, exchange(): got = lax.all_to_all(pay.reshape(chunks), 'seq', 0, 0, tiled=True)  25.3 us
    pallas_call x5, Pallas kernels, call(): pl.pallas_call(functools.partial(kernel, s), in_specs=[there if c == 'h'...  17.6 us
    all_to_all x1, blocking collectives, exchange(): lax.all_to_all(back.reshape(chunks), 'seq', 0, 0, tiled=True)  10.4 us
    psum x1, blocking collectives, body(): sums = lax.psum(sums, 'tp')  5.67 us
    all_to_all x1, starting transfers between devices, exchange(): lax.all_to_all(back.reshape(chunks), 'seq', 0, 0, tiled=True)  3.52 us
    all_to_all x1, waiting for transfers between devices, exchange(): lax.all_to_all(back.reshape(chunks), 'seq', 0, 0, tiled=True)  3.02 us
  transfers between devices with their start and end apart: 1, of which 1 were waited for; matrix products, arithmetic and copies ran while one was open for 0% of the time, Pallas kernels for 7%

profile of v1, /device:TPU:0, one launch (start us, length us, event | category | flops | bytes accessed | tf_op | source)
XLA Modules:
  0.0 67.1 jit_solution(4586073613246383315)
XLA Ops:
  0.6 3.3 %shard_map.129 = bf16[704,128]{1,0:T(8,128)(2,1)S(1)} custom-call(bf16[128,2048]{1,0:T(8,128)(2,1)} %refs_2_.1, bf16[128,2048]{1,0:T(8,128)(2,1)} %k_ref.1, bf16[128,2048]{1,0:T(8,128)(2,1)} %v_ref.1, f32[3,3,2048]{2,1,0:T(4,128)} %filter_ref.7, f32[16,2048]{1,0:T(8,128)} %decay_ref.7), custom_call_target="tpu_custom_call" | custom-call | tf_op jit(solution)/shard_map/pallas_call | solution.py:715
  3.9 0.0 copy-start
  3.9 0.0 copy-start.2
  3.9 14.9 %all_to_all.20 = bf16[8,88,128]{2,1,0:T(8,128)(2,1)S(1)} all-to-all(bf16[8,88,128]{2,1,0:T(8,128)(2,1)S(1)} %bitcast.11), channel_id=1, replica_groups=mesh['seq'=8,'tp'=4] {'seq'}, dimensions={0} | all-to-all | bytes 360448 | tf_op jit(solution)/shard_map/all_to_all | solution.py:337
  18.9 0.0 copy-done
  18.9 0.0 copy-done.2
  18.9 0.0 copy-start.8
  18.9 0.8 %shard_map.130 = bf16[704,128]{1,0:T(8,128)(2,1)} custom-call(bf16[704,128]{1,0:T(8,128)(2,1)S(1)} %bitcast.10, f32[16,2048]{1,0:T(8,128)S(1)} %copy-done, f32[3,3,2048]{2,1,0:T(4,128)S(1)} %copy-done.2), custom_call_target="tpu_custom_call" | custom-call | tf_op jit(solution)/shard_map/pallas_call | solution.py:338
  19.7 0.0 copy-start.10
  19.7 3.5 %all-to-all-start.1 = ((bf16[8,88,128]{2,1,0:T(8,128)(2,1)}), bf16[8,88,128]{2,1,0:T(8,128)(2,1)S(1)}, u32[]{:S(2)}, u32[]{:S(2)}) async-start(bf16[8,88,128]{2,1,0:T(8,128)(2,1)} %bitcast.2), calls=%async_computation.1 | async-start | bytes 360448 | tf_op jit(solution)/shard_map/all_to_all | solution.py:344
  23.2 0.0 copy-start.1
  23.2 0.0 copy-start.3
  23.2 0.0 copy-start.4
  23.2 0.0 copy-start.7
  23.3 0.0 copy-start.9
  23.3 4.5 %shard_map.128 = (f32[2048,128]{1,0:T(8,128)S(1)}, f32[64,128]{1,0:T(8,128)S(1)}) custom-call(bf16[128,2048]{1,0:T(8,128)(2,1)} %k_ref.1, bf16[128,2048]{1,0:T(8,128)(2,1)} %v_ref.1, f32[3,3,2048]{2,1,0:T(4,128)} %filter_ref.7, f32[16,2048]{1,0:T(8,128)} %decay_ref.7, f32[16,2048]{1,0:T(8,128)} %residue_ref.3), custom_call_target="tpu_custom_call" | custom-call | flops 19660800 | bytes 3145728 | tf_op jit(solution)/shard_map/pallas_call | solution.py:715
  27.8 3.0 %all-to-all-done.1 = bf16[8,88,128]{2,1,0:T(8,128)(2,1)S(1)} async-done(((bf16[8,88,128]{2,1,0:T(8,128)(2,1)}), bf16[8,88,128]{2,1,0:T(8,128)(2,1)S(1)}, u32[]{:S(2)}, u32[]{:S(2)}) %all-to-all-start.1) | async-done | bytes 180256 | tf_op jit(solution)/shard_map/all_to_all | solution.py:344
  30.8 0.0 copy-done.8
  30.8 0.0 copy-done.10
  30.8 0.0 copy-done.1
  30.8 0.0 copy-done.3
  30.8 0.0 copy-done.4
  30.8 0.0 copy-done.7
  30.9 0.0 copy-done.9
  30.9 2.4 %shard_map.131 = (f32[2048,128]{1,0:T(8,128)S(1)}, f32[2,128]{1,0:T(2,128)S(1)}, f32[160,128]{1,0:T(8,128)S(1)}) custom-call(f32[2048,128]{1,0:T(8,128)S(1)} %get-tuple-element.19.inside_ref, f32[64,128]{1,0:T(8,128)S(1)} %get-tuple-element.20.first_ref, bf16[128,2048]{1,0:T(8,128)(2,1)S(1)} %copy-done.4, ...), custom_call_target="tpu_custom_call", output_to_operand_aliasing={{0}: (0, {})} | custom-call | tf_op jit(solution)/shard_map/pallas_call | solution.py:715
  33.2 5.7 %psum.7.refs_0_ = f32[2,128]{1,0:T(2,128)S(1)} all-reduce(f32[2,128]{1,0:T(2,128)S(1)} %get-tuple-element.21), channel_id=1, replica_groups=mesh['seq'=8,'tp'=4] {'tp'}, use_global_device_ids=true, to_apply=%region_0.0 | all-reduce | flops 256 | bytes 2048 | tf_op jit(solution)/shard_map/psum | solution.py:762
  38.9 2.8 %shard_map.132 = (bf16[128,2048]{1,0:T(8,128)(2,1)}, bf16[128,2048]{1,0:T(8,128)(2,1)}, bf16[128,2048]{1,0:T(8,128)(2,1)}, f32[2048,128]{1,0:T(8,128)S(1)}, f32[...) custom-call(f32[2,128]{1,0:T(2,128)S(1)} %psum.7.refs_0_, f32[2048,128]{1,0:T(8,128)S(1)} %get-tuple-element.22.refs_1_, ...), custom_call_target="tpu_custom_call" | custom-call | tf_op jit(solution)/shard_map/pallas_call | solution.py:715
  41.7 0.0 copy-start.6
  41.8 10.4 %all_to_all.21 = f32[8,40,128]{2,1,0:T(8,128)S(1)} all-to-all(f32[8,40,128]{2,1,0:T(8,128)S(1)} %bitcast.15), channel_id=1, replica_groups=mesh['seq'=8,'tp'=4] {'seq'}, dimensions={0} | all-to-all | bytes 327680 | tf_op jit(solution)/shard_map/all_to_all | solution.py:337
  52.2 0.0 copy-start.5
  52.2 10.4 %all_to_all.22 = f32[8,40,128]{2,1,0:T(8,128)S(1)} all-to-all(f32[8,40,128]{2,1,0:T(8,128)S(1)} %bitcast.14), channel_id=1, replica_groups=mesh['seq'=8,'tp'=4] {'seq'}, dimensions={0} | all-to-all | bytes 327680 | tf_op jit(solution)/shard_map/all_to_all | solution.py:344
  62.6 0.0 copy-done.6
  62.6 0.0 copy-done.5
  62.6 4.6 %shard_map.134 = (bf16[128,2048]{1,0:T(8,128)(2,1)}, bf16[128,2048]{1,0:T(8,128)(2,1)}, bf16[128,2048]{1,0:T(8,128)(2,1)}) custom-call(bf16[128,2048]{1,0:T(8,128)(2,1)S(1)} %copy-done.5, bf16[128,2048]{1,0:T(8,128)(2,1)S(1)} %copy-done.6, f32[2048,128]{1,0:T(8,128)S(1)} %get-tuple-element.26.dconv_ref, ...), custom_call_target="tpu_custom_call", output_to_operand_aliasing={{0}: (9, {})} | custom-call | tf_op jit(solution)/shard_map/pallas_call | solution.py:715
  (1 shorter events, 0.0 us)
Async XLA Ops:
  3.9 14.9 %copy-start = (f32[16,2048]{1,0:T(8,128)S(1)}, f32[16,2048]{1,0:T(8,128)}, u32[]{:S(2)}) copy-start(f32[16,2048]{1,0:T(8,128)} %decay_ref.7) | copy-start | bytes 393220
  3.9 14.9 %copy-start.2 = (f32[3,3,2048]{2,1,0:T(4,128)S(1)}, f32[3,3,2048]{2,1,0:T(4,128)}, u32[]{:S(2)}) copy-start(f32[3,3,2048]{2,1,0:T(4,128)} %filter_ref.7) | copy-start | bytes 221188
  18.9 12.0 %copy-start.8 = (bf16[128,2048]{1,0:T(8,128)(2,1)S(1)}, bf16[128,2048]{1,0:T(8,128)(2,1)}, u32[]{:S(2)}) copy-start(bf16[128,2048]{1,0:T(8,128)(2,1)} %refs_4_.1) | copy-start | bytes 1572868
  19.7 11.1 %copy-start.10 = (f32[2048]{0:T(1024)S(1)}, f32[2048]{0:T(1024)}, u32[]{:S(2)}) copy-start(f32[2048]{0:T(1024)} %param.16) | copy-start | bytes 24580
  19.7 11.1 %all-to-all-start.1 = ((bf16[8,88,128]{2,1,0:T(8,128)(2,1)}), bf16[8,88,128]{2,1,0:T(8,128)(2,1)S(1)}, u32[]{:S(2)}, u32[]{:S(2)}) async-start(bf16[8,88,128]{2,1,0:T(8,128)(2,1)} %bitcast.2), calls=%async_computation.1 | async-start | bytes 360448 | tf_op jit(solution)/shard_map/all_to_all | solution.py:344
  23.2 7.6 %copy-start.1 = (f32[16,2048]{1,0:T(8,128)S(1)}, f32[16,2048]{1,0:T(8,128)}, u32[]{:S(2)}) copy-start(f32[16,2048]{1,0:T(8,128)} %decay_ref.7) | copy-start | bytes 393220
  23.2 7.6 %copy-start.3 = (f32[3,3,2048]{2,1,0:T(4,128)S(1)}, f32[3,3,2048]{2,1,0:T(4,128)}, u32[]{:S(2)}) copy-start(f32[3,3,2048]{2,1,0:T(4,128)} %filter_ref.7) | copy-start | bytes 221188
  23.2 7.6 %copy-start.4 = (bf16[128,2048]{1,0:T(8,128)(2,1)S(1)}, bf16[128,2048]{1,0:T(8,128)(2,1)}, u32[]{:S(2)}) copy-start(bf16[128,2048]{1,0:T(8,128)(2,1)} %refs_2_.1) | copy-start | bytes 1572868
  23.2 7.6 %copy-start.7 = (bf16[128,2048]{1,0:T(8,128)(2,1)S(1)}, bf16[128,2048]{1,0:T(8,128)(2,1)}, u32[]{:S(2)}) copy-start(bf16[128,2048]{1,0:T(8,128)(2,1)} %refs_3_.1) | copy-start | bytes 1572868
  23.3 7.6 %copy-start.9 = (f32[16,2048]{1,0:T(8,128)S(1)}, f32[16,2048]{1,0:T(8,128)}, u32[]{:S(2)}) copy-start(f32[16,2048]{1,0:T(8,128)} %residue_ref.3) | copy-start | bytes 393220
  41.7 20.8 %copy-start.6 = (bf16[128,2048]{1,0:T(8,128)(2,1)S(1)}, bf16[128,2048]{1,0:T(8,128)(2,1)}, u32[]{:S(2)}) copy-start(bf16[128,2048]{1,0:T(8,128)(2,1)} %v_ref.1) | copy-start | bytes 1572868
  52.2 10.4 %copy-start.5 = (bf16[128,2048]{1,0:T(8,128)(2,1)S(1)}, bf16[128,2048]{1,0:T(8,128)(2,1)}, u32[]{:S(2)}) copy-start(bf16[128,2048]{1,0:T(8,128)(2,1)} %k_ref.1) | copy-start | bytes 1572868

commit v2 on v1

--- a/solution.py
+++ b/solution.py
@@ -151,6 +151,24 @@
     return taps[0] * now + taps[1] * before + taps[2] * before2
 
 
+def products(s, k_ref, v_ref, ks, vs, to_ref, taps_k, taps_v, h):
+    def step(i, held):
+        stage(s, k_ref, ks, i, h)
+        stage(s, v_ref, vs, i, h)
+        k1, k2, v1, v2 = held
+        for block, offset in sixteen(0):
+            rows = staged(s, 2 * i + block, offset, h)
+            k0, v0 = ks[rows, :], vs[rows, :]
+            product = mix(taps_k, k0, k1, k2) * mix(taps_v, v0, v1, v2)
+            if block == 0 and offset < 2:
+                product = jnp.where(i == 0, 0.0, product)
+            to_ref[major(s, (2 * i + block) * SUB + offset, h), :] = product
+            k1, k2, v1, v2 = k0, k1, v0, v1
+        return k1, k2, v1, v2
+
+    return lax.fori_loop(0, s.length // 16, step, (jnp.zeros((SUB, LANES), f32),) * 4)
+
+
 def recur(s, from_ref, to_ref, p, w, states, h, reverse=False):
     steps = s.length // 16
 
@@ -200,7 +218,7 @@
 
 def begin_kernel(
     s, q_hbm, k_hbm, v_hbm, filter_hbm, decay_hbm, pay_ref,
-    kb, vb, qb, fb, db, ks, vs, qs, pay_s, taps, poles, sems,
+    kb, vb, qb, fb, db, ks, vs, prod, qs, pay_s, taps, poles, sems,
 ):
     copies = [(decay_hbm, db), (filter_hbm, fb), (q_hbm.at[pl.ds(s.length - 16, 16), :], qb)]
     for h in range(s.halves):
@@ -214,7 +232,6 @@
     copies[1].wait()
     stage_taps(s, fb, taps)
     blank = jnp.zeros((SUB, LANES), f32)
-    steps = s.length // 16
     copies[2].wait()
     stage_wide(s, qb, qs)
 
@@ -225,25 +242,15 @@
         p = mode_tiles(s, poles, h)
         taps_k, taps_v = (tap_tiles(s, taps, i, h) for i in (1, 2))
 
-        def bring(i):
-            stage(s, kb, ks, i, h)
-            stage(s, vb, vs, i, h)
-
-        def step(i, carry):
-            (k1, k2, v1, v2), states = carry
+        held = products(s, kb, vb, ks, vs, prod, taps_k, taps_v, h)
+
+        def step(i, states):
             for block, offset in sixteen(0):
-                rows = staged(s, 2 * i + block, offset, h)
-                k0, v0 = ks[rows, :], vs[rows, :]
-                product = mix(taps_k, k0, k1, k2) * mix(taps_v, v0, v1, v2)
-                if block == 0 and offset < 2:
-                    product = jnp.where(i == 0, 0.0, product)
+                product = prod[major(s, (2 * i + block) * SUB + offset, h), :]
                 states = [p[m] * states[m] + product for m in range(s.modes)]
-                k1, k2, v1, v2 = k0, k1, v0, v1
-            bring(jnp.minimum(i + 1, steps - 1))
-            return (k1, k2, v1, v2), states
-
-        bring(0)
-        held, states = lax.fori_loop(0, steps, step, ((blank,) * 4, [blank] * s.modes))
+            return states
+
+        states = lax.fori_loop(0, s.length // 16, step, [blank] * s.modes)
         put_states(s, pay_s, states, h)
         k1, k2, v1, v2 = held
         first = [staged(s, 0, offset, h) for offset in range(2)]
@@ -367,8 +374,8 @@
 
 
 def inside_kernel(
-    s, k_hbm, v_hbm, filter_hbm, decay_hbm, residue_hbm, inside_ref, first_ref,
-    kb, vb, fb, db, rb, ks, vs, prod, taps, poles, weights, sems,
+    s, k_hbm, v_hbm, filter_hbm, decay_hbm, residue_hbm, inside_ref, first_ref, taps, poles, weights,
+    kb, vb, fb, db, rb, ks, vs, prod, sems,
 ):
     pairs = [(decay_hbm, db), (residue_hbm, rb), (filter_hbm, fb), (k_hbm, kb), (v_hbm, vb)]
     copies = [pltpu.make_async_copy(a, b, sems.at[i]) for i, (a, b) in enumerate(pairs)]
@@ -380,26 +387,11 @@
     stage_modes(s, rb, weights, lambda x: x)
     stage_taps(s, fb, taps)
     blank = jnp.zeros((SUB, LANES), f32)
-    steps = s.length // 16
 
     def half(h):
         taps_k, taps_v = (tap_tiles(s, taps, i, h) for i in (1, 2))
 
-        def products(i, held):
-            stage(s, kb, ks, i, h)
-            stage(s, vb, vs, i, h)
-            k1, k2, v1, v2 = held
-            for block, offset in sixteen(0):
-                rows = staged(s, 2 * i + block, offset, h)
-                k0, v0 = ks[rows, :], vs[rows, :]
-                product = mix(taps_k, k0, k1, k2) * mix(taps_v, v0, v1, v2)
-                if block == 0 and offset < 2:
-                    product = jnp.where(i == 0, 0.0, product)
-                prod[major(s, (2 * i + block) * SUB + offset, h), :] = product
-                k1, k2, v1, v2 = k0, k1, v0, v1
-            return k1, k2, v1, v2
-
-        lax.fori_loop(0, steps, products, (blank,) * 4)
+        products(s, kb, vb, ks, vs, prod, taps_k, taps_v, h)
         for i, (ref, part) in enumerate(((ks, taps_k), (vs, taps_v))):
             x0, x1 = (ref[staged(s, 0, offset, h), :] for offset in range(2))
             first_ref[major(s, 2 * i, h), :] = part[0] * x0
@@ -410,14 +402,10 @@
 
 
 def forward_kernel(
-    s, inside_ref, first_ref, q_ref, stream_ref, cot_ref, back_ref, filter_ref, decay_ref, residue_ref, gain_ref,
+    s, inside_ref, first_ref, q_ref, stream_ref, cot_ref, back_ref, taps, poles, weights, gain_ref,
     conv_ref, sums_ref, near_ref,
-    qs, xs, gs, back_s, taps, poles, weights, squares, inners,
+    qs, xs, gs, back_s, squares, inners,
 ):
-    stage_modes(s, decay_ref, poles, lambda x: jnp.exp(-x))
-    stage_modes(s, residue_ref, weights, lambda x: x)
-    stage_taps(s, filter_ref, taps)
-
     widened(back_ref, back_s)
     steps = s.length // 16
 
@@ -491,16 +479,14 @@
 
 
 def norm_kernel(
-    s, width, sums_ref, conv_ref, q_ref, stream_ref, cot_ref, near_ref, filter_ref, decay_ref, gain_ref,
+    s, width, sums_ref, conv_ref, q_ref, stream_ref, cot_ref, near_ref, taps, poles, gain_ref,
     normed_hbm, dstream_hbm, qgrad_hbm, dconv_ref, tail_ref, pay_ref,
-    qs, xs, gs, ns, ds, normed_b, dstream_b, qgrad_b, taps, poles, inv_s, coef_s, sems,
+    qs, xs, gs, ns, ds, normed_b, dstream_b, qgrad_b, inv_s, coef_s, sems,
 ):
     inverse = lax.rsqrt(sums_ref[0:1, :] / width + epsilon)
     coef = inverse * inverse * inverse * sums_ref[1:2, :] / width
     inv_s[...] = jnp.broadcast_to(inverse, (LANES, s.length)).T
     coef_s[...] = jnp.broadcast_to(coef, (LANES, s.length)).T
-    stage_modes(s, decay_ref, poles, lambda x: jnp.exp(-x))
-    stage_taps(s, filter_ref, taps)
     blank = jnp.zeros((SUB, LANES), f32)
     steps = s.length // 16
 
@@ -587,14 +573,11 @@
 
 
 def backward_kernel(
-    s, k_ref, v_ref, dconv_ref, tail_ref, near_ref, back_ref, filter_ref, decay_ref, residue_ref, qgrad_in,
+    s, k_ref, v_ref, dconv_ref, tail_ref, near_ref, back_ref, taps, poles, weights, qgrad_in,
     qgrad_hbm, kgrad_hbm, vgrad_hbm,
-    ks, vs, dprod, qs, kgrad_b, vgrad_b, qgrad_b, taps, poles, weights, sems,
+    ks, vs, dprod, qs, kgrad_b, vgrad_b, qgrad_b, sems,
 ):
     del qgrad_in
-    stage_modes(s, decay_ref, poles, lambda x: jnp.exp(-x))
-    stage_modes(s, residue_ref, weights, lambda x: x)
-    stage_taps(s, filter_ref, taps)
     steps = s.length // 16
 
     def back(r, h):
@@ -740,14 +723,15 @@
         begin_kernel, "hhhhh", "v",
         (jax.ShapeDtypeStruct(forward_shape, bf16),),
         [narrow_s, narrow_s, last_s, filter_s, rates_s]
-        + [wide_s, wide_s, tail_s, pltpu.VMEM(forward_shape, f32), taps_s, mode_s]
+        + [wide_s] * 3 + [tail_s, pltpu.VMEM(forward_shape, f32), taps_s, mode_s]
         + [pltpu.SemaphoreType.DMA((3 + 2 * s.halves,))],
         far(query_in, key_in, value_in, short_filter, decay_rate),
     )
-    inside, first = call(
-        inside_kernel, "hhhhh", "vv", (wide, jax.ShapeDtypeStruct((4 * s.tiles, LANES), f32)),
+    inside, first, taps, poles, weights = call(
+        inside_kernel, "hhhhh", "vvvvv",
+        (wide, *(jax.ShapeDtypeStruct(x, f32) for x in ((4 * s.tiles, LANES), taps_s.shape, mode_s.shape, mode_s.shape))),
         [narrow_s, narrow_s, filter_s, rates_s, rates_s]
-        + [wide_s] * 3 + [taps_s, mode_s, mode_s, pltpu.SemaphoreType.DMA((5,))],
+        + [wide_s] * 3 + [pltpu.SemaphoreType.DMA((5,))],
         far(key_in, value_in, short_filter, decay_rate, residue),
         cost=cost(75, 3),
     )
@@ -755,8 +739,8 @@
     conv, sums, near = call(
         forward_kernel, "v" * 10, "vvv",
         (wide, jax.ShapeDtypeStruct((2, length), f32), near_shape),
-        [wide_s] * 3 + [pltpu.VMEM(forward_shape, f32), taps_s, mode_s, mode_s, sum_s, sum_s],
-        (inside, first, query_in, stream, cotangent, back, short_filter, decay_rate, residue, gain),
+        [wide_s] * 3 + [pltpu.VMEM(forward_shape, f32), sum_s, sum_s],
+        (inside, first, query_in, stream, cotangent, back, taps, poles, weights, gain),
         {0: 0},
     )
     sums = lax.psum(sums, "tp")
@@ -765,16 +749,16 @@
         (narrow, narrow, narrow, wide, jax.ShapeDtypeStruct((rows, LANES), f32), jax.ShapeDtypeStruct(s.exchange_shape(modes, BACKWARD_EXTRA), f32)),
         [pltpu.VMEM(((length + 32) * s.tiles, LANES), f32)] + [longer_s] * 2 + [wide_s] * 2 + [narrow_s] * 2
         + [pltpu.VMEM((length + 16, channels), bf16)]
-        + [taps_s, mode_s, square_s, square_s, pltpu.SemaphoreType.DMA((3 * s.halves,))],
-        (sums, conv, query_in, stream, cotangent, near, short_filter, decay_rate, gain),
+        + [square_s, square_s, pltpu.SemaphoreType.DMA((3 * s.halves,))],
+        (sums, conv, query_in, stream, cotangent, near, taps, poles, gain),
     )
     back_back = exchange(s, pay_back, decay_rate, short_filter, False)
     query_grad, key_grad, value_grad = call(
         backward_kernel, "v" * 9 + "h", "hhh",
         (narrow, narrow, narrow),
-        [longer_s] * 2 + [wide_s, tail_s] + [narrow_s] * 2 + [last_s, taps_s, mode_s, mode_s]
+        [longer_s] * 2 + [wide_s, tail_s] + [narrow_s] * 2 + [last_s]
         + [pltpu.SemaphoreType.DMA((1 + 2 * s.halves,))],
-        (key_in, value_in, dconv, tail, near, back_back, short_filter, decay_rate, residue, query_grad),
+        (key_in, value_in, dconv, tail, near, back_back, taps, poles, weights, query_grad),
         {9: 0},
     )
     return (normed, dstream, query_grad, key_grad, value_grad)

time: 67.6 us -> 68 us (level)
  no operation moved by 1% of the time
where the time goes in v2:
time: 68 us; the launch traced here: 67.6 us
  blocking collectives  41.9 us (62%)
  Pallas kernels  18.3 us (27%)
  starting transfers between devices  3.52 us (5%)
  waiting for transfers between devices  3.06 us (4%)
  between operations  0.74 us (1%)
    all_to_all x2, blocking collectives, exchange(): got = lax.all_to_all(pay.reshape(chunks), 'seq', 0, 0, tiled=True)  25.9 us
    pallas_call x5, Pallas kernels, call(): pl.pallas_call(functools.partial(kernel, s), in_specs=[there if c == 'h'...  17.4 us
    all_to_all x1, blocking collectives, exchange(): lax.all_to_all(back.reshape(chunks), 'seq', 0, 0, tiled=True)  10.4 us
    psum x1, blocking collectives, body(): sums = lax.psum(sums, 'tp')  5.67 us
    all_to_all x1, starting transfers between devices, exchange(): lax.all_to_all(back.reshape(chunks), 'seq', 0, 0, tiled=True)  3.52 us
    all_to_all x1, waiting for transfers between devices, exchange(): lax.all_to_all(back.reshape(chunks), 'seq', 0, 0, tiled=True)  3.06 us
  transfers between devices with their start and end apart: 1, of which 1 were waited for; matrix products, arithmetic and copies ran while one was open for 0% of the time, Pallas kernels for 7%

profile of v2, /device:TPU:0, one launch (start us, length us, event | category | flops | bytes accessed | tf_op | source)
XLA Modules:
  0.0 67.6 jit_solution(10604098015836317142)
XLA Ops:
  0.6 3.2 %shard_map.129 = bf16[704,128]{1,0:T(8,128)(2,1)S(1)} custom-call(bf16[128,2048]{1,0:T(8,128)(2,1)} %refs_2_.1, bf16[128,2048]{1,0:T(8,128)(2,1)} %k_ref.1, bf16[128,2048]{1,0:T(8,128)(2,1)} %v_ref.1, f32[3,3,2048]{2,1,0:T(4,128)} %filter_ref.3, f32[16,2048]{1,0:T(8,128)} %decay_ref.3), custom_call_target="tpu_custom_call" | custom-call | tf_op jit(solution)/shard_map/pallas_call | solution.py:698
  3.9 0.0 copy-start.5
  3.9 0.0 copy-start.7
  3.9 14.9 %all_to_all.20 = bf16[8,88,128]{2,1,0:T(8,128)(2,1)S(1)} all-to-all(bf16[8,88,128]{2,1,0:T(8,128)(2,1)S(1)} %bitcast.11), channel_id=1, replica_groups=mesh['seq'=8,'tp'=4] {'seq'}, dimensions={0} | all-to-all | bytes 360448 | tf_op jit(solution)/shard_map/all_to_all | solution.py:344
  18.8 0.0 copy-done.5
  18.8 0.0 copy-done.7
  18.8 0.8 %shard_map.130 = bf16[704,128]{1,0:T(8,128)(2,1)} custom-call(bf16[704,128]{1,0:T(8,128)(2,1)S(1)} %bitcast.10, f32[16,2048]{1,0:T(8,128)S(1)} %copy-done.5, f32[3,3,2048]{2,1,0:T(4,128)S(1)} %copy-done.7), custom_call_target="tpu_custom_call" | custom-call | tf_op jit(solution)/shard_map/pallas_call | solution.py:345
  19.6 0.0 copy-start.4
  19.6 3.5 %all-to-all-start.1 = ((bf16[8,88,128]{2,1,0:T(8,128)(2,1)}), bf16[8,88,128]{2,1,0:T(8,128)(2,1)S(1)}, u32[]{:S(2)}, u32[]{:S(2)}) async-start(bf16[8,88,128]{2,1,0:T(8,128)(2,1)} %bitcast.2), calls=%async_computation.1 | async-start | bytes 360448 | tf_op jit(solution)/shard_map/all_to_all | solution.py:351
  23.2 0.0 copy-start
  23.2 0.0 copy-start.3
  23.2 4.5 %shard_map.128 = (f32[2048,128]{1,0:T(8,128)S(1)}, f32[64,128]{1,0:T(8,128)S(1)}, f32[384,128]{1,0:T(8,128)S(1)}, f32[256,128]{1,0:T(8,128)S(1)}, f32[256,128]{1,0:T(8,128)S(1)}) custom-call(bf16[128,2048]{1,0:T(8,128)(2,1)} %k_ref.1, bf16[128,2048]{1,0:T(8,128)(2,1)} %v_ref.1, f32[3,3,2048]{2,1,0:T(4,128)} %filter_ref.3, f32[16,2048]{1,0:T(8,128)} %decay_ref.3, ...), custom_call_target="tpu_custom_call" | custom-call | flops 19660800 | bytes 3145728 | tf_op jit(solution)/shard_map/pallas_call | solution.py:698
  27.7 0.0 copy-start.9
  27.7 3.1 %all-to-all-done.1 = bf16[8,88,128]{2,1,0:T(8,128)(2,1)S(1)} async-done(((bf16[8,88,128]{2,1,0:T(8,128)(2,1)}), bf16[8,88,128]{2,1,0:T(8,128)(2,1)S(1)}, u32[]{:S(2)}, u32[]{:S(2)}) %all-to-all-start.1) | async-done | bytes 180256 | tf_op jit(solution)/shard_map/all_to_all | solution.py:351
  30.8 0.0 copy-done.4
  30.8 0.0 copy-done
  30.8 0.0 copy-done.3
  30.8 0.0 copy-done.9
  30.8 2.3 %shard_map.131 = (f32[2048,128]{1,0:T(8,128)S(1)}, f32[2,128]{1,0:T(2,128)S(1)}, f32[160,128]{1,0:T(8,128)S(1)}) custom-call(f32[2048,128]{1,0:T(8,128)S(1)} %get-tuple-element.22.inside_ref, f32[64,128]{1,0:T(8,128)S(1)} %get-tuple-element.23.first_ref, bf16[128,2048]{1,0:T(8,128)(2,1)S(1)} %copy-done, ...), custom_call_target="tpu_custom_call", output_to_operand_aliasing={{0}: (0, {})} | custom-call | tf_op jit(solution)/shard_map/pallas_call | solution.py:698
  33.1 5.7 %psum.7.refs_0_ = f32[2,128]{1,0:T(2,128)S(1)} all-reduce(f32[2,128]{1,0:T(2,128)S(1)} %get-tuple-element.27), channel_id=1, replica_groups=mesh['seq'=8,'tp'=4] {'tp'}, use_global_device_ids=true, to_apply=%region_0.0 | all-reduce | flops 256 | bytes 2048 | tf_op jit(solution)/shard_map/psum | solution.py:746
  38.8 0.0 copy-start.6
  38.8 0.0 copy-start.8
  38.8 2.8 %shard_map.132 = (bf16[128,2048]{1,0:T(8,128)(2,1)}, bf16[128,2048]{1,0:T(8,128)(2,1)}, bf16[128,2048]{1,0:T(8,128)(2,1)}, f32[2048,128]{1,0:T(8,128)S(1)}, f32[...) custom-call(f32[2,128]{1,0:T(2,128)S(1)} %psum.7.refs_0_, f32[2048,128]{1,0:T(8,128)S(1)} %get-tuple-element.28.refs_1_, ...), custom_call_target="tpu_custom_call" | custom-call | tf_op jit(solution)/shard_map/pallas_call | solution.py:698
  41.6 0.0 copy-start.2
  41.6 11.0 %all_to_all.21 = f32[8,40,128]{2,1,0:T(8,128)S(1)} all-to-all(f32[8,40,128]{2,1,0:T(8,128)S(1)} %bitcast.15), channel_id=1, replica_groups=mesh['seq'=8,'tp'=4] {'seq'}, dimensions={0} | all-to-all | bytes 327680 | tf_op jit(solution)/shard_map/all_to_all | solution.py:344
  52.6 0.0 copy-start.1
  52.6 0.0 copy-done.6
  52.6 0.0 copy-done.8
  52.7 10.4 %all_to_all.22 = f32[8,40,128]{2,1,0:T(8,128)S(1)} all-to-all(f32[8,40,128]{2,1,0:T(8,128)S(1)} %bitcast.13), channel_id=1, replica_groups=mesh['seq'=8,'tp'=4] {'seq'}, dimensions={0} | all-to-all | bytes 327680 | tf_op jit(solution)/shard_map/all_to_all | solution.py:351
  63.0 0.0 copy-done.2
  63.0 0.0 copy-done.1
  63.0 4.6 %shard_map.134 = (bf16[128,2048]{1,0:T(8,128)(2,1)}, bf16[128,2048]{1,0:T(8,128)(2,1)}, bf16[128,2048]{1,0:T(8,128)(2,1)}) custom-call(bf16[128,2048]{1,0:T(8,128)(2,1)S(1)} %copy-done.1, bf16[128,2048]{1,0:T(8,128)(2,1)S(1)} %copy-done.2, f32[2048,128]{1,0:T(8,128)S(1)} %get-tuple-element.32.dconv_ref, ...), custom_call_target="tpu_custom_call", output_to_operand_aliasing={{0}: (9, {})} | custom-call | tf_op jit(solution)/shard_map/pallas_call | solution.py:698
  (1 shorter events, 0.0 us)
Async XLA Ops:
  3.9 14.9 %copy-start.5 = (f32[16,2048]{1,0:T(8,128)S(1)}, f32[16,2048]{1,0:T(8,128)}, u32[]{:S(2)}) copy-start(f32[16,2048]{1,0:T(8,128)} %decay_ref.3) | copy-start | bytes 393220
  3.9 14.9 %copy-start.7 = (f32[3,3,2048]{2,1,0:T(4,128)S(1)}, f32[3,3,2048]{2,1,0:T(4,128)}, u32[]{:S(2)}) copy-start(f32[3,3,2048]{2,1,0:T(4,128)} %filter_ref.3) | copy-start | bytes 221188
  19.6 11.1 %copy-start.4 = (bf16[128,2048]{1,0:T(8,128)(2,1)S(1)}, bf16[128,2048]{1,0:T(8,128)(2,1)}, u32[]{:S(2)}) copy-start(bf16[128,2048]{1,0:T(8,128)(2,1)} %refs_4_.1) | copy-start | bytes 1572868
  19.6 11.1 %all-to-all-start.1 = ((bf16[8,88,128]{2,1,0:T(8,128)(2,1)}), bf16[8,88,128]{2,1,0:T(8,128)(2,1)S(1)}, u32[]{:S(2)}, u32[]{:S(2)}) async-start(bf16[8,88,128]{2,1,0:T(8,128)(2,1)} %bitcast.2), calls=%async_computation.1 | async-start | bytes 360448 | tf_op jit(solution)/shard_map/all_to_all | solution.py:351
  23.2 7.6 %copy-start = (bf16[128,2048]{1,0:T(8,128)(2,1)S(1)}, bf16[128,2048]{1,0:T(8,128)(2,1)}, u32[]{:S(2)}) copy-start(bf16[128,2048]{1,0:T(8,128)(2,1)} %refs_2_.1) | copy-start | bytes 1572868
  23.2 7.6 %copy-start.3 = (bf16[128,2048]{1,0:T(8,128)(2,1)S(1)}, bf16[128,2048]{1,0:T(8,128)(2,1)}, u32[]{:S(2)}) copy-start(bf16[128,2048]{1,0:T(8,128)(2,1)} %refs_3_.1) | copy-start | bytes 1572868
  27.7 3.1 %copy-start.9 = (f32[2048]{0:T(1024)S(1)}, f32[2048]{0:T(1024)}, u32[]{:S(2)}) copy-start(f32[2048]{0:T(1024)} %param.16) | copy-start | bytes 24580
  38.8 13.8 %copy-start.6 = (f32[16,2048]{1,0:T(8,128)S(1)}, f32[16,2048]{1,0:T(8,128)}, u32[]{:S(2)}) copy-start(f32[16,2048]{1,0:T(8,128)} %decay_ref.3) | copy-start | bytes 393220
  38.8 13.8 %copy-start.8 = (f32[3,3,2048]{2,1,0:T(4,128)S(1)}, f32[3,3,2048]{2,1,0:T(4,128)}, u32[]{:S(2)}) copy-start(f32[3,3,2048]{2,1,0:T(4,128)} %filter_ref.3) | copy-start | bytes 221188
  41.6 21.4 %copy-start.2 = (bf16[128,2048]{1,0:T(8,128)(2,1)S(1)}, bf16[128,2048]{1,0:T(8,128)(2,1)}, u32[]{:S(2)}) copy-start(bf16[128,2048]{1,0:T(8,128)(2,1)} %v_ref.1) | copy-start | bytes 1572868
  52.6 10.4 %copy-start.1 = (bf16[128,2048]{1,0:T(8,128)(2,1)S(1)}, bf16[128,2048]{1,0:T(8,128)(2,1)}, u32[]{:S(2)}) copy-start(bf16[128,2048]{1,0:T(8,128)(2,1)} %k_ref.1) | copy-start | bytes 1572868

commit v3 on v1

--- a/solution.py
+++ b/solution.py
@@ -492,8 +492,8 @@
 
 def norm_kernel(
     s, width, sums_ref, conv_ref, q_ref, stream_ref, cot_ref, near_ref, filter_ref, decay_ref, gain_ref,
-    normed_hbm, dstream_hbm, qgrad_hbm, dconv_ref, tail_ref, pay_ref,
-    qs, xs, gs, ns, ds, normed_b, dstream_b, qgrad_b, taps, poles, inv_s, coef_s, sems,
+    normed_hbm, dstream_hbm, qgrad_hbm, dconv_hbm, tail_hbm, pay_ref,
+    qs, xs, gs, ns, ds, dconv_ref, normed_b, dstream_b, qgrad_b, taps, poles, inv_s, coef_s, sems,
 ):
     inverse = lax.rsqrt(sums_ref[0:1, :] / width + epsilon)
     coef = inverse * inverse * inverse * sums_ref[1:2, :] / width
@@ -557,8 +557,13 @@
             copy.start()
 
     each_half(s, half)
-    start = steps * 2 * s.tiles * SUB
-    tail_ref[...] = qs[start : start + 2 * s.tiles * SUB, :]
+    tail = pl.ds(steps * 2 * s.tiles * SUB, 2 * s.tiles * SUB)
+    later = [
+        pltpu.make_async_copy(dconv_ref, dconv_hbm, sems.at[3 * s.halves]),
+        pltpu.make_async_copy(qs.at[tail], tail_hbm, sems.at[3 * s.halves + 1]),
+    ]
+    for copy in later:
+        copy.start()
 
     def ends(h):
         p = mode_tiles(s, poles, h)
@@ -584,14 +589,37 @@
             copy.wait()
 
     each_half(s, finish)
+    for copy in later:
+        copy.wait()
+
+
+def inside_back_kernel(s, dconv_hbm, decay_hbm, residue_hbm, inside_ref, cs, db, rb, poles, weights, sems):
+    pairs = [(decay_hbm, db), (residue_hbm, rb), (dconv_hbm, cs)]
+    copies = [pltpu.make_async_copy(a, b, sems.at[i]) for i, (a, b) in enumerate(pairs)]
+    for copy in copies:
+        copy.start()
+    for copy in copies[:2]:
+        copy.wait()
+    stage_modes(s, db, poles, lambda x: jnp.exp(-x))
+    stage_modes(s, rb, weights, lambda x: x)
+    copies[2].wait()
+    blank = jnp.zeros((SUB, LANES), f32)
+
+    def half(h):
+        p, w = mode_tiles(s, poles, h), mode_tiles(s, weights, h)
+        recur(s, cs, inside_ref, p, w, [blank] * s.modes, h, reverse=True)
+
+    each_half(s, half)
 
 
 def backward_kernel(
-    s, k_ref, v_ref, dconv_ref, tail_ref, near_ref, back_ref, filter_ref, decay_ref, residue_ref, qgrad_in,
+    s, k_ref, v_ref, inside_ref, tail_hbm, near_ref, back_ref, filter_ref, decay_ref, residue_ref, qgrad_in,
     qgrad_hbm, kgrad_hbm, vgrad_hbm,
-    ks, vs, dprod, qs, kgrad_b, vgrad_b, qgrad_b, taps, poles, weights, sems,
+    ks, vs, qs, kgrad_b, vgrad_b, qgrad_b, taps, poles, weights, sems,
 ):
     del qgrad_in
+    tail = pltpu.make_async_copy(tail_hbm, qs, sems.at[2 * s.halves + 1])
+    tail.start()
     stage_modes(s, decay_ref, poles, lambda x: jnp.exp(-x))
     stage_modes(s, residue_ref, weights, lambda x: x)
     stage_taps(s, filter_ref, taps)
@@ -600,7 +628,15 @@
     def back(r, h):
         return back_ref[backward_slice(s, r, h), :]
 
-    qs[...] = tail_ref[...]
+    def pieces(h):
+        cut = columns(h)
+        sources = [(kgrad_b, kgrad_hbm), (vgrad_b, vgrad_hbm)]
+        return [
+            pltpu.make_async_copy(a.at[:, cut], b.at[:, cut], sems.at[2 * h + i])
+            for i, (a, b) in enumerate(sources)
+        ]
+
+    last = pltpu.make_async_copy(qgrad_b, qgrad_hbm.at[pl.ds(s.length - 16, 16), :], sems.at[2 * s.halves])
 
     def tails(h):
         taps_q = tap_tiles(s, taps, 0, h)
@@ -610,23 +646,9 @@
         qs[rows[1], :] = qs[rows[1], :] + (taps_q[1] * dq0 + taps_q[2] * dq1)
         unstage(s, qs, qgrad_b, 0, h)
 
-    each_half(s, tails)
-    last = pltpu.make_async_copy(qgrad_b, qgrad_hbm.at[pl.ds(s.length - 16, 16), :], sems.at[2 * s.halves])
-    last.start()
-
-    def pieces(h):
-        cut = columns(h)
-        sources = [(kgrad_b, kgrad_hbm), (vgrad_b, vgrad_hbm)]
-        return [
-            pltpu.make_async_copy(a.at[:, cut], b.at[:, cut], sems.at[2 * h + i])
-            for i, (a, b) in enumerate(sources)
-        ]
-
     def half(h):
         p = mode_tiles(s, poles, h)
         w = mode_tiles(s, weights, h)
-        arriving = [back(m, h) for m in range(s.modes)]
-        recur(s, dconv_ref, dprod, p, w, arriving, h, reverse=True)
         taps_k, taps_v = (tap_tiles(s, taps, i, h) for i in (1, 2))
 
         def bring(i):
@@ -657,7 +679,7 @@
         inputs, grads, _ = advance(inputs, grads, ks[ends[0], :], vs[ends[0], :], d0)
 
         def step(i, carry):
-            inputs, grads = carry
+            states, inputs, grads = carry
             i = steps - 1 - i
 
             @pl.when(i > 0)
@@ -665,18 +687,26 @@
                 bring(jnp.maximum(i - 1, 0))
 
             for block, offset in sixteen(0, True):
-                d = dprod[major(s, (2 * i + block) * SUB + offset, h), :]
+                states = [p[m] * states[m] for m in range(s.modes)]
+                d = inside_ref[major(s, (2 * i + block) * SUB + offset, h), :] + total(states)
                 rows = staged_before(s, 2 * i + block + 2, offset, h)
                 inputs, grads, out = advance(inputs, grads, ks[rows, :], vs[rows, :], d)
                 rows = staged(s, 2 * i + block + 2, offset, h)
                 ks[rows, :], vs[rows, :] = out
             unstage(s, ks, kgrad_b, i + 1, h, i)
             unstage(s, vs, vgrad_b, i + 1, h, i)
-            return inputs, grads
-
-        lax.fori_loop(0, steps, step, (inputs, grads))
+            return states, inputs, grads
+
+        states = [w[m] * arriving[m] for m in range(s.modes)]
+        lax.fori_loop(0, steps, step, (states, inputs, grads))
         for copy in pieces(h):
             copy.start()
+
+        @pl.when(h == 0)
+        def _():
+            tail.wait()
+            each_half(s, tails)
+            last.start()
 
     each_half(s, half)
     last.wait()
@@ -761,20 +791,26 @@
     )
     sums = lax.psum(sums, "tp")
     normed, dstream, query_grad, dconv, tail, pay_back = call(
-        lambda s, *refs: norm_kernel(s, total_width, *refs), "v" * 9, "hhhvvv",
+        lambda s, *refs: norm_kernel(s, total_width, *refs), "v" * 9, "hhhhhv",
         (narrow, narrow, narrow, wide, jax.ShapeDtypeStruct((rows, LANES), f32), jax.ShapeDtypeStruct(s.exchange_shape(modes, BACKWARD_EXTRA), f32)),
-        [pltpu.VMEM(((length + 32) * s.tiles, LANES), f32)] + [longer_s] * 2 + [wide_s] * 2 + [narrow_s] * 2
+        [pltpu.VMEM(((length + 32) * s.tiles, LANES), f32)] + [longer_s] * 2 + [wide_s] * 3 + [narrow_s] * 2
         + [pltpu.VMEM((length + 16, channels), bf16)]
-        + [taps_s, mode_s, square_s, square_s, pltpu.SemaphoreType.DMA((3 * s.halves,))],
+        + [taps_s, mode_s, square_s, square_s, pltpu.SemaphoreType.DMA((3 * s.halves + 2,))],
         (sums, conv, query_in, stream, cotangent, near, short_filter, decay_rate, gain),
+    )
+    (inside_back,) = call(
+        inside_back_kernel, "hhh", "v", (wide,),
+        [wide_s, rates_s, rates_s, mode_s, mode_s, pltpu.SemaphoreType.DMA((3,))],
+        far(dconv, decay_rate, residue),
+        cost=cost(64, 3),
     )
     back_back = exchange(s, pay_back, decay_rate, short_filter, False)
     query_grad, key_grad, value_grad = call(
-        backward_kernel, "v" * 9 + "h", "hhh",
+        backward_kernel, "vvvhvvvvvh", "hhh",
         (narrow, narrow, narrow),
-        [longer_s] * 2 + [wide_s, tail_s] + [narrow_s] * 2 + [last_s, taps_s, mode_s, mode_s]
-        + [pltpu.SemaphoreType.DMA((1 + 2 * s.halves,))],
-        (key_in, value_in, dconv, tail, near, back_back, short_filter, decay_rate, residue, query_grad),
+        [longer_s] * 2 + [tail_s] + [narrow_s] * 2 + [last_s, taps_s, mode_s, mode_s]
+        + [pltpu.SemaphoreType.DMA((2 + 2 * s.halves,))],
+        (key_in, value_in, inside_back, tail, near, back_back, short_filter, decay_rate, residue, query_grad),
         {9: 0},
     )
     return (normed, dstream, query_grad, key_grad, value_grad)

time: 67.6 us -> 69.3 us (1.025)
  blocking collectives: 41.3 us -> 30.9 us
  Pallas kernels: 18.4 us -> 22.4 us
  waiting for transfers between devices: 3.02 us -> 6.75 us
  starting transfers between devices: 3.52 us -> 6.9 us
  local copies, waits for them, and re-layouts: 0.06 us -> 1.05 us
    all_to_all x1 -> x0, blocking collectives: 10.4 us -> none  [exchange(): lax.all_to_all(back.reshape(chunks), 'seq', 0, 0, tiled=True)]
    all_to_all x1 -> x2, waiting for transfers between devices: 3.02 us -> 6.75 us  [exchange(): lax.all_to_all(back.reshape(chunks), 'seq', 0, 0, tiled=True)]
    all_to_all x1 -> x2, starting transfers between devices: 3.52 us -> 6.9 us  [exchange(): lax.all_to_all(back.reshape(chunks), 'seq', 0, 0, tiled=True)]
    pallas_call x5 -> x6, Pallas kernels: 17.6 us -> 20.9 us  [call(): pl.pallas_call(functools.partial(kernel, s), in_specs=[there if c == 'h'...]
    unnamed x22 -> x28, local copies, waits for them, and re-layouts: 0.06 us -> 1.05 us
  transfers between devices with their start and end apart: 1 -> 2, of which waited for: 1 -> 2; matrix products, arithmetic and copies ran while one was open for 0% -> 0% of each run, Pallas kernels for 7% -> 12%
where the time goes in v3:
time: 69.3 us; the launch traced here: 68.8 us
  blocking collectives  30.9 us (45%)
  Pallas kernels  22.4 us (32%)
  starting transfers between devices  6.9 us (10%)
  waiting for transfers between devices  6.75 us (10%)
  local copies, waits for them, and re-layouts  1.05 us (2%)
  between operations  0.83 us (1%)
    all_to_all x2, blocking collectives, exchange(): got = lax.all_to_all(pay.reshape(chunks), 'seq', 0, 0, tiled=True)  25.2 us
    pallas_call x6, Pallas kernels, call(): pl.pallas_call(functools.partial(kernel, s), in_specs=[there if c == 'h'...  20.9 us
    all_to_all x2, starting transfers between devices, exchange(): lax.all_to_all(back.reshape(chunks), 'seq', 0, 0, tiled=True)  6.9 us
    all_to_all x2, waiting for transfers between devices, exchange(): lax.all_to_all(back.reshape(chunks), 'seq', 0, 0, tiled=True)  6.75 us
    psum x1, blocking collectives, body(): sums = lax.psum(sums, 'tp')  5.67 us
    pallas_call x2, Pallas kernels, exchange(): pl.pallas_call(functools.partial(middle_kernel, s, forward), out_shape=ja...  1.51 us
  transfers between devices with their start and end apart: 2, of which 2 were waited for; matrix products, arithmetic and copies ran while one was open for 0% of the time, Pallas kernels for 12%

profile of v3, /device:TPU:0, one launch (start us, length us, event | category | flops | bytes accessed | tf_op | source)
XLA Modules:
  0.0 68.8 jit_solution(3062109533368653832)
XLA Ops:
  0.6 3.3 %shard_map.129 = bf16[704,128]{1,0:T(8,128)(2,1)S(1)} custom-call(bf16[128,2048]{1,0:T(8,128)(2,1)} %refs_2_.1, bf16[128,2048]{1,0:T(8,128)(2,1)} %k_ref.1, bf16[128,2048]{1,0:T(8,128)(2,1)} %v_ref.1, f32[3,3,2048]{2,1,0:T(4,128)} %filter_ref.7, f32[16,2048]{1,0:T(8,128)} %decay_ref.7), custom_call_target="tpu_custom_call" | custom-call | tf_op jit(solution)/shard_map/pallas_call | solution.py:745
  3.9 0.0 copy-start
  3.9 0.0 copy-start.3
  3.9 14.9 %all_to_all.20 = bf16[8,88,128]{2,1,0:T(8,128)(2,1)S(1)} all-to-all(bf16[8,88,128]{2,1,0:T(8,128)(2,1)S(1)} %bitcast.11), channel_id=1, replica_groups=mesh['seq'=8,'tp'=4] {'seq'}, dimensions={0} | all-to-all | bytes 360448 | tf_op jit(solution)/shard_map/all_to_all | solution.py:337
  18.9 0.0 copy-done
  18.9 0.0 copy-done.3
  18.9 0.0 copy-start.9
  18.9 0.8 %shard_map.130 = bf16[704,128]{1,0:T(8,128)(2,1)} custom-call(bf16[704,128]{1,0:T(8,128)(2,1)S(1)} %bitcast.10, f32[16,2048]{1,0:T(8,128)S(1)} %copy-done, f32[3,3,2048]{2,1,0:T(4,128)S(1)} %copy-done.3), custom_call_target="tpu_custom_call" | custom-call | tf_op jit(solution)/shard_map/pallas_call | solution.py:338
  19.7 0.0 copy-start.13
  19.7 3.5 %all-to-all-start.1 = ((bf16[8,88,128]{2,1,0:T(8,128)(2,1)}), bf16[8,88,128]{2,1,0:T(8,128)(2,1)S(1)}, u32[]{:S(2)}, u32[]{:S(2)}) async-start(bf16[8,88,128]{2,1,0:T(8,128)(2,1)} %bitcast.2), calls=%async_computation.1 | async-start | bytes 360448 | tf_op jit(solution)/shard_map/all_to_all | solution.py:344
  23.2 0.0 copy-start.1
  23.2 0.0 copy-start.4
  23.2 0.0 copy-start.5
  23.2 0.0 copy-start.8
  23.3 0.0 copy-start.10
  23.3 4.5 %shard_map.128 = (f32[2048,128]{1,0:T(8,128)S(1)}, f32[64,128]{1,0:T(8,128)S(1)}) custom-call(bf16[128,2048]{1,0:T(8,128)(2,1)} %k_ref.1, bf16[128,2048]{1,0:T(8,128)(2,1)} %v_ref.1, f32[3,3,2048]{2,1,0:T(4,128)} %filter_ref.7, f32[16,2048]{1,0:T(8,128)} %decay_ref.7, f32[16,2048]{1,0:T(8,128)} %residue_ref.3), custom_call_target="tpu_custom_call" | custom-call | flops 19660800 | bytes 3145728 | tf_op jit(solution)/shard_map/pallas_call | solution.py:745
  27.8 3.0 %all-to-all-done.1 = bf16[8,88,128]{2,1,0:T(8,128)(2,1)S(1)} async-done(((bf16[8,88,128]{2,1,0:T(8,128)(2,1)}), bf16[8,88,128]{2,1,0:T(8,128)(2,1)S(1)}, u32[]{:S(2)}, u32[]{:S(2)}) %all-to-all-start.1) | async-done | bytes 180256 | tf_op jit(solution)/shard_map/all_to_all | solution.py:344
  30.8 0.0 copy-done.9
  30.8 0.0 copy-done.13
  30.8 0.0 copy-done.1
  30.8 0.0 copy-done.4
  30.8 0.0 copy-done.5
  30.8 0.0 copy-done.8
  30.9 0.0 copy-done.10
  30.9 2.4 %shard_map.131 = (f32[2048,128]{1,0:T(8,128)S(1)}, f32[2,128]{1,0:T(2,128)S(1)}, f32[160,128]{1,0:T(8,128)S(1)}) custom-call(f32[2048,128]{1,0:T(8,128)S(1)} %get-tuple-element.19.inside_ref, f32[64,128]{1,0:T(8,128)S(1)} %get-tuple-element.20.first_ref, bf16[128,2048]{1,0:T(8,128)(2,1)S(1)} %copy-done.5, ...), custom_call_target="tpu_custom_call", output_to_operand_aliasing={{0}: (0, {})} | custom-call | tf_op jit(solution)/shard_map/pallas_call | solution.py:745
  33.2 5.7 %psum.7.refs_0_ = f32[2,128]{1,0:T(2,128)S(1)} all-reduce(f32[2,128]{1,0:T(2,128)S(1)} %get-tuple-element.21), channel_id=1, replica_groups=mesh['seq'=8,'tp'=4] {'tp'}, use_global_device_ids=true, to_apply=%region_0.0 | all-reduce | flops 256 | bytes 2048 | tf_op jit(solution)/shard_map/psum | solution.py:792
  38.9 3.1 %shard_map.132 = (bf16[128,2048]{1,0:T(8,128)(2,1)}, bf16[128,2048]{1,0:T(8,128)(2,1)}, bf16[128,2048]{1,0:T(8,128)(2,1)}, f32[2048,128]{1,0:T(8,128)S(1)}, f32[...) custom-call(f32[2,128]{1,0:T(2,128)S(1)} %psum.7.refs_0_, f32[2048,128]{1,0:T(8,128)S(1)} %get-tuple-element.22.refs_1_, ...), custom_call_target="tpu_custom_call" | custom-call | tf_op jit(solution)/shard_map/pallas_call | solution.py:745
  42.0 0.0 copy-start.12
  42.0 1.0 %copy-done.12 = f32[2048,128]{1,0:T(8,128)} copy-done((f32[2048,128]{1,0:T(8,128)}, f32[2048,128]{1,0:T(8,128)S(1)}, u32[]{:S(2)}) %copy-start.12) | copy-done | bytes 1048600
  43.0 10.3 %all_to_all.21 = f32[8,40,128]{2,1,0:T(8,128)S(1)} all-to-all(f32[8,40,128]{2,1,0:T(8,128)S(1)} %bitcast.14), channel_id=1, replica_groups=mesh['seq'=8,'tp'=4] {'seq'}, dimensions={0} | all-to-all | bytes 327680 | tf_op jit(solution)/shard_map/all_to_all | solution.py:337
  53.2 0.7 %shard_map.134 = f32[320,128]{1,0:T(8,128)} custom-call(f32[320,128]{1,0:T(8,128)S(1)} %bitcast.13, f32[16,2048]{1,0:T(8,128)S(1)} %copy-done.1, f32[3,3,2048]{2,1,0:T(4,128)S(1)} %copy-done.4), custom_call_target="tpu_custom_call" | custom-call | tf_op jit(solution)/shard_map/pallas_call | solution.py:338
  53.9 3.4 %all-to-all-start.3 = ((f32[8,40,128]{2,1,0:T(8,128)}), f32[8,40,128]{2,1,0:T(8,128)S(1)}, u32[]{:S(2)}, u32[]{:S(2)}) async-start(f32[8,40,128]{2,1,0:T(8,128)} %bitcast.7), calls=%async_computation.3 | async-start | bytes 327680 | tf_op jit(solution)/shard_map/all_to_all | solution.py:344
  57.3 0.0 copy-start.2
  57.3 0.0 copy-start.6
  57.3 0.0 copy-start.7
  57.4 0.0 copy-start.11
  57.4 3.7 %shard_map.133.inside_ref = f32[2048,128]{1,0:T(8,128)S(1)} custom-call(f32[2048,128]{1,0:T(8,128)} %copy-done.12, f32[16,2048]{1,0:T(8,128)} %decay_ref.7, f32[16,2048]{1,0:T(8,128)} %residue_ref.3), custom_call_target="tpu_custom_call" | custom-call | flops 16777216 | bytes 3145728 | tf_op jit(solution)/shard_map/pallas_call | solution.py:745
  61.1 3.7 %all-to-all-done.3 = f32[8,40,128]{2,1,0:T(8,128)S(1)} async-done(((f32[8,40,128]{2,1,0:T(8,128)}), f32[8,40,128]{2,1,0:T(8,128)S(1)}, u32[]{:S(2)}, u32[]{:S(2)}) %all-to-all-start.3) | async-done | bytes 163872 | tf_op jit(solution)/shard_map/all_to_all | solution.py:344
  64.8 0.0 copy-done.2
  64.8 0.0 copy-done.6
  64.8 0.0 copy-done.7
  64.8 0.0 copy-done.11
  64.8 4.0 %shard_map.135 = (bf16[128,2048]{1,0:T(8,128)(2,1)}, bf16[128,2048]{1,0:T(8,128)(2,1)}, bf16[128,2048]{1,0:T(8,128)(2,1)}) custom-call(bf16[128,2048]{1,0:T(8,128)(2,1)S(1)} %copy-done.6, bf16[128,2048]{1,0:T(8,128)(2,1)S(1)} %copy-done.7, f32[2048,128]{1,0:T(8,128)S(1)} %shard_map.133.inside_ref, ...), custom_call_target="tpu_custom_call", output_to_operand_aliasing={{0}: (9, {})} | custom-call | tf_op jit(solution)/shard_map/pallas_call | solution.py:745
Async XLA Ops:
  3.9 14.9 %copy-start = (f32[16,2048]{1,0:T(8,128)S(1)}, f32[16,2048]{1,0:T(8,128)}, u32[]{:S(2)}) copy-start(f32[16,2048]{1,0:T(8,128)} %decay_ref.7) | copy-start | bytes 393220
  3.9 14.9 %copy-start.3 = (f32[3,3,2048]{2,1,0:T(4,128)S(1)}, f32[3,3,2048]{2,1,0:T(4,128)}, u32[]{:S(2)}) copy-start(f32[3,3,2048]{2,1,0:T(4,128)} %filter_ref.7) | copy-start | bytes 221188
  18.9 12.0 %copy-start.9 = (bf16[128,2048]{1,0:T(8,128)(2,1)S(1)}, bf16[128,2048]{1,0:T(8,128)(2,1)}, u32[]{:S(2)}) copy-start(bf16[128,2048]{1,0:T(8,128)(2,1)} %refs_4_.1) | copy-start | bytes 1572868
  19.7 11.1 %copy-start.13 = (f32[2048]{0:T(1024)S(1)}, f32[2048]{0:T(1024)}, u32[]{:S(2)}) copy-start(f32[2048]{0:T(1024)} %param.16) | copy-start | bytes 24580
  19.7 11.1 %all-to-all-start.1 = ((bf16[8,88,128]{2,1,0:T(8,128)(2,1)}), bf16[8,88,128]{2,1,0:T(8,128)(2,1)S(1)}, u32[]{:S(2)}, u32[]{:S(2)}) async-start(bf16[8,88,128]{2,1,0:T(8,128)(2,1)} %bitcast.2), calls=%async_computation.1 | async-start | bytes 360448 | tf_op jit(solution)/shard_map/all_to_all | solution.py:344
  23.2 7.6 %copy-start.1 = (f32[16,2048]{1,0:T(8,128)S(1)}, f32[16,2048]{1,0:T(8,128)}, u32[]{:S(2)}) copy-start(f32[16,2048]{1,0:T(8,128)} %decay_ref.7) | copy-start | bytes 393220
  23.2 7.6 %copy-start.4 = (f32[3,3,2048]{2,1,0:T(4,128)S(1)}, f32[3,3,2048]{2,1,0:T(4,128)}, u32[]{:S(2)}) copy-start(f32[3,3,2048]{2,1,0:T(4,128)} %filter_ref.7) | copy-start | bytes 221188
  23.2 7.6 %copy-start.5 = (bf16[128,2048]{1,0:T(8,128)(2,1)S(1)}, bf16[128,2048]{1,0:T(8,128)(2,1)}, u32[]{:S(2)}) copy-start(bf16[128,2048]{1,0:T(8,128)(2,1)} %refs_2_.1) | copy-start | bytes 1572868
  23.2 7.6 %copy-start.8 = (bf16[128,2048]{1,0:T(8,128)(2,1)S(1)}, bf16[128,2048]{1,0:T(8,128)(2,1)}, u32[]{:S(2)}) copy-start(bf16[128,2048]{1,0:T(8,128)(2,1)} %refs_3_.1) | copy-start | bytes 1572868
  23.3 7.6 %copy-start.10 = (f32[16,2048]{1,0:T(8,128)S(1)}, f32[16,2048]{1,0:T(8,128)}, u32[]{:S(2)}) copy-start(f32[16,2048]{1,0:T(8,128)} %residue_ref.3) | copy-start | bytes 393220
  42.0 1.0 %copy-start.12 = (f32[2048,128]{1,0:T(8,128)}, f32[2048,128]{1,0:T(8,128)S(1)}, u32[]{:S(2)}) copy-start(f32[2048,128]{1,0:T(8,128)S(1)} %get-tuple-element.26.dconv_hbm) | copy-start | bytes 3145732
  53.9 10.9 %all-to-all-start.3 = ((f32[8,40,128]{2,1,0:T(8,128)}), f32[8,40,128]{2,1,0:T(8,128)S(1)}, u32[]{:S(2)}, u32[]{:S(2)}) async-start(f32[8,40,128]{2,1,0:T(8,128)} %bitcast.7), calls=%async_computation.3 | async-start | bytes 327680 | tf_op jit(solution)/shard_map/all_to_all | solution.py:344
  57.3 7.5 %copy-start.2 = (f32[16,2048]{1,0:T(8,128)S(1)}, f32[16,2048]{1,0:T(8,128)}, u32[]{:S(2)}) copy-start(f32[16,2048]{1,0:T(8,128)} %decay_ref.7) | copy-start | bytes 393220
  57.3 7.5 %copy-start.6 = (bf16[128,2048]{1,0:T(8,128)(2,1)S(1)}, bf16[128,2048]{1,0:T(8,128)(2,1)}, u32[]{:S(2)}) copy-start(bf16[128,2048]{1,0:T(8,128)(2,1)} %k_ref.1) | copy-start | bytes 1572868
  57.3 7.5 %copy-start.7 = (bf16[128,2048]{1,0:T(8,128)(2,1)S(1)}, bf16[128,2048]{1,0:T(8,128)(2,1)}, u32[]{:S(2)}) copy-start(bf16[128,2048]{1,0:T(8,128)(2,1)} %v_ref.1) | copy-start | bytes 1572868
  57.4 7.5 %copy-start.11 = (f32[16,2048]{1,0:T(8,128)S(1)}, f32[16,2048]{1,0:T(8,128)}, u32[]{:S(2)}) copy-start(f32[16,2048]{1,0:T(8,128)} %residue_ref.3) | copy-start | bytes 393220

commit v4 on v2

--- a/solution.py
+++ b/solution.py
@@ -225,8 +225,8 @@
         cut = pl.ds(h * GROUP, GROUP)
         copies += [(k_hbm.at[:, cut], kb.at[:, cut]), (v_hbm.at[:, cut], vb.at[:, cut])]
     copies = [pltpu.make_async_copy(a, b, sems.at[i]) for i, (a, b) in enumerate(copies)]
-    for copy in copies:
-        copy.start()
+    for i, copy in enumerate(copies):
+        copy.start(priority=i % 2)
     copies[0].wait()
     stage_modes(s, db, poles, lambda x: jnp.exp(-x))
     copies[1].wait()
@@ -374,19 +374,20 @@
 
 
 def inside_kernel(
-    s, k_hbm, v_hbm, filter_hbm, decay_hbm, residue_hbm, inside_ref, first_ref, taps, poles, weights,
-    kb, vb, fb, db, rb, ks, vs, prod, sems,
+    s, k_hbm, v_hbm, filter_hbm, decay_hbm, residue_hbm, inside_ref, first_ref,
+    kb, vb, fb, db, rb, ks, vs, prod, taps, poles, weights, sems,
 ):
     pairs = [(decay_hbm, db), (residue_hbm, rb), (filter_hbm, fb), (k_hbm, kb), (v_hbm, vb)]
     copies = [pltpu.make_async_copy(a, b, sems.at[i]) for i, (a, b) in enumerate(pairs)]
-    for copy in copies:
-        copy.start()
+    for i, copy in enumerate(copies):
+        copy.start(priority=i % 2)
     for copy in copies:
         copy.wait()
     stage_modes(s, db, poles, lambda x: jnp.exp(-x))
     stage_modes(s, rb, weights, lambda x: x)
     stage_taps(s, fb, taps)
     blank = jnp.zeros((SUB, LANES), f32)
+    steps = s.length // 16
 
     def half(h):
         taps_k, taps_v = (tap_tiles(s, taps, i, h) for i in (1, 2))
@@ -402,10 +403,14 @@
 
 
 def forward_kernel(
-    s, inside_ref, first_ref, q_ref, stream_ref, cot_ref, back_ref, taps, poles, weights, gain_ref,
+    s, inside_ref, first_ref, q_ref, stream_ref, cot_ref, back_ref, filter_ref, decay_ref, residue_ref, gain_ref,
     conv_ref, sums_ref, near_ref,
-    qs, xs, gs, back_s, squares, inners,
+    qs, xs, gs, back_s, taps, poles, weights, squares, inners,
 ):
+    stage_modes(s, decay_ref, poles, lambda x: jnp.exp(-x))
+    stage_modes(s, residue_ref, weights, lambda x: x)
+    stage_taps(s, filter_ref, taps)
+
     widened(back_ref, back_s)
     steps = s.length // 16
 
@@ -479,14 +484,16 @@
 
 
 def norm_kernel(
-    s, width, sums_ref, conv_ref, q_ref, stream_ref, cot_ref, near_ref, taps, poles, gain_ref,
+    s, width, sums_ref, conv_ref, q_ref, stream_ref, cot_ref, near_ref, filter_ref, decay_ref, gain_ref,
     normed_hbm, dstream_hbm, qgrad_hbm, dconv_ref, tail_ref, pay_ref,
-    qs, xs, gs, ns, ds, normed_b, dstream_b, qgrad_b, inv_s, coef_s, sems,
+    qs, xs, gs, ns, ds, normed_b, dstream_b, qgrad_b, taps, poles, inv_s, coef_s, sems,
 ):
     inverse = lax.rsqrt(sums_ref[0:1, :] / width + epsilon)
     coef = inverse * inverse * inverse * sums_ref[1:2, :] / width
     inv_s[...] = jnp.broadcast_to(inverse, (LANES, s.length)).T
     coef_s[...] = jnp.broadcast_to(coef, (LANES, s.length)).T
+    stage_modes(s, decay_ref, poles, lambda x: jnp.exp(-x))
+    stage_taps(s, filter_ref, taps)
     blank = jnp.zeros((SUB, LANES), f32)
     steps = s.length // 16
 
@@ -539,8 +546,8 @@
         _, _, dq1, dq2 = lax.fori_loop(0, steps, step, held)
         qs[staged(s, 2 * steps + 1, 6, h), :] = taps_q[0] * dq2 + taps_q[1] * dq1
         qs[staged(s, 2 * steps + 1, 7, h), :] = taps_q[0] * dq1
-        for copy in pieces(h):
-            copy.start()
+        for i, copy in enumerate(pieces(h)):
+            copy.start(priority=i % 2)
 
     each_half(s, half)
     start = steps * 2 * s.tiles * SUB
@@ -573,11 +580,14 @@
 
 
 def backward_kernel(
-    s, k_ref, v_ref, dconv_ref, tail_ref, near_ref, back_ref, taps, poles, weights, qgrad_in,
+    s, k_ref, v_ref, dconv_ref, tail_ref, near_ref, back_ref, filter_ref, decay_ref, residue_ref, qgrad_in,
     qgrad_hbm, kgrad_hbm, vgrad_hbm,
-    ks, vs, dprod, qs, kgrad_b, vgrad_b, qgrad_b, sems,
+    ks, vs, dprod, qs, kgrad_b, vgrad_b, qgrad_b, taps, poles, weights, sems,
 ):
     del qgrad_in
+    stage_modes(s, decay_ref, poles, lambda x: jnp.exp(-x))
+    stage_modes(s, residue_ref, weights, lambda x: x)
+    stage_taps(s, filter_ref, taps)
     steps = s.length // 16
 
     def back(r, h):
@@ -658,8 +668,8 @@
             return inputs, grads
 
         lax.fori_loop(0, steps, step, (inputs, grads))
-        for copy in pieces(h):
-            copy.start()
+        for i, copy in enumerate(pieces(h)):
+            copy.start(priority=i % 2)
 
     each_half(s, half)
     last.wait()
@@ -727,11 +737,10 @@
         + [pltpu.SemaphoreType.DMA((3 + 2 * s.halves,))],
         far(query_in, key_in, value_in, short_filter, decay_rate),
     )
-    inside, first, taps, poles, weights = call(
-        inside_kernel, "hhhhh", "vvvvv",
-        (wide, *(jax.ShapeDtypeStruct(x, f32) for x in ((4 * s.tiles, LANES), taps_s.shape, mode_s.shape, mode_s.shape))),
+    inside, first = call(
+        inside_kernel, "hhhhh", "vv", (wide, jax.ShapeDtypeStruct((4 * s.tiles, LANES), f32)),
         [narrow_s, narrow_s, filter_s, rates_s, rates_s]
-        + [wide_s] * 3 + [pltpu.SemaphoreType.DMA((5,))],
+        + [wide_s] * 3 + [taps_s, mode_s, mode_s, pltpu.SemaphoreType.DMA((5,))],
         far(key_in, value_in, short_filter, decay_rate, residue),
         cost=cost(75, 3),
     )
@@ -739,8 +748,8 @@
     conv, sums, near = call(
         forward_kernel, "v" * 10, "vvv",
         (wide, jax.ShapeDtypeStruct((2, length), f32), near_shape),
-        [wide_s] * 3 + [pltpu.VMEM(forward_shape, f32), sum_s, sum_s],
-        (inside, first, query_in, stream, cotangent, back, taps, poles, weights, gain),
+        [wide_s] * 3 + [pltpu.VMEM(forward_shape, f32), taps_s, mode_s, mode_s, sum_s, sum_s],
+        (inside, first, query_in, stream, cotangent, back, short_filter, decay_rate, residue, gain),
         {0: 0},
     )
     sums = lax.psum(sums, "tp")
@@ -749,16 +758,16 @@
         (narrow, narrow, narrow, wide, jax.ShapeDtypeStruct((rows, LANES), f32), jax.ShapeDtypeStruct(s.exchange_shape(modes, BACKWARD_EXTRA), f32)),
         [pltpu.VMEM(((length + 32) * s.tiles, LANES), f32)] + [longer_s] * 2 + [wide_s] * 2 + [narrow_s] * 2
         + [pltpu.VMEM((length + 16, channels), bf16)]
-        + [square_s, square_s, pltpu.SemaphoreType.DMA((3 * s.halves,))],
-        (sums, conv, query_in, stream, cotangent, near, taps, poles, gain),
+        + [taps_s, mode_s, square_s, square_s, pltpu.SemaphoreType.DMA((3 * s.halves,))],
+        (sums, conv, query_in, stream, cotangent, near, short_filter, decay_rate, gain),
     )
     back_back = exchange(s, pay_back, decay_rate, short_filter, False)
     query_grad, key_grad, value_grad = call(
         backward_kernel, "v" * 9 + "h", "hhh",
         (narrow, narrow, narrow),
-        [longer_s] * 2 + [wide_s, tail_s] + [narrow_s] * 2 + [last_s]
+        [longer_s] * 2 + [wide_s, tail_s] + [narrow_s] * 2 + [last_s, taps_s, mode_s, mode_s]
         + [pltpu.SemaphoreType.DMA((1 + 2 * s.halves,))],
-        (key_in, value_in, dconv, tail, near, back_back, taps, poles, weights, query_grad),
+        (key_in, value_in, dconv, tail, near, back_back, short_filter, decay_rate, residue, query_grad),
         {9: 0},
     )
     return (normed, dstream, query_grad, key_grad, value_grad)

time: 68 us -> 67.6 us (level)
  no operation moved by 1% of the time
where the time goes in v4:
time: 67.6 us; the launch traced here: 67.2 us
  blocking collectives  41.4 us (61%)
  Pallas kernels  18.4 us (27%)
  starting transfers between devices  3.52 us (5%)
  waiting for transfers between devices  3.02 us (4%)
  between operations  0.78 us (1%)
    all_to_all x2, blocking collectives, exchange(): got = lax.all_to_all(pay.reshape(chunks), 'seq', 0, 0, tiled=True)  25.3 us
    pallas_call x5, Pallas kernels, call(): pl.pallas_call(functools.partial(kernel, s), in_specs=[there if c == 'h'...  17.6 us
    all_to_all x1, blocking collectives, exchange(): lax.all_to_all(back.reshape(chunks), 'seq', 0, 0, tiled=True)  10.4 us
    psum x1, blocking collectives, body(): sums = lax.psum(sums, 'tp')  5.67 us
    all_to_all x1, starting transfers between devices, exchange(): lax.all_to_all(back.reshape(chunks), 'seq', 0, 0, tiled=True)  3.52 us
    all_to_all x1, waiting for transfers between devices, exchange(): lax.all_to_all(back.reshape(chunks), 'seq', 0, 0, tiled=True)  3.02 us
  transfers between devices with their start and end apart: 1, of which 1 were waited for; matrix products, arithmetic and copies ran while one was open for 0% of the time, Pallas kernels for 7%

profile of v4, /device:TPU:0, one launch (start us, length us, event | category | flops | bytes accessed | tf_op | source)
XLA Modules:
  0.0 67.2 jit_solution(7229097791770899023)
XLA Ops:
  0.6 3.3 %shard_map.129 = bf16[704,128]{1,0:T(8,128)(2,1)S(1)} custom-call(bf16[128,2048]{1,0:T(8,128)(2,1)} %refs_2_.1, bf16[128,2048]{1,0:T(8,128)(2,1)} %k_ref.1, bf16[128,2048]{1,0:T(8,128)(2,1)} %v_ref.1, f32[3,3,2048]{2,1,0:T(4,128)} %filter_ref.7, f32[16,2048]{1,0:T(8,128)} %decay_ref.7), custom_call_target="tpu_custom_call" | custom-call | tf_op jit(solution)/shard_map/pallas_call | solution.py:708
  3.9 0.0 copy-start
  4.0 0.0 copy-start.2
  4.0 14.9 %all_to_all.20 = bf16[8,88,128]{2,1,0:T(8,128)(2,1)S(1)} all-to-all(bf16[8,88,128]{2,1,0:T(8,128)(2,1)S(1)} %bitcast.11), channel_id=1, replica_groups=mesh['seq'=8,'tp'=4] {'seq'}, dimensions={0} | all-to-all | bytes 360448 | tf_op jit(solution)/shard_map/all_to_all | solution.py:344
  18.9 0.0 copy-done
  18.9 0.0 copy-done.2
  18.9 0.0 copy-start.8
  18.9 0.8 %shard_map.130 = bf16[704,128]{1,0:T(8,128)(2,1)} custom-call(bf16[704,128]{1,0:T(8,128)(2,1)S(1)} %bitcast.10, f32[16,2048]{1,0:T(8,128)S(1)} %copy-done, f32[3,3,2048]{2,1,0:T(4,128)S(1)} %copy-done.2), custom_call_target="tpu_custom_call" | custom-call | tf_op jit(solution)/shard_map/pallas_call | solution.py:345
  19.7 0.0 copy-start.10
  19.7 3.5 %all-to-all-start.1 = ((bf16[8,88,128]{2,1,0:T(8,128)(2,1)}), bf16[8,88,128]{2,1,0:T(8,128)(2,1)S(1)}, u32[]{:S(2)}, u32[]{:S(2)}) async-start(bf16[8,88,128]{2,1,0:T(8,128)(2,1)} %bitcast.2), calls=%async_computation.1 | async-start | bytes 360448 | tf_op jit(solution)/shard_map/all_to_all | solution.py:351
  23.2 0.0 copy-start.1
  23.2 0.0 copy-start.3
  23.3 0.0 copy-start.4
  23.3 0.0 copy-start.7
  23.3 0.0 copy-start.9
  23.3 4.5 %shard_map.128 = (f32[2048,128]{1,0:T(8,128)S(1)}, f32[64,128]{1,0:T(8,128)S(1)}) custom-call(bf16[128,2048]{1,0:T(8,128)(2,1)} %k_ref.1, bf16[128,2048]{1,0:T(8,128)(2,1)} %v_ref.1, f32[3,3,2048]{2,1,0:T(4,128)} %filter_ref.7, f32[16,2048]{1,0:T(8,128)} %decay_ref.7, f32[16,2048]{1,0:T(8,128)} %residue_ref.3), custom_call_target="tpu_custom_call" | custom-call | flops 19660800 | bytes 3145728 | tf_op jit(solution)/shard_map/pallas_call | solution.py:708
  27.8 3.0 %all-to-all-done.1 = bf16[8,88,128]{2,1,0:T(8,128)(2,1)S(1)} async-done(((bf16[8,88,128]{2,1,0:T(8,128)(2,1)}), bf16[8,88,128]{2,1,0:T(8,128)(2,1)S(1)}, u32[]{:S(2)}, u32[]{:S(2)}) %all-to-all-start.1) | async-done | bytes 180256 | tf_op jit(solution)/shard_map/all_to_all | solution.py:351
  30.8 0.0 copy-done.8
  30.8 0.0 copy-done.10
  30.8 0.0 copy-done.1
  30.9 0.0 copy-done.3
  30.9 0.0 copy-done.4
  30.9 0.0 copy-done.7
  30.9 0.0 copy-done.9
  30.9 2.4 %shard_map.131 = (f32[2048,128]{1,0:T(8,128)S(1)}, f32[2,128]{1,0:T(2,128)S(1)}, f32[160,128]{1,0:T(8,128)S(1)}) custom-call(f32[2048,128]{1,0:T(8,128)S(1)} %get-tuple-element.19.inside_ref, f32[64,128]{1,0:T(8,128)S(1)} %get-tuple-element.20.first_ref, bf16[128,2048]{1,0:T(8,128)(2,1)S(1)} %copy-done.4, ...), custom_call_target="tpu_custom_call", output_to_operand_aliasing={{0}: (0, {})} | custom-call | tf_op jit(solution)/shard_map/pallas_call | solution.py:708
  33.3 5.7 %psum.7.refs_0_ = f32[2,128]{1,0:T(2,128)S(1)} all-reduce(f32[2,128]{1,0:T(2,128)S(1)} %get-tuple-element.21), channel_id=1, replica_groups=mesh['seq'=8,'tp'=4] {'tp'}, use_global_device_ids=true, to_apply=%region_0.0 | all-reduce | flops 256 | bytes 2048 | tf_op jit(solution)/shard_map/psum | solution.py:755
  38.9 2.8 %shard_map.132 = (bf16[128,2048]{1,0:T(8,128)(2,1)}, bf16[128,2048]{1,0:T(8,128)(2,1)}, bf16[128,2048]{1,0:T(8,128)(2,1)}, f32[2048,128]{1,0:T(8,128)S(1)}, f32[...) custom-call(f32[2,128]{1,0:T(2,128)S(1)} %psum.7.refs_0_, f32[2048,128]{1,0:T(8,128)S(1)} %get-tuple-element.22.refs_1_, ...), custom_call_target="tpu_custom_call" | custom-call | tf_op jit(solution)/shard_map/pallas_call | solution.py:708
  41.8 0.0 copy-start.6
  41.8 10.4 %all_to_all.21 = f32[8,40,128]{2,1,0:T(8,128)S(1)} all-to-all(f32[8,40,128]{2,1,0:T(8,128)S(1)} %bitcast.15), channel_id=1, replica_groups=mesh['seq'=8,'tp'=4] {'seq'}, dimensions={0} | all-to-all | bytes 327680 | tf_op jit(solution)/shard_map/all_to_all | solution.py:344
  52.2 0.0 copy-start.5
  52.2 10.4 %all_to_all.22 = f32[8,40,128]{2,1,0:T(8,128)S(1)} all-to-all(f32[8,40,128]{2,1,0:T(8,128)S(1)} %bitcast.14), channel_id=1, replica_groups=mesh['seq'=8,'tp'=4] {'seq'}, dimensions={0} | all-to-all | bytes 327680 | tf_op jit(solution)/shard_map/all_to_all | solution.py:351
  62.6 0.0 copy-done.6
  62.6 0.0 copy-done.5
  62.6 4.6 %shard_map.134 = (bf16[128,2048]{1,0:T(8,128)(2,1)}, bf16[128,2048]{1,0:T(8,128)(2,1)}, bf16[128,2048]{1,0:T(8,128)(2,1)}) custom-call(bf16[128,2048]{1,0:T(8,128)(2,1)S(1)} %copy-done.5, bf16[128,2048]{1,0:T(8,128)(2,1)S(1)} %copy-done.6, f32[2048,128]{1,0:T(8,128)S(1)} %get-tuple-element.26.dconv_ref, ...), custom_call_target="tpu_custom_call", output_to_operand_aliasing={{0}: (9, {})} | custom-call | tf_op jit(solution)/shard_map/pallas_call | solution.py:708
  (1 shorter events, 0.0 us)
Async XLA Ops:
  3.9 14.9 %copy-start = (f32[16,2048]{1,0:T(8,128)S(1)}, f32[16,2048]{1,0:T(8,128)}, u32[]{:S(2)}) copy-start(f32[16,2048]{1,0:T(8,128)} %decay_ref.7) | copy-start | bytes 393220
  4.0 14.9 %copy-start.2 = (f32[3,3,2048]{2,1,0:T(4,128)S(1)}, f32[3,3,2048]{2,1,0:T(4,128)}, u32[]{:S(2)}) copy-start(f32[3,3,2048]{2,1,0:T(4,128)} %filter_ref.7) | copy-start | bytes 221188
  18.9 12.0 %copy-start.8 = (bf16[128,2048]{1,0:T(8,128)(2,1)S(1)}, bf16[128,2048]{1,0:T(8,128)(2,1)}, u32[]{:S(2)}) copy-start(bf16[128,2048]{1,0:T(8,128)(2,1)} %refs_4_.1) | copy-start | bytes 1572868
  19.7 11.1 %copy-start.10 = (f32[2048]{0:T(1024)S(1)}, f32[2048]{0:T(1024)}, u32[]{:S(2)}) copy-start(f32[2048]{0:T(1024)} %param.16) | copy-start | bytes 24580
  19.7 11.1 %all-to-all-start.1 = ((bf16[8,88,128]{2,1,0:T(8,128)(2,1)}), bf16[8,88,128]{2,1,0:T(8,128)(2,1)S(1)}, u32[]{:S(2)}, u32[]{:S(2)}) async-start(bf16[8,88,128]{2,1,0:T(8,128)(2,1)} %bitcast.2), calls=%async_computation.1 | async-start | bytes 360448 | tf_op jit(solution)/shard_map/all_to_all | solution.py:351
  23.2 7.6 %copy-start.1 = (f32[16,2048]{1,0:T(8,128)S(1)}, f32[16,2048]{1,0:T(8,128)}, u32[]{:S(2)}) copy-start(f32[16,2048]{1,0:T(8,128)} %decay_ref.7) | copy-start | bytes 393220
  23.2 7.6 %copy-start.3 = (f32[3,3,2048]{2,1,0:T(4,128)S(1)}, f32[3,3,2048]{2,1,0:T(4,128)}, u32[]{:S(2)}) copy-start(f32[3,3,2048]{2,1,0:T(4,128)} %filter_ref.7) | copy-start | bytes 221188
  23.3 7.6 %copy-start.4 = (bf16[128,2048]{1,0:T(8,128)(2,1)S(1)}, bf16[128,2048]{1,0:T(8,128)(2,1)}, u32[]{:S(2)}) copy-start(bf16[128,2048]{1,0:T(8,128)(2,1)} %refs_2_.1) | copy-start | bytes 1572868
  23.3 7.6 %copy-start.7 = (bf16[128,2048]{1,0:T(8,128)(2,1)S(1)}, bf16[128,2048]{1,0:T(8,128)(2,1)}, u32[]{:S(2)}) copy-start(bf16[128,2048]{1,0:T(8,128)(2,1)} %refs_3_.1) | copy-start | bytes 1572868
  23.3 7.6 %copy-start.9 = (f32[16,2048]{1,0:T(8,128)S(1)}, f32[16,2048]{1,0:T(8,128)}, u32[]{:S(2)}) copy-start(f32[16,2048]{1,0:T(8,128)} %residue_ref.3) | copy-start | bytes 393220
  41.8 20.8 %copy-start.6 = (bf16[128,2048]{1,0:T(8,128)(2,1)S(1)}, bf16[128,2048]{1,0:T(8,128)(2,1)}, u32[]{:S(2)}) copy-start(bf16[128,2048]{1,0:T(8,128)(2,1)} %v_ref.1) | copy-start | bytes 1572868
  52.2 10.4 %copy-start.5 = (bf16[128,2048]{1,0:T(8,128)(2,1)S(1)}, bf16[128,2048]{1,0:T(8,128)(2,1)}, u32[]{:S(2)}) copy-start(bf16[128,2048]{1,0:T(8,128)(2,1)} %k_ref.1) | copy-start | bytes 1572868

commit v5 on v4

--- a/solution.py
+++ b/solution.py
@@ -114,6 +114,16 @@
     return pairs[::-1] if reverse else pairs
 
 
+def long_steps(s):
+    blocks = s.length // SUB
+    return next(n for n in (4, 2, 1) if blocks % n == 0)
+
+
+def positions(blocks, reverse=False):
+    pairs = [(block, offset) for block in range(blocks) for offset in range(SUB)]
+    return pairs[::-1] if reverse else pairs
+
+
 def stage_modes(s, x_ref, out_ref, f):
     for g in range(s.modes // SUB):
         rows = f(x_ref[g * SUB : (g + 1) * SUB, :])
@@ -170,12 +180,13 @@
 
 
 def recur(s, from_ref, to_ref, p, w, states, h, reverse=False):
-    steps = s.length // 16
+    blocks = long_steps(s)
+    steps = s.length // (SUB * blocks)
 
     def step(i, states):
         i = steps - 1 - i if reverse else i
-        for block, offset in sixteen(0, reverse):
-            rows = major(s, (2 * i + block) * SUB + offset, h)
+        for block, offset in positions(blocks, reverse):
+            rows = major(s, (blocks * i + block) * SUB + offset, h)
             signal = from_ref[rows, :]
             states = [p[m] * states[m] + signal for m in range(s.modes)]
             to_ref[rows, :] = total([w[m] * states[m] for m in range(s.modes)])
@@ -244,13 +255,15 @@
 
         held = products(s, kb, vb, ks, vs, prod, taps_k, taps_v, h)
 
+        blocks = long_steps(s)
+
         def step(i, states):
-            for block, offset in sixteen(0):
-                product = prod[major(s, (2 * i + block) * SUB + offset, h), :]
+            for block, offset in positions(blocks):
+                product = prod[major(s, (blocks * i + block) * SUB + offset, h), :]
                 states = [p[m] * states[m] + product for m in range(s.modes)]
             return states
 
-        states = lax.fori_loop(0, s.length // 16, step, [blank] * s.modes)
+        states = lax.fori_loop(0, s.length // (SUB * blocks), step, [blank] * s.modes)
         put_states(s, pay_s, states, h)
         k1, k2, v1, v2 = held
         first = [staged(s, 0, offset, h) for offset in range(2)]
@@ -556,14 +569,17 @@
     def ends(h):
         p = mode_tiles(s, poles, h)
 
+        blocks = long_steps(s)
+        many = s.length // (SUB * blocks)
+
         def step(i, states):
-            for block, offset in sixteen(0, True):
-                t = (2 * (steps - 1 - i) + block) * SUB + offset
+            for block, offset in positions(blocks, True):
+                t = (blocks * (many - 1 - i) + block) * SUB + offset
                 dconv = dconv_ref[major(s, t, h), :]
                 states = [p[m] * states[m] + dconv for m in range(s.modes)]
             return states
 
-        states = lax.fori_loop(0, steps, step, [blank] * s.modes)
+        states = lax.fori_loop(0, many, step, [blank] * s.modes)
         for m in range(s.modes):
             pay_ref[backward_slice(s, m, h), :] = states[m]
         first = [ds[staged(s, 0, offset, h), :] * conv_ref[major(s, offset, h), :] for offset in range(2)]

time: 67.6 us -> 67.5 us (level)
  no operation moved by 1% of the time
where the time goes in v5:
time: 67.5 us; the launch traced here: 67 us
  blocking collectives  41.3 us (61%)
  Pallas kernels  18.3 us (27%)
  starting transfers between devices  3.52 us (5%)
  waiting for transfers between devices  3.05 us (5%)
  between operations  0.78 us (1%)
    all_to_all x2, blocking collectives, exchange(): got = lax.all_to_all(pay.reshape(chunks), 'seq', 0, 0, tiled=True)  25.3 us
    pallas_call x5, Pallas kernels, call(): pl.pallas_call(functools.partial(kernel, s), in_specs=[there if c == 'h'...  17.4 us
    all_to_all x1, blocking collectives, exchange(): lax.all_to_all(back.reshape(chunks), 'seq', 0, 0, tiled=True)  10.4 us
    psum x1, blocking collectives, body(): sums = lax.psum(sums, 'tp')  5.67 us
    all_to_all x1, starting transfers between devices, exchange(): lax.all_to_all(back.reshape(chunks), 'seq', 0, 0, tiled=True)  3.52 us
    all_to_all x1, waiting for transfers between devices, exchange(): lax.all_to_all(back.reshape(chunks), 'seq', 0, 0, tiled=True)  3.05 us
  transfers between devices with their start and end apart: 1, of which 1 were waited for; matrix products, arithmetic and copies ran while one was open for 0% of the time, Pallas kernels for 7%

profile of v5, /device:TPU:0, one launch (start us, length us, event | category | flops | bytes accessed | tf_op | source)
XLA Modules:
  0.0 67.0 jit_solution(678523420300537340)
XLA Ops:
  0.6 3.3 %shard_map.129 = bf16[704,128]{1,0:T(8,128)(2,1)S(1)} custom-call(bf16[128,2048]{1,0:T(8,128)(2,1)} %refs_2_.1, bf16[128,2048]{1,0:T(8,128)(2,1)} %k_ref.1, bf16[128,2048]{1,0:T(8,128)(2,1)} %v_ref.1, f32[3,3,2048]{2,1,0:T(4,128)} %filter_ref.7, f32[16,2048]{1,0:T(8,128)} %decay_ref.7), custom_call_target="tpu_custom_call" | custom-call | tf_op jit(solution)/shard_map/pallas_call | solution.py:724
  3.9 0.0 copy-start
  3.9 0.0 copy-start.2
  3.9 14.9 %all_to_all.20 = bf16[8,88,128]{2,1,0:T(8,128)(2,1)S(1)} all-to-all(bf16[8,88,128]{2,1,0:T(8,128)(2,1)S(1)} %bitcast.11), channel_id=1, replica_groups=mesh['seq'=8,'tp'=4] {'seq'}, dimensions={0} | all-to-all | bytes 360448 | tf_op jit(solution)/shard_map/all_to_all | solution.py:357
  18.8 0.0 copy-done
  18.8 0.0 copy-done.2
  18.8 0.0 copy-start.8
  18.8 0.8 %shard_map.130 = bf16[704,128]{1,0:T(8,128)(2,1)} custom-call(bf16[704,128]{1,0:T(8,128)(2,1)S(1)} %bitcast.10, f32[16,2048]{1,0:T(8,128)S(1)} %copy-done, f32[3,3,2048]{2,1,0:T(4,128)S(1)} %copy-done.2), custom_call_target="tpu_custom_call" | custom-call | tf_op jit(solution)/shard_map/pallas_call | solution.py:358
  19.7 0.0 copy-start.10
  19.7 3.5 %all-to-all-start.1 = ((bf16[8,88,128]{2,1,0:T(8,128)(2,1)}), bf16[8,88,128]{2,1,0:T(8,128)(2,1)S(1)}, u32[]{:S(2)}, u32[]{:S(2)}) async-start(bf16[8,88,128]{2,1,0:T(8,128)(2,1)} %bitcast.2), calls=%async_computation.1 | async-start | bytes 360448 | tf_op jit(solution)/shard_map/all_to_all | solution.py:364
  23.2 0.0 copy-start.1
  23.2 0.0 copy-start.3
  23.2 0.0 copy-start.4
  23.2 0.0 copy-start.7
  23.2 0.0 copy-start.9
  23.2 4.5 %shard_map.128 = (f32[2048,128]{1,0:T(8,128)S(1)}, f32[64,128]{1,0:T(8,128)S(1)}) custom-call(bf16[128,2048]{1,0:T(8,128)(2,1)} %k_ref.1, bf16[128,2048]{1,0:T(8,128)(2,1)} %v_ref.1, f32[3,3,2048]{2,1,0:T(4,128)} %filter_ref.7, f32[16,2048]{1,0:T(8,128)} %decay_ref.7, f32[16,2048]{1,0:T(8,128)} %residue_ref.3), custom_call_target="tpu_custom_call" | custom-call | flops 19660800 | bytes 3145728 | tf_op jit(solution)/shard_map/pallas_call | solution.py:724
  27.7 3.0 %all-to-all-done.1 = bf16[8,88,128]{2,1,0:T(8,128)(2,1)S(1)} async-done(((bf16[8,88,128]{2,1,0:T(8,128)(2,1)}), bf16[8,88,128]{2,1,0:T(8,128)(2,1)S(1)}, u32[]{:S(2)}, u32[]{:S(2)}) %all-to-all-start.1) | async-done | bytes 180256 | tf_op jit(solution)/shard_map/all_to_all | solution.py:364
  30.8 0.0 copy-done.8
  30.8 0.0 copy-done.10
  30.8 0.0 copy-done.1
  30.8 0.0 copy-done.3
  30.8 0.0 copy-done.4
  30.8 0.0 copy-done.7
  30.8 0.0 copy-done.9
  30.8 2.4 %shard_map.131 = (f32[2048,128]{1,0:T(8,128)S(1)}, f32[2,128]{1,0:T(2,128)S(1)}, f32[160,128]{1,0:T(8,128)S(1)}) custom-call(f32[2048,128]{1,0:T(8,128)S(1)} %get-tuple-element.19.inside_ref, f32[64,128]{1,0:T(8,128)S(1)} %get-tuple-element.20.first_ref, bf16[128,2048]{1,0:T(8,128)(2,1)S(1)} %copy-done.4, ...), custom_call_target="tpu_custom_call", output_to_operand_aliasing={{0}: (0, {})} | custom-call | tf_op jit(solution)/shard_map/pallas_call | solution.py:724
  33.2 5.7 %psum.7.refs_0_ = f32[2,128]{1,0:T(2,128)S(1)} all-reduce(f32[2,128]{1,0:T(2,128)S(1)} %get-tuple-element.21), channel_id=1, replica_groups=mesh['seq'=8,'tp'=4] {'tp'}, use_global_device_ids=true, to_apply=%region_0.0 | all-reduce | flops 256 | bytes 2048 | tf_op jit(solution)/shard_map/psum | solution.py:771
  38.9 2.8 %shard_map.132 = (bf16[128,2048]{1,0:T(8,128)(2,1)}, bf16[128,2048]{1,0:T(8,128)(2,1)}, bf16[128,2048]{1,0:T(8,128)(2,1)}, f32[2048,128]{1,0:T(8,128)S(1)}, f32[...) custom-call(f32[2,128]{1,0:T(2,128)S(1)} %psum.7.refs_0_, f32[2048,128]{1,0:T(8,128)S(1)} %get-tuple-element.22.refs_1_, ...), custom_call_target="tpu_custom_call" | custom-call | tf_op jit(solution)/shard_map/pallas_call | solution.py:724
  41.7 0.0 copy-start.6
  41.7 10.4 %all_to_all.21 = f32[8,40,128]{2,1,0:T(8,128)S(1)} all-to-all(f32[8,40,128]{2,1,0:T(8,128)S(1)} %bitcast.15), channel_id=1, replica_groups=mesh['seq'=8,'tp'=4] {'seq'}, dimensions={0} | all-to-all | bytes 327680 | tf_op jit(solution)/shard_map/all_to_all | solution.py:357
  52.1 0.0 copy-start.5
  52.1 10.4 %all_to_all.22 = f32[8,40,128]{2,1,0:T(8,128)S(1)} all-to-all(f32[8,40,128]{2,1,0:T(8,128)S(1)} %bitcast.14), channel_id=1, replica_groups=mesh['seq'=8,'tp'=4] {'seq'}, dimensions={0} | all-to-all | bytes 327680 | tf_op jit(solution)/shard_map/all_to_all | solution.py:364
  62.5 0.0 copy-done.6
  62.5 0.0 copy-done.5
  62.5 4.5 %shard_map.134 = (bf16[128,2048]{1,0:T(8,128)(2,1)}, bf16[128,2048]{1,0:T(8,128)(2,1)}, bf16[128,2048]{1,0:T(8,128)(2,1)}) custom-call(bf16[128,2048]{1,0:T(8,128)(2,1)S(1)} %copy-done.5, bf16[128,2048]{1,0:T(8,128)(2,1)S(1)} %copy-done.6, f32[2048,128]{1,0:T(8,128)S(1)} %get-tuple-element.26.dconv_ref, ...), custom_call_target="tpu_custom_call", output_to_operand_aliasing={{0}: (9, {})} | custom-call | tf_op jit(solution)/shard_map/pallas_call | solution.py:724
  (1 shorter events, 0.0 us)
Async XLA Ops:
  3.9 14.9 %copy-start = (f32[16,2048]{1,0:T(8,128)S(1)}, f32[16,2048]{1,0:T(8,128)}, u32[]{:S(2)}) copy-start(f32[16,2048]{1,0:T(8,128)} %decay_ref.7) | copy-start | bytes 393220
  3.9 14.9 %copy-start.2 = (f32[3,3,2048]{2,1,0:T(4,128)S(1)}, f32[3,3,2048]{2,1,0:T(4,128)}, u32[]{:S(2)}) copy-start(f32[3,3,2048]{2,1,0:T(4,128)} %filter_ref.7) | copy-start | bytes 221188
  18.8 12.0 %copy-start.8 = (bf16[128,2048]{1,0:T(8,128)(2,1)S(1)}, bf16[128,2048]{1,0:T(8,128)(2,1)}, u32[]{:S(2)}) copy-start(bf16[128,2048]{1,0:T(8,128)(2,1)} %refs_4_.1) | copy-start | bytes 1572868
  19.7 11.1 %copy-start.10 = (f32[2048]{0:T(1024)S(1)}, f32[2048]{0:T(1024)}, u32[]{:S(2)}) copy-start(f32[2048]{0:T(1024)} %param.16) | copy-start | bytes 24580
  19.7 11.1 %all-to-all-start.1 = ((bf16[8,88,128]{2,1,0:T(8,128)(2,1)}), bf16[8,88,128]{2,1,0:T(8,128)(2,1)S(1)}, u32[]{:S(2)}, u32[]{:S(2)}) async-start(bf16[8,88,128]{2,1,0:T(8,128)(2,1)} %bitcast.2), calls=%async_computation.1 | async-start | bytes 360448 | tf_op jit(solution)/shard_map/all_to_all | solution.py:364
  23.2 7.6 %copy-start.1 = (f32[16,2048]{1,0:T(8,128)S(1)}, f32[16,2048]{1,0:T(8,128)}, u32[]{:S(2)}) copy-start(f32[16,2048]{1,0:T(8,128)} %decay_ref.7) | copy-start | bytes 393220
  23.2 7.6 %copy-start.3 = (f32[3,3,2048]{2,1,0:T(4,128)S(1)}, f32[3,3,2048]{2,1,0:T(4,128)}, u32[]{:S(2)}) copy-start(f32[3,3,2048]{2,1,0:T(4,128)} %filter_ref.7) | copy-start | bytes 221188
  23.2 7.6 %copy-start.4 = (bf16[128,2048]{1,0:T(8,128)(2,1)S(1)}, bf16[128,2048]{1,0:T(8,128)(2,1)}, u32[]{:S(2)}) copy-start(bf16[128,2048]{1,0:T(8,128)(2,1)} %refs_2_.1) | copy-start | bytes 1572868
  23.2 7.6 %copy-start.7 = (bf16[128,2048]{1,0:T(8,128)(2,1)S(1)}, bf16[128,2048]{1,0:T(8,128)(2,1)}, u32[]{:S(2)}) copy-start(bf16[128,2048]{1,0:T(8,128)(2,1)} %refs_3_.1) | copy-start | bytes 1572868
  23.2 7.6 %copy-start.9 = (f32[16,2048]{1,0:T(8,128)S(1)}, f32[16,2048]{1,0:T(8,128)}, u32[]{:S(2)}) copy-start(f32[16,2048]{1,0:T(8,128)} %residue_ref.3) | copy-start | bytes 393220
  41.7 20.8 %copy-start.6 = (bf16[128,2048]{1,0:T(8,128)(2,1)S(1)}, bf16[128,2048]{1,0:T(8,128)(2,1)}, u32[]{:S(2)}) copy-start(bf16[128,2048]{1,0:T(8,128)(2,1)} %v_ref.1) | copy-start | bytes 1572868
  52.1 10.4 %copy-start.5 = (bf16[128,2048]{1,0:T(8,128)(2,1)S(1)}, bf16[128,2048]{1,0:T(8,128)(2,1)}, u32[]{:S(2)}) copy-start(bf16[128,2048]{1,0:T(8,128)(2,1)} %k_ref.1) | copy-start | bytes 1572868

commit v6 on v5

--- a/solution.py
+++ b/solution.py
@@ -114,6 +114,12 @@
     return pairs[::-1] if reverse else pairs
 
 
+def paired_loop(steps, step, carry):
+    if steps % 2:
+        return lax.fori_loop(0, steps, step, carry)
+    return lax.fori_loop(0, steps // 2, lambda i, carry: step(2 * i + 1, step(2 * i, carry)), carry)
+
+
 def long_steps(s):
     blocks = s.length // SUB
     return next(n for n in (4, 2, 1) if blocks % n == 0)
@@ -176,7 +182,7 @@
             k1, k2, v1, v2 = k0, k1, v0, v1
         return k1, k2, v1, v2
 
-    return lax.fori_loop(0, s.length // 16, step, (jnp.zeros((SUB, LANES), f32),) * 4)
+    return paired_loop(s.length // 16, step, (jnp.zeros((SUB, LANES), f32),) * 4)
 
 
 def recur(s, from_ref, to_ref, p, w, states, h, reverse=False):
@@ -483,7 +489,7 @@
             return (q1, q2), states
 
         bring(0)
-        lax.fori_loop(0, steps, step, ((qb, qa), states))
+        paired_loop(steps, step, ((qb, qa), states))
 
     each_half(s, half)
     for r, ref in enumerate((squares, inners)):
@@ -556,7 +562,7 @@
 
         bring(0)
         held = (near_ref[major(s, 5, h), :], near_ref[major(s, 4, h), :], blank, blank)
-        _, _, dq1, dq2 = lax.fori_loop(0, steps, step, held)
+        _, _, dq1, dq2 = paired_loop(steps, step, held)
         qs[staged(s, 2 * steps + 1, 6, h), :] = taps_q[0] * dq2 + taps_q[1] * dq1
         qs[staged(s, 2 * steps + 1, 7, h), :] = taps_q[0] * dq1
         for i, copy in enumerate(pieces(h)):
@@ -683,7 +689,7 @@
             unstage(s, vs, vgrad_b, i + 1, h, i)
             return inputs, grads
 
-        lax.fori_loop(0, steps, step, (inputs, grads))
+        paired_loop(steps, step, (inputs, grads))
         for i, copy in enumerate(pieces(h)):
             copy.start(priority=i % 2)
 

time: 67.5 us -> 67.2 us (level)
  no operation moved by 1% of the time
where the time goes in v6:
time: 67.2 us; the launch traced here: 66.8 us
  blocking collectives  41.3 us (61%)
  Pallas kernels  18 us (27%)
  starting transfers between devices  3.52 us (5%)
  waiting for transfers between devices  3.13 us (5%)
  between operations  0.78 us (1%)
    all_to_all x2, blocking collectives, exchange(): got = lax.all_to_all(pay.reshape(chunks), 'seq', 0, 0, tiled=True)  25.2 us
    pallas_call x5, Pallas kernels, call(): pl.pallas_call(functools.partial(kernel, s), in_specs=[there if c == 'h'...  17.1 us
    all_to_all x1, blocking collectives, exchange(): lax.all_to_all(back.reshape(chunks), 'seq', 0, 0, tiled=True)  10.4 us
    psum x1, blocking collectives, body(): sums = lax.psum(sums, 'tp')  5.67 us
    all_to_all x1, starting transfers between devices, exchange(): lax.all_to_all(back.reshape(chunks), 'seq', 0, 0, tiled=True)  3.52 us
    all_to_all x1, waiting for transfers between devices, exchange(): lax.all_to_all(back.reshape(chunks), 'seq', 0, 0, tiled=True)  3.13 us
  transfers between devices with their start and end apart: 1, of which 1 were waited for; matrix products, arithmetic and copies ran while one was open for 0% of the time, Pallas kernels for 7%

profile of v6, /device:TPU:0, one launch (start us, length us, event | category | flops | bytes accessed | tf_op | source)
XLA Modules:
  0.0 66.8 jit_solution(17072579722283305433)
XLA Ops:
  0.6 3.2 %shard_map.129 = bf16[704,128]{1,0:T(8,128)(2,1)S(1)} custom-call(bf16[128,2048]{1,0:T(8,128)(2,1)} %refs_2_.1, bf16[128,2048]{1,0:T(8,128)(2,1)} %k_ref.1, bf16[128,2048]{1,0:T(8,128)(2,1)} %v_ref.1, f32[3,3,2048]{2,1,0:T(4,128)} %filter_ref.7, f32[16,2048]{1,0:T(8,128)} %decay_ref.7), custom_call_target="tpu_custom_call" | custom-call | tf_op jit(solution)/shard_map/pallas_call | solution.py:730
  3.8 0.0 copy-start
  3.8 0.0 copy-start.2
  3.8 14.9 %all_to_all.20 = bf16[8,88,128]{2,1,0:T(8,128)(2,1)S(1)} all-to-all(bf16[8,88,128]{2,1,0:T(8,128)(2,1)S(1)} %bitcast.11), channel_id=1, replica_groups=mesh['seq'=8,'tp'=4] {'seq'}, dimensions={0} | all-to-all | bytes 360448 | tf_op jit(solution)/shard_map/all_to_all | solution.py:363
  18.7 0.0 copy-done
  18.7 0.0 copy-done.2
  18.8 0.0 copy-start.8
  18.8 0.8 %shard_map.130 = bf16[704,128]{1,0:T(8,128)(2,1)} custom-call(bf16[704,128]{1,0:T(8,128)(2,1)S(1)} %bitcast.10, f32[16,2048]{1,0:T(8,128)S(1)} %copy-done, f32[3,3,2048]{2,1,0:T(4,128)S(1)} %copy-done.2), custom_call_target="tpu_custom_call" | custom-call | tf_op jit(solution)/shard_map/pallas_call | solution.py:364
  19.6 0.0 copy-start.10
  19.6 3.5 %all-to-all-start.1 = ((bf16[8,88,128]{2,1,0:T(8,128)(2,1)}), bf16[8,88,128]{2,1,0:T(8,128)(2,1)S(1)}, u32[]{:S(2)}, u32[]{:S(2)}) async-start(bf16[8,88,128]{2,1,0:T(8,128)(2,1)} %bitcast.2), calls=%async_computation.1 | async-start | bytes 360448 | tf_op jit(solution)/shard_map/all_to_all | solution.py:370
  23.1 0.0 copy-start.1
  23.1 0.0 copy-start.3
  23.1 0.0 copy-start.4
  23.1 0.0 copy-start.7
  23.1 0.0 copy-start.9
  23.2 4.4 %shard_map.128 = (f32[2048,128]{1,0:T(8,128)S(1)}, f32[64,128]{1,0:T(8,128)S(1)}) custom-call(bf16[128,2048]{1,0:T(8,128)(2,1)} %k_ref.1, bf16[128,2048]{1,0:T(8,128)(2,1)} %v_ref.1, f32[3,3,2048]{2,1,0:T(4,128)} %filter_ref.7, f32[16,2048]{1,0:T(8,128)} %decay_ref.7, f32[16,2048]{1,0:T(8,128)} %residue_ref.3), custom_call_target="tpu_custom_call" | custom-call | flops 19660800 | bytes 3145728 | tf_op jit(solution)/shard_map/pallas_call | solution.py:730
  27.6 3.1 %all-to-all-done.1 = bf16[8,88,128]{2,1,0:T(8,128)(2,1)S(1)} async-done(((bf16[8,88,128]{2,1,0:T(8,128)(2,1)}), bf16[8,88,128]{2,1,0:T(8,128)(2,1)S(1)}, u32[]{:S(2)}, u32[]{:S(2)}) %all-to-all-start.1) | async-done | bytes 180256 | tf_op jit(solution)/shard_map/all_to_all | solution.py:370
  30.7 0.0 copy-done.8
  30.7 0.0 copy-done.10
  30.7 0.0 copy-done.1
  30.7 0.0 copy-done.3
  30.7 0.0 copy-done.4
  30.7 0.0 copy-done.7
  30.7 0.0 copy-done.9
  30.8 2.3 %shard_map.131 = (f32[2048,128]{1,0:T(8,128)S(1)}, f32[2,128]{1,0:T(2,128)S(1)}, f32[160,128]{1,0:T(8,128)S(1)}) custom-call(f32[2048,128]{1,0:T(8,128)S(1)} %get-tuple-element.19.inside_ref, f32[64,128]{1,0:T(8,128)S(1)} %get-tuple-element.20.first_ref, bf16[128,2048]{1,0:T(8,128)(2,1)S(1)} %copy-done.4, ...), custom_call_target="tpu_custom_call", output_to_operand_aliasing={{0}: (0, {})} | custom-call | tf_op jit(solution)/shard_map/pallas_call | solution.py:730
  33.1 5.7 %psum.7.refs_0_ = f32[2,128]{1,0:T(2,128)S(1)} all-reduce(f32[2,128]{1,0:T(2,128)S(1)} %get-tuple-element.21), channel_id=1, replica_groups=mesh['seq'=8,'tp'=4] {'tp'}, use_global_device_ids=true, to_apply=%region_0.0 | all-reduce | flops 256 | bytes 2048 | tf_op jit(solution)/shard_map/psum | solution.py:777
  38.7 2.8 %shard_map.132 = (bf16[128,2048]{1,0:T(8,128)(2,1)}, bf16[128,2048]{1,0:T(8,128)(2,1)}, bf16[128,2048]{1,0:T(8,128)(2,1)}, f32[2048,128]{1,0:T(8,128)S(1)}, f32[...) custom-call(f32[2,128]{1,0:T(2,128)S(1)} %psum.7.refs_0_, f32[2048,128]{1,0:T(8,128)S(1)} %get-tuple-element.22.refs_1_, ...), custom_call_target="tpu_custom_call" | custom-call | tf_op jit(solution)/shard_map/pallas_call | solution.py:730
  41.5 0.0 copy-start.6
  41.5 10.3 %all_to_all.21 = f32[8,40,128]{2,1,0:T(8,128)S(1)} all-to-all(f32[8,40,128]{2,1,0:T(8,128)S(1)} %bitcast.15), channel_id=1, replica_groups=mesh['seq'=8,'tp'=4] {'seq'}, dimensions={0} | all-to-all | bytes 327680 | tf_op jit(solution)/shard_map/all_to_all | solution.py:363
  51.8 0.0 copy-start.5
  51.9 10.4 %all_to_all.22 = f32[8,40,128]{2,1,0:T(8,128)S(1)} all-to-all(f32[8,40,128]{2,1,0:T(8,128)S(1)} %bitcast.14), channel_id=1, replica_groups=mesh['seq'=8,'tp'=4] {'seq'}, dimensions={0} | all-to-all | bytes 327680 | tf_op jit(solution)/shard_map/all_to_all | solution.py:370
  62.3 0.0 copy-done.6
  62.3 0.0 copy-done.5
  62.3 4.5 %shard_map.134 = (bf16[128,2048]{1,0:T(8,128)(2,1)}, bf16[128,2048]{1,0:T(8,128)(2,1)}, bf16[128,2048]{1,0:T(8,128)(2,1)}) custom-call(bf16[128,2048]{1,0:T(8,128)(2,1)S(1)} %copy-done.5, bf16[128,2048]{1,0:T(8,128)(2,1)S(1)} %copy-done.6, f32[2048,128]{1,0:T(8,128)S(1)} %get-tuple-element.26.dconv_ref, ...), custom_call_target="tpu_custom_call", output_to_operand_aliasing={{0}: (9, {})} | custom-call | tf_op jit(solution)/shard_map/pallas_call | solution.py:730
  (1 shorter events, 0.0 us)
Async XLA Ops:
  3.8 14.9 %copy-start = (f32[16,2048]{1,0:T(8,128)S(1)}, f32[16,2048]{1,0:T(8,128)}, u32[]{:S(2)}) copy-start(f32[16,2048]{1,0:T(8,128)} %decay_ref.7) | copy-start | bytes 393220
  3.8 14.9 %copy-start.2 = (f32[3,3,2048]{2,1,0:T(4,128)S(1)}, f32[3,3,2048]{2,1,0:T(4,128)}, u32[]{:S(2)}) copy-start(f32[3,3,2048]{2,1,0:T(4,128)} %filter_ref.7) | copy-start | bytes 221188
  18.8 12.0 %copy-start.8 = (bf16[128,2048]{1,0:T(8,128)(2,1)S(1)}, bf16[128,2048]{1,0:T(8,128)(2,1)}, u32[]{:S(2)}) copy-start(bf16[128,2048]{1,0:T(8,128)(2,1)} %refs_4_.1) | copy-start | bytes 1572868
  19.6 11.1 %copy-start.10 = (f32[2048]{0:T(1024)S(1)}, f32[2048]{0:T(1024)}, u32[]{:S(2)}) copy-start(f32[2048]{0:T(1024)} %param.16) | copy-start | bytes 24580
  19.6 11.1 %all-to-all-start.1 = ((bf16[8,88,128]{2,1,0:T(8,128)(2,1)}), bf16[8,88,128]{2,1,0:T(8,128)(2,1)S(1)}, u32[]{:S(2)}, u32[]{:S(2)}) async-start(bf16[8,88,128]{2,1,0:T(8,128)(2,1)} %bitcast.2), calls=%async_computation.1 | async-start | bytes 360448 | tf_op jit(solution)/shard_map/all_to_all | solution.py:370
  23.1 7.6 %copy-start.1 = (f32[16,2048]{1,0:T(8,128)S(1)}, f32[16,2048]{1,0:T(8,128)}, u32[]{:S(2)}) copy-start(f32[16,2048]{1,0:T(8,128)} %decay_ref.7) | copy-start | bytes 393220
  23.1 7.6 %copy-start.3 = (f32[3,3,2048]{2,1,0:T(4,128)S(1)}, f32[3,3,2048]{2,1,0:T(4,128)}, u32[]{:S(2)}) copy-start(f32[3,3,2048]{2,1,0:T(4,128)} %filter_ref.7) | copy-start | bytes 221188
  23.1 7.6 %copy-start.4 = (bf16[128,2048]{1,0:T(8,128)(2,1)S(1)}, bf16[128,2048]{1,0:T(8,128)(2,1)}, u32[]{:S(2)}) copy-start(bf16[128,2048]{1,0:T(8,128)(2,1)} %refs_2_.1) | copy-start | bytes 1572868
  23.1 7.6 %copy-start.7 = (bf16[128,2048]{1,0:T(8,128)(2,1)S(1)}, bf16[128,2048]{1,0:T(8,128)(2,1)}, u32[]{:S(2)}) copy-start(bf16[128,2048]{1,0:T(8,128)(2,1)} %refs_3_.1) | copy-start | bytes 1572868
  23.1 7.6 %copy-start.9 = (f32[16,2048]{1,0:T(8,128)S(1)}, f32[16,2048]{1,0:T(8,128)}, u32[]{:S(2)}) copy-start(f32[16,2048]{1,0:T(8,128)} %residue_ref.3) | copy-start | bytes 393220
  41.5 20.8 %copy-start.6 = (bf16[128,2048]{1,0:T(8,128)(2,1)S(1)}, bf16[128,2048]{1,0:T(8,128)(2,1)}, u32[]{:S(2)}) copy-start(bf16[128,2048]{1,0:T(8,128)(2,1)} %v_ref.1) | copy-start | bytes 1572868
  51.8 10.4 %copy-start.5 = (bf16[128,2048]{1,0:T(8,128)(2,1)S(1)}, bf16[128,2048]{1,0:T(8,128)(2,1)}, u32[]{:S(2)}) copy-start(bf16[128,2048]{1,0:T(8,128)(2,1)} %k_ref.1) | copy-start | bytes 1572868

commit v7 on v6

--- a/solution.py
+++ b/solution.py
@@ -393,8 +393,8 @@
 
 
 def inside_kernel(
-    s, k_hbm, v_hbm, filter_hbm, decay_hbm, residue_hbm, inside_ref, first_ref,
-    kb, vb, fb, db, rb, ks, vs, prod, taps, poles, weights, sems,
+    s, k_hbm, v_hbm, filter_hbm, decay_hbm, residue_hbm, inside_ref, first_ref, taps, poles, weights,
+    kb, vb, fb, db, rb, ks, vs, prod, sems,
 ):
     pairs = [(decay_hbm, db), (residue_hbm, rb), (filter_hbm, fb), (k_hbm, kb), (v_hbm, vb)]
     copies = [pltpu.make_async_copy(a, b, sems.at[i]) for i, (a, b) in enumerate(pairs)]
@@ -422,14 +422,10 @@
 
 
 def forward_kernel(
-    s, inside_ref, first_ref, q_ref, stream_ref, cot_ref, back_ref, filter_ref, decay_ref, residue_ref, gain_ref,
+    s, inside_ref, first_ref, q_ref, stream_ref, cot_ref, back_ref, taps, poles, weights, gain_ref,
     conv_ref, sums_ref, near_ref,
-    qs, xs, gs, back_s, taps, poles, weights, squares, inners,
+    qs, xs, gs, back_s, squares, inners,
 ):
-    stage_modes(s, decay_ref, poles, lambda x: jnp.exp(-x))
-    stage_modes(s, residue_ref, weights, lambda x: x)
-    stage_taps(s, filter_ref, taps)
-
     widened(back_ref, back_s)
     steps = s.length // 16
 
@@ -759,10 +755,12 @@
         + [pltpu.SemaphoreType.DMA((3 + 2 * s.halves,))],
         far(query_in, key_in, value_in, short_filter, decay_rate),
     )
-    inside, first = call(
-        inside_kernel, "hhhhh", "vv", (wide, jax.ShapeDtypeStruct((4 * s.tiles, LANES), f32)),
+    tiled = [jax.ShapeDtypeStruct(x.shape, f32) for x in (taps_s, mode_s, mode_s)]
+    inside, first, *tiled = call(
+        inside_kernel, "hhhhh", "vvvvv",
+        (wide, jax.ShapeDtypeStruct((4 * s.tiles, LANES), f32), *tiled),
         [narrow_s, narrow_s, filter_s, rates_s, rates_s]
-        + [wide_s] * 3 + [taps_s, mode_s, mode_s, pltpu.SemaphoreType.DMA((5,))],
+        + [wide_s] * 3 + [pltpu.SemaphoreType.DMA((5,))],
         far(key_in, value_in, short_filter, decay_rate, residue),
         cost=cost(75, 3),
     )
@@ -770,8 +768,8 @@
     conv, sums, near = call(
         forward_kernel, "v" * 10, "vvv",
         (wide, jax.ShapeDtypeStruct((2, length), f32), near_shape),
-        [wide_s] * 3 + [pltpu.VMEM(forward_shape, f32), taps_s, mode_s, mode_s, sum_s, sum_s],
-        (inside, first, query_in, stream, cotangent, back, short_filter, decay_rate, residue, gain),
+        [wide_s] * 3 + [pltpu.VMEM(forward_shape, f32), sum_s, sum_s],
+        (inside, first, query_in, stream, cotangent, back, *tiled, gain),
         {0: 0},
     )
     sums = lax.psum(sums, "tp")

time: 67.2 us -> 69.3 us (1.031)
  local copies, waits for them, and re-layouts: 0.06 us -> 1.61 us
  blocking collectives: 41.3 us -> 42.5 us
    unnamed x22 -> x26, local copies, waits for them, and re-layouts: 0.06 us -> 1.61 us
    all_to_all x2, blocking collectives: 25.2 us -> 26.5 us  [exchange(): got = lax.all_to_all(pay.reshape(chunks), 'seq', 0, 0, tiled=True)]
  transfers between devices with their start and end apart: 1 -> 1, of which waited for: 1 -> 1; matrix products, arithmetic and copies ran while one was open for 0% -> 0% of each run, Pallas kernels for 7% -> 6%
where the time goes in v7:
time: 69.3 us; the launch traced here: 68.8 us
  blocking collectives  42.5 us (61%)
  Pallas kernels  17.9 us (26%)
  starting transfers between devices  3.52 us (5%)
  waiting for transfers between devices  2.52 us (4%)
  local copies, waits for them, and re-layouts  1.61 us (2%)
  between operations  0.76 us (1%)
    all_to_all x2, blocking collectives, exchange(): got = lax.all_to_all(pay.reshape(chunks), 'seq', 0, 0, tiled=True)  26.5 us
    pallas_call x5, Pallas kernels, call(): pl.pallas_call(functools.partial(kernel, s), in_specs=[there if c == 'h'...  17.1 us
    all_to_all x1, blocking collectives, exchange(): lax.all_to_all(back.reshape(chunks), 'seq', 0, 0, tiled=True)  10.4 us
    psum x1, blocking collectives, body(): sums = lax.psum(sums, 'tp')  5.67 us
    all_to_all x1, starting transfers between devices, exchange(): lax.all_to_all(back.reshape(chunks), 'seq', 0, 0, tiled=True)  3.52 us
    all_to_all x1, waiting for transfers between devices, exchange(): lax.all_to_all(back.reshape(chunks), 'seq', 0, 0, tiled=True)  2.52 us
    unnamed x26, local copies, waits for them, and re-layouts  1.61 us
  transfers between devices with their start and end apart: 1, of which 1 were waited for; matrix products, arithmetic and copies ran while one was open for 0% of the time, Pallas kernels for 6%

profile of v7, /device:TPU:0, one launch (start us, length us, event | category | flops | bytes accessed | tf_op | source)
XLA Modules:
  0.0 68.8 jit_solution(7169660887708489432)
XLA Ops:
  0.6 3.2 %shard_map.129 = bf16[704,128]{1,0:T(8,128)(2,1)S(1)} custom-call(bf16[128,2048]{1,0:T(8,128)(2,1)} %refs_2_.1, bf16[128,2048]{1,0:T(8,128)(2,1)} %k_ref.1, bf16[128,2048]{1,0:T(8,128)(2,1)} %v_ref.1, f32[3,3,2048]{2,1,0:T(4,128)} %filter_ref.5, f32[16,2048]{1,0:T(8,128)} %decay_ref.5), custom_call_target="tpu_custom_call" | custom-call | tf_op jit(solution)/shard_map/pallas_call | solution.py:726
  3.8 0.0 copy-start.3
  3.8 0.0 copy-start.5
  3.8 14.9 %all_to_all.20 = bf16[8,88,128]{2,1,0:T(8,128)(2,1)S(1)} all-to-all(bf16[8,88,128]{2,1,0:T(8,128)(2,1)S(1)} %bitcast.11), channel_id=1, replica_groups=mesh['seq'=8,'tp'=4] {'seq'}, dimensions={0} | all-to-all | bytes 360448 | tf_op jit(solution)/shard_map/all_to_all | solution.py:363
  18.7 0.0 copy-done.3
  18.7 0.0 copy-done.5
  18.8 0.8 %shard_map.130 = bf16[704,128]{1,0:T(8,128)(2,1)} custom-call(bf16[704,128]{1,0:T(8,128)(2,1)S(1)} %bitcast.10, f32[16,2048]{1,0:T(8,128)S(1)} %copy-done.3, f32[3,3,2048]{2,1,0:T(4,128)S(1)} %copy-done.5), custom_call_target="tpu_custom_call" | custom-call | tf_op jit(solution)/shard_map/pallas_call | solution.py:364
  19.6 0.0 copy-start.8
  19.6 3.5 %all-to-all-start.1 = ((bf16[8,88,128]{2,1,0:T(8,128)(2,1)}), bf16[8,88,128]{2,1,0:T(8,128)(2,1)S(1)}, u32[]{:S(2)}, u32[]{:S(2)}) async-start(bf16[8,88,128]{2,1,0:T(8,128)(2,1)} %bitcast.2), calls=%async_computation.1 | async-start | bytes 360448 | tf_op jit(solution)/shard_map/all_to_all | solution.py:370
  23.1 0.0 copy-start
  23.1 0.0 copy-start.7
  23.1 4.4 %shard_map.128 = (f32[2048,128]{1,0:T(8,128)S(1)}, f32[64,128]{1,0:T(8,128)S(1)}, f32[384,128]{1,0:T(8,128)S(1)}, f32[256,128]{1,0:T(8,128)S(1)}, f32[256,128]{1,0:T(8,128)S(1)}) custom-call(bf16[128,2048]{1,0:T(8,128)(2,1)} %k_ref.1, bf16[128,2048]{1,0:T(8,128)(2,1)} %v_ref.1, f32[3,3,2048]{2,1,0:T(4,128)} %filter_ref.5, f32[16,2048]{1,0:T(8,128)} %decay_ref.5, ...), custom_call_target="tpu_custom_call" | custom-call | flops 19660800 | bytes 3145728 | tf_op jit(solution)/shard_map/pallas_call | solution.py:726
  27.5 0.0 copy-start.10
  27.5 0.6 copy-done.10
  28.2 0.0 copy-start.12
  28.2 2.5 %all-to-all-done.1 = bf16[8,88,128]{2,1,0:T(8,128)(2,1)S(1)} async-done(((bf16[8,88,128]{2,1,0:T(8,128)(2,1)}), bf16[8,88,128]{2,1,0:T(8,128)(2,1)S(1)}, u32[]{:S(2)}, u32[]{:S(2)}) %all-to-all-start.1) | async-done | bytes 180256 | tf_op jit(solution)/shard_map/all_to_all | solution.py:370
  30.7 0.0 copy-done.8
  30.7 0.0 copy-done
  30.7 0.0 copy-done.7
  30.7 0.0 copy-done.12
  30.7 0.0 copy-start.11
  30.7 0.9 %copy-done.11 = f32[256,128]{1,0:T(8,128)S(1)} copy-done((f32[256,128]{1,0:T(8,128)S(1)}, f32[256,128]{1,0:T(8,128)}, u32[]{:S(2)}) %copy-start.11) | copy-done | bytes 131096
  31.6 0.0 copy-start.4
  31.6 0.0 copy-start.6
  31.6 2.3 %shard_map.131 = (f32[2048,128]{1,0:T(8,128)S(1)}, f32[2,128]{1,0:T(2,128)S(1)}, f32[160,128]{1,0:T(8,128)S(1)}) custom-call(f32[2048,128]{1,0:T(8,128)S(1)} %get-tuple-element.22.inside_ref, f32[64,128]{1,0:T(8,128)S(1)} %get-tuple-element.23.first_ref, bf16[128,2048]{1,0:T(8,128)(2,1)S(1)} %copy-done, ...), custom_call_target="tpu_custom_call", output_to_operand_aliasing={{0}: (0, {})} | custom-call | tf_op jit(solution)/shard_map/pallas_call | solution.py:726
  33.9 5.7 %psum.7.refs_0_ = f32[2,128]{1,0:T(2,128)S(1)} all-reduce(f32[2,128]{1,0:T(2,128)S(1)} %get-tuple-element.27), channel_id=1, replica_groups=mesh['seq'=8,'tp'=4] {'tp'}, use_global_device_ids=true, to_apply=%region_0.0 | all-reduce | flops 256 | bytes 2048 | tf_op jit(solution)/shard_map/psum | solution.py:775
  39.6 0.0 copy-done.4
  39.6 0.0 copy-done.6
  39.6 2.8 %shard_map.132 = (bf16[128,2048]{1,0:T(8,128)(2,1)}, bf16[128,2048]{1,0:T(8,128)(2,1)}, bf16[128,2048]{1,0:T(8,128)(2,1)}, f32[2048,128]{1,0:T(8,128)S(1)}, f32[...) custom-call(f32[2,128]{1,0:T(2,128)S(1)} %psum.7.refs_0_, f32[2048,128]{1,0:T(8,128)S(1)} %get-tuple-element.28.refs_1_, ...), custom_call_target="tpu_custom_call" | custom-call | tf_op jit(solution)/shard_map/pallas_call | solution.py:726
  42.3 0.0 copy-start.2
  42.3 11.6 %all_to_all.21 = f32[8,40,128]{2,1,0:T(8,128)S(1)} all-to-all(f32[8,40,128]{2,1,0:T(8,128)S(1)} %bitcast.15), channel_id=1, replica_groups=mesh['seq'=8,'tp'=4] {'seq'}, dimensions={0} | all-to-all | bytes 327680 | tf_op jit(solution)/shard_map/all_to_all | solution.py:363
  53.9 0.0 copy-start.1
  53.9 0.0 copy-start.9
  53.9 10.4 %all_to_all.22 = f32[8,40,128]{2,1,0:T(8,128)S(1)} all-to-all(f32[8,40,128]{2,1,0:T(8,128)S(1)} %bitcast.14), channel_id=1, replica_groups=mesh['seq'=8,'tp'=4] {'seq'}, dimensions={0} | all-to-all | bytes 327680 | tf_op jit(solution)/shard_map/all_to_all | solution.py:370
  64.3 0.0 copy-done.2
  64.3 0.0 copy-done.1
  64.3 0.0 copy-done.9
  64.3 4.5 %shard_map.134 = (bf16[128,2048]{1,0:T(8,128)(2,1)}, bf16[128,2048]{1,0:T(8,128)(2,1)}, bf16[128,2048]{1,0:T(8,128)(2,1)}) custom-call(bf16[128,2048]{1,0:T(8,128)(2,1)S(1)} %copy-done.1, bf16[128,2048]{1,0:T(8,128)(2,1)S(1)} %copy-done.2, f32[2048,128]{1,0:T(8,128)S(1)} %get-tuple-element.32.dconv_ref, ...), custom_call_target="tpu_custom_call", output_to_operand_aliasing={{0}: (9, {})} | custom-call | tf_op jit(solution)/shard_map/pallas_call | solution.py:726
  (1 shorter events, 0.0 us)
Async XLA Ops:
  3.8 14.9 %copy-start.3 = (f32[16,2048]{1,0:T(8,128)S(1)}, f32[16,2048]{1,0:T(8,128)}, u32[]{:S(2)}) copy-start(f32[16,2048]{1,0:T(8,128)} %decay_ref.5) | copy-start | bytes 393220
  3.8 14.9 %copy-start.5 = (f32[3,3,2048]{2,1,0:T(4,128)S(1)}, f32[3,3,2048]{2,1,0:T(4,128)}, u32[]{:S(2)}) copy-start(f32[3,3,2048]{2,1,0:T(4,128)} %filter_ref.5) | copy-start | bytes 221188
  19.6 11.1 %copy-start.8 = (bf16[128,2048]{1,0:T(8,128)(2,1)S(1)}, bf16[128,2048]{1,0:T(8,128)(2,1)}, u32[]{:S(2)}) copy-start(bf16[128,2048]{1,0:T(8,128)(2,1)} %refs_4_.1) | copy-start | bytes 1572868
  19.6 11.1 %all-to-all-start.1 = ((bf16[8,88,128]{2,1,0:T(8,128)(2,1)}), bf16[8,88,128]{2,1,0:T(8,128)(2,1)S(1)}, u32[]{:S(2)}, u32[]{:S(2)}) async-start(bf16[8,88,128]{2,1,0:T(8,128)(2,1)} %bitcast.2), calls=%async_computation.1 | async-start | bytes 360448 | tf_op jit(solution)/shard_map/all_to_all | solution.py:370
  23.1 7.6 %copy-start = (bf16[128,2048]{1,0:T(8,128)(2,1)S(1)}, bf16[128,2048]{1,0:T(8,128)(2,1)}, u32[]{:S(2)}) copy-start(bf16[128,2048]{1,0:T(8,128)(2,1)} %refs_2_.1) | copy-start | bytes 1572868
  23.1 7.6 %copy-start.7 = (bf16[128,2048]{1,0:T(8,128)(2,1)S(1)}, bf16[128,2048]{1,0:T(8,128)(2,1)}, u32[]{:S(2)}) copy-start(bf16[128,2048]{1,0:T(8,128)(2,1)} %refs_3_.1) | copy-start | bytes 1572868
  27.5 0.7 copy-start.10
  28.2 2.5 %copy-start.12 = (f32[2048]{0:T(1024)S(1)}, f32[2048]{0:T(1024)}, u32[]{:S(2)}) copy-start(f32[2048]{0:T(1024)} %param.16) | copy-start | bytes 24580
  30.7 0.9 %copy-start.11 = (f32[256,128]{1,0:T(8,128)S(1)}, f32[256,128]{1,0:T(8,128)}, u32[]{:S(2)}) copy-start(f32[256,128]{1,0:T(8,128)} %copy-done.10) | copy-start | bytes 393220
  31.6 7.9 %copy-start.4 = (f32[16,2048]{1,0:T(8,128)S(1)}, f32[16,2048]{1,0:T(8,128)}, u32[]{:S(2)}) copy-start(f32[16,2048]{1,0:T(8,128)} %decay_ref.5) | copy-start | bytes 393220
  31.6 7.9 %copy-start.6 = (f32[3,3,2048]{2,1,0:T(4,128)S(1)}, f32[3,3,2048]{2,1,0:T(4,128)}, u32[]{:S(2)}) copy-start(f32[3,3,2048]{2,1,0:T(4,128)} %filter_ref.5) | copy-start | bytes 221188
  42.3 22.0 %copy-start.2 = (bf16[128,2048]{1,0:T(8,128)(2,1)S(1)}, bf16[128,2048]{1,0:T(8,128)(2,1)}, u32[]{:S(2)}) copy-start(bf16[128,2048]{1,0:T(8,128)(2,1)} %v_ref.1) | copy-start | bytes 1572868
  53.9 10.4 %copy-start.1 = (bf16[128,2048]{1,0:T(8,128)(2,1)S(1)}, bf16[128,2048]{1,0:T(8,128)(2,1)}, u32[]{:S(2)}) copy-start(bf16[128,2048]{1,0:T(8,128)(2,1)} %k_ref.1) | copy-start | bytes 1572868
  53.9 10.4 %copy-start.9 = (f32[16,2048]{1,0:T(8,128)S(1)}, f32[16,2048]{1,0:T(8,128)}, u32[]{:S(2)}) copy-start(f32[16,2048]{1,0:T(8,128)} %residue_ref.1) | copy-start | bytes 393220
